TPU v7x, 32 devices: a whole 2x2x4 slice. The times are simulated.
32 devices in a mesh: row: 2 (over core), col: 8 (over z, y), layer: 2 (over x).
Axes of the slice: x: 2, y: 2, z: 4, core: 2. Of those that a mesh axis runs over, the one named last changes fastest.
Arguments:
- u_values: float32 [64, 4, 2, 128, 128], P(('row', 'col'), None, 'layer'), may hold values from -0.1875 to 0.1875
- u_mask: int32 [64, 4, 2], P(('row', 'col'), None, 'layer'), may hold values 0 or 1
- p_values: float32 [32, 2, 8, 128, 128], P(('row', 'col'), 'layer'), may hold values from -6 to 6
- p_mask: int32 [32, 2, 8], P(('row', 'col'), 'layer'), may hold values 0 or 1
- t_mask: int32 [64, 4, 2], P(('row', 'col'), None, 'layer'), may hold values 0 or 1
- out_mask: int32 [32, 2, 8], P(('row', 'col'), 'layer'), may hold values 0 or 1
Outputs:
- new_density: float32 [32, 2, 8, 128, 128], P(('row', 'col'), 'layer')
All inputs are finite; a program needn't handle non-finite values. No bound on the sum of `u_mask` or of `p_mask` or of `t_mask` or of `out_mask` on one device may be relied on, other than what follows from the above.
Results may differ from a plain program's by a relative error of at most 0.0001.
Values sent between devices are 32-bit elements; how exact they have to be, the bound alone decides.
No kernel may reach another device: no remote copies, remote signals or barrier semaphores. Data moves between devices by JAX's collectives and lax.ppermute only.
A program may use at most 64 MiB of HBM per device.

v0:
```python
import jax
import jax.numpy as jnp
from jax import lax
from jax.sharding import PartitionSpec as P

NO = 8


def extended(cells, sides, width):
    for axis, dim in sides:
        count = lax.axis_size(axis)
        ends = count - 1
        head = lax.slice_in_dim(cells, 0, width, axis=dim)
        tail = lax.slice_in_dim(cells, cells.shape[dim] - width, cells.shape[dim], axis=dim)
        cells = jnp.concatenate(
            [
                lax.ppermute(tail, axis, [(i, (i + 1) % count) for i in range(ends)]),
                cells,
                lax.ppermute(head, axis, [((i + 1) % count, i) for i in range(ends)]),
            ],
            axis=dim,
        )
    return cells


def fetch_rows(u_band):
    return extended(u_band, ((("row", "col"), 0),), NO // 2)


def on_device(u_values, u_mask, p_values, p_mask, t_mask, out_mask):
    slab_rows = u_values.shape[0]
    group_size = u_values.shape[1]
    block_size = u_values.shape[3]
    layer_count = lax.axis_size("layer")
    slab_count = lax.axis_size(("row", "col"))
    band_reach = NO // 2
    total_rows = slab_rows * slab_count
    per_layer = slab_rows // layer_count
    layer_id = lax.axis_index("layer")
    slab_id = lax.axis_index(("row", "col"))
    row_index = jnp.arange(slab_rows, dtype=jnp.int32)
    row_class = row_index % layer_count
    first_offset = (layer_id - row_class) % layer_count
    slot_index = jnp.arange(group_size, dtype=jnp.int32)
    block_col = (
        slab_id * slab_rows
        + row_index[:, None]
        - band_reach
        + first_offset[:, None]
        + layer_count * slot_index[None, :]
    )
    class_valid = (block_col >= 0) & (block_col < total_rows)
    u_keep = jnp.where(class_valid, u_mask[:, :, 0], 0).astype(jnp.float32)
    t_keep = jnp.where(class_valid, t_mask[:, :, 0], 0).astype(jnp.float32)
    u_band = u_values[:, :, 0] * u_keep[:, :, None, None]
    local_index = jnp.arange(per_layer, dtype=jnp.int32)
    own_rows = slab_id * slab_rows + layer_count * local_index + layer_id
    band_col = own_rows[:, None] - band_reach + jnp.arange(NO, dtype=jnp.int32)[None, :]
    row_valid = (band_col >= 0) & (band_col < total_rows)
    p_keep = jnp.where(row_valid, p_mask[:, 0], 0).astype(jnp.float32)
    o_keep = jnp.where(row_valid, out_mask[:, 0], 0).astype(jnp.float32)
    p_band = p_values[:, 0] * p_keep[:, :, None, None]
    p_extended = extended(p_band, ((("row", "col"), 0),), band_reach // layer_count)
    u_split = u_band.reshape(per_layer, layer_count, group_size, block_size, block_size)
    pieces = []
    for r in range(layer_count):
        lead_shift = (layer_id - r) % layer_count
        step_down = (layer_id < r).astype(jnp.int32)
        running = jnp.zeros((per_layer, NO, block_size, block_size), jnp.float32)
        for m in range(group_size):
            p_rows = lax.dynamic_slice_in_dim(p_extended, m + step_down, per_layer, 0)
            product = jnp.einsum(
                "bxy,boyz->boxz", u_split[:, r, m], p_rows, precision=lax.Precision.HIGHEST
            )
            padded = jnp.pad(product, ((0, 0), (NO, NO), (0, 0), (0, 0)))
            running = running + lax.dynamic_slice_in_dim(
                padded, NO + band_reach - lead_shift - layer_count * m, NO, 1
            )
        classed = jnp.roll(
            running.reshape(per_layer, group_size, layer_count, block_size, block_size), r, axis=2
        )
        pieces.append(classed)
    stacked = jnp.stack(pieces, axis=1).reshape(
        slab_rows, group_size, layer_count, block_size, block_size
    )
    partial_value = lax.psum_scatter(stacked, "layer", scatter_dimension=2, tiled=True)
    t_band = partial_value[:, :, 0] * t_keep[:, :, None, None]
    u_extended = fetch_rows(u_band)
    t_classes = t_band.reshape(per_layer, layer_count, group_size, block_size, block_size)
    columns = []
    for op in range(NO):
        u_slice = u_extended[op : op + slab_rows].reshape(
            per_layer, layer_count, group_size, block_size, block_size
        )
        u_padded = jnp.pad(u_slice, ((0, 0), (0, 0), (1, 1), (0, 0), (0, 0)))
        residue = (op - band_reach) % layer_count
        base_shift = (op - band_reach) // layer_count
        lower = max(0, base_shift)
        upper = min(group_size, base_shift + 1 + group_size)
        by_class = []
        for c in range(layer_count):
            class_first = (layer_id - c) % layer_count
            shift = base_shift + (class_first < residue).astype(jnp.int32)
            start = lower - shift + 1
            chosen = lax.dynamic_slice_in_dim(u_padded[:, c], start, upper - lower, 1)
            by_class.append(
                jnp.einsum(
                    "qmab,qmcb->qac",
                    t_classes[:, c, lower:upper],
                    chosen,
                    precision=lax.Precision.HIGHEST,
                )
            )
        columns.append(jnp.stack(by_class, axis=1).reshape(slab_rows, block_size, block_size))
    new_part = jnp.stack(columns, axis=1).reshape(
        per_layer, layer_count, NO, block_size, block_size
    )
    summed = lax.psum_scatter(new_part, "layer", scatter_dimension=1, tiled=True)
    return summed * o_keep[:, None, :, None, None]


def solution(mesh):
    placed = (
        P(("row", "col"), None, "layer", None, None),
        P(("row", "col"), None, "layer"),
        P(("row", "col"), "layer", None, None, None),
        P(("row", "col"), "layer", None),
        P(("row", "col"), None, "layer"),
        P(("row", "col"), "layer", None),
    )
    return jax.shard_map(
        on_device,
        mesh=mesh,
        in_specs=placed,
        out_specs=P(("row", "col"), "layer", None, None, None),
        check_vma=False,
    )
```

profile of v0, /device:TPU:0, one launch (start us, length us, event | category | flops | bytes accessed | tf_op | source)
XLA Modules:
  0.0 257.2 jit_solution(17291048007225741419)
XLA Ops:
  6.5 1.6 copy.38
  8.5 4.9 %collective-permute-start = (f32[2,8,128,128]{2,3,1,0:T(8,128)S(1)}, f32[2,8,128,128]{2,3,1,0:T(8,128)S(1)}, u32[]{:S(2)}, u32[]{:S(2)}) collective-permute-start(f32[2,8,128,128]{2,3,1,0:T(8,128)S(1)} %bitcast_multiply_fusion.1), channel_id=1, source_target_pairs={{0,2},{2,4},{4,6},{6,8},{8,10},{10,12},{12,14},{14,16},{16,18},{18... | collective-permute-start | bytes 3145736 | tf_op jit(solution)/shard_map/ppermute | solution.py:17
  13.4 1.3 collective-permute-start.1
  14.8 1.1 bitcast_multiply_fusion
  15.9 5.5 %collective-permute-start.2 = (f32[4,4,128,128]{3,2,1,0:T(8,128)}, f32[4,4,128,128]{3,2,1,0:T(8,128)}, u32[]{:S(2)}, u32[]{:S(2)}) collective-permute-start(f32[4,4,128,128]{3,2,1,0:T(8,128)} %bitcast_multiply_fusion), channel_id=1, source_target_pairs={{0,2},{2,4},{4,6},{6,8},{8,10},{10,12},{12,14},{14,16},{16,18},{18... | collective-permute-start | bytes 3145736 | tf_op jit(solution)/shard_map/ppermute | solution.py:17
  21.5 1.3 collective-permute-start.3
  23.8 1.4 pad_slice_fusion.15
  25.2 56.6 %collective-permute-done = f32[2,8,128,128]{2,3,1,0:T(8,128)S(1)} collective-permute-done((f32[2,8,128,128]{2,3,1,0:T(8,128)S(1)}, f32[2,8,128,128]{2,3,1,0:T(8,128)S(1)}, u32[]{:S(2)}, u32[]{:S(2)}) %collective-permute-start) | collective-permute-done | bytes 1048608 | tf_op jit(solution)/shard_map/ppermute | solution.py:17
  81.8 1.0 copy-done.20
  82.8 2.1 pad_maximum_fusion
  84.9 1.0 convolution_bitcast_fusion.4
  85.9 1.0 convolution_bitcast_fusion.5
  87.0 1.0 convolution_bitcast_fusion.6
  88.0 1.0 convolution_bitcast_fusion.7
  89.0 2.0 convolution_bitcast_fusion
  91.0 2.0 convolution_bitcast_fusion.1
  93.1 2.0 convolution_bitcast_fusion.2
  95.1 1.5 fusion.6
  96.6 2.5 copy.43
  99.1 2.1 convolution_bitcast_fusion.3
  101.2 1.7 fusion.9
  103.5 0.7 copy-done.4
  104.2 1.5 pad_maximum_fusion.1
  106.0 3.4 %pad_maximum_fusion.2 = (f32[4,4,128,128]{3,2,1,0:T(8,128)S(1)}, f32[4,4,128,128]{3,2,1,0:T(8,128)S(1)}, f32[4,4,128,128]{3,2,1,0:T(8,128)S(1)}, f32[4,4,128,128...) fusion(f32[4,4,128,128]{3,2,1,0:T(8,128)} %collective-permute-done.3, ...), kind=kLoop, calls=%fused_computation.68 | loop fusion | flops 1572864 | bytes 9437184 | tf_op jit(solution)/shard_map/concatenate | solution.py:15
  109.4 1.3 pad_slice_fusion.21
  110.7 1.4 pad_slice_fusion.23
  112.1 1.3 pad_slice_fusion.19
  113.5 1.3 pad_slice_fusion.17
  114.8 1.1 pad_slice_fusion.13
  115.9 1.3 pad_slice_fusion.11
  117.2 1.4 pad_slice_fusion.9
  118.6 51.3 %all-reduce.21.cloned.1.call-done = f32[4,4,2,128,128]{4,3,2,1,0:T(8,128)} async-done(((f32[4,4,2,128,128]{4,3,2,1,0:T(8,128)}), f32[4,4,2,128,128]{4,3,2,1,0:T(8,128)}) %all-reduce.21.cloned.1.call-update) | async-done | bytes 2097168
  170.0 2.1 constant_dynamic-slice_fusion.2
  172.2 0.6 convolution_bitcast_fusion.21
  172.8 0.6 convolution_bitcast_fusion.20
  173.5 0.6 convolution_bitcast_fusion.23
  174.8 0.6 convolution_bitcast_fusion.18
  177.5 0.6 convolution_bitcast_fusion.14
  178.1 0.6 convolution_bitcast_fusion.15
  178.8 0.6 convolution_bitcast_fusion.12
  179.4 0.6 convolution_bitcast_fusion.13
  180.1 0.6 convolution_bitcast_fusion.10
  180.7 0.6 convolution_bitcast_fusion.11
  182.0 0.6 convolution_bitcast_fusion.9
  182.9 1.3 copy-done.6
  184.3 63.0 %all-reduce.23.cloned.1.call-done = f32[2,2,8,128,128]{4,3,0,1,2:T(8,128)} async-done(((f32[2,2,8,128,128]{4,3,0,1,2:T(8,128)}), f32[2,2,8,128,128]{4,3,0,1,2:T(8,128)}) %all-reduce.23.cloned.1.call-update) | async-done | bytes 2097168
  247.3 2.0 dynamic-slice_multiply_fusion
  249.3 1.1 copy.56
  (86 shorter events, 5.7 us)
Async XLA Ops:
  6.5 1.7 copy-start.24
  6.5 1.7 copy-start.23
  6.5 163.4 %all-reduce.21.cloned.1.call-start = ((), (), s32[]{:S(2)}) async-start(), calls=%async_computation | async-start | bytes 4194304
  6.5 8.2 %copy-start.21 = (s32[4,4,1]{1,2,0:T(1,128)S(1)}, s32[4,4,1]{1,2,0:T(1,128)}, u32[]{:S(2)}) copy-start(s32[4,4,1]{1,2,0:T(1,128)} %param.7) | copy-start | bytes 196
  6.5 8.3 %copy-start.3 = (f32[4,4,1,128,128]{4,3,2,1,0:T(8,128)S(1)}, f32[4,4,1,128,128]{4,3,2,1,0:T(8,128)}, u32[]{:S(2)}) copy-start(f32[4,4,1,128,128]{4,3,2,1,0:T(8,128)} %param.6) | copy-start | bytes 3145732
  8.3 14.5 %copy-start.22 = (s32[4,4,1]{1,2,0:T(1,128)S(1)}, s32[4,4,1]{1,2,0:T(1,128)}, u32[]{:S(2)}) copy-start(s32[4,4,1]{1,2,0:T(1,128)} %param.10) | copy-start | bytes 196
  8.3 14.7 %copy-start.25 = (u32[32]{0:T(128)S(1)}, u32[32]{0:T(128)}, u32[]{:S(2)}) copy-start(u32[32]{0:T(128)} %constant.214) | copy-start | bytes 388
  8.5 73.4 %copy-start.5 = (f32[2,8,128,128]{2,3,1,0:T(8,128)}, f32[2,8,128,128]{2,3,1,0:T(8,128)S(1)}, u32[]{:S(2)}) copy-start(f32[2,8,128,128]{2,3,1,0:T(8,128)S(1)} %bitcast_multiply_fusion.1) | copy-start | bytes 3145732
  8.5 73.4 %collective-permute-start = (f32[2,8,128,128]{2,3,1,0:T(8,128)S(1)}, f32[2,8,128,128]{2,3,1,0:T(8,128)S(1)}, u32[]{:S(2)}, u32[]{:S(2)}) collective-permute-start(f32[2,8,128,128]{2,3,1,0:T(8,128)S(1)} %bitcast_multiply_fusion.1), channel_id=1, source_target_pairs={{0,2},{2,4},{4,6},{6,8},{8,10},{10,12},{12,14},{14,16},{16,18},{18... | collective-permute-start | bytes 3145736 | tf_op jit(solution)/shard_map/ppermute | solution.py:17
  13.4 69.4 %collective-permute-start.1 = (f32[2,8,128,128]{2,3,1,0:T(8,128)S(1)}, f32[2,8,128,128]{2,3,1,0:T(8,128)}, u32[]{:S(2)}, u32[]{:S(2)}) collective-permute-start(f32[2,8,128,128]{2,3,1,0:T(8,128)S(1)} %bitcast_multiply_fusion.1), channel_id=1, source_target_pairs={{2,0},{4,2},{6,4},{8,6},{10,8},{12,10},{14,12},{16,14},{18,16},{20... | collective-permute-start | bytes 3145736 | tf_op jit(solution)/shard_map/ppermute | solution.py:19
  15.9 90.0 %collective-permute-start.2 = (f32[4,4,128,128]{3,2,1,0:T(8,128)}, f32[4,4,128,128]{3,2,1,0:T(8,128)}, u32[]{:S(2)}, u32[]{:S(2)}) collective-permute-start(f32[4,4,128,128]{3,2,1,0:T(8,128)} %bitcast_multiply_fusion), channel_id=1, source_target_pairs={{0,2},{2,4},{4,6},{6,8},{8,10},{10,12},{12,14},{14,16},{16,18},{18... | collective-permute-start | bytes 3145736 | tf_op jit(solution)/shard_map/ppermute | solution.py:17
  21.5 84.5 %collective-permute-start.3 = (f32[4,4,128,128]{3,2,1,0:T(8,128)}, f32[4,4,128,128]{3,2,1,0:T(8,128)}, u32[]{:S(2)}, u32[]{:S(2)}) collective-permute-start(f32[4,4,128,128]{3,2,1,0:T(8,128)} %bitcast_multiply_fusion), channel_id=1, source_target_pairs={{2,0},{4,2},{6,4},{8,6},{10,8},{12,10},{14,12},{16,14},{18,16},{20... | collective-permute-start | bytes 3145736 | tf_op jit(solution)/shard_map/ppermute | solution.py:19
  23.8 69.3 %copy-start = (f32[2,2,4,128,128]{4,3,0,2,1:T(8,128)}, f32[2,2,4,128,128]{4,3,0,2,1:T(8,128)S(1)}, u32[]{:S(2)}) copy-start(f32[2,2,4,128,128]{4,3,0,2,1:T(8,128)S(1)} %copy_multiply_fusion.1) | copy-start | bytes 3145732
  81.8 1.0 copy-start.20
  99.1 2.1 copy-start.1
  99.1 2.1 copy-start.2
  103.0 1.2 copy-start.4
  105.7 141.6 %all-reduce.23.cloned.1.call-start = ((), (), s32[]{:S(2)}) async-start(), calls=%async_computation.1 | async-start | bytes 4194304
  170.0 2.2 copy-start.19
  170.0 2.9 %copy-start.18 = (f32[2,1,6,128,128]{4,3,2,0,1:T(8,128)S(1)}, f32[2,1,6,128,128]{4,3,2,0,1:T(8,128)}, u32[]{:S(2)}) copy-start(f32[2,1,6,128,128]{4,3,2,0,1:T(8,128)} %get-tuple-element.27) | copy-start | bytes 2359300
  172.2 2.6 %copy-start.13 = (f32[2,1,6,128,128]{4,3,2,0,1:T(8,128)S(1)}, f32[2,1,6,128,128]{4,3,2,0,1:T(8,128)}, u32[]{:S(2)}) copy-start(f32[2,1,6,128,128]{4,3,2,0,1:T(8,128)} %get-tuple-element.25) | copy-start | bytes 2359300
  172.8 2.6 %copy-start.12 = (f32[2,1,6,128,128]{4,3,2,0,1:T(8,128)S(1)}, f32[2,1,6,128,128]{4,3,2,0,1:T(8,128)}, u32[]{:S(2)}) copy-start(f32[2,1,6,128,128]{4,3,2,0,1:T(8,128)} %get-tuple-element.24) | copy-start | bytes 2359300
  174.1 2.0 copy-start.11
  174.8 2.0 copy-start.10
  174.8 2.6 %copy-start.8 = (f32[2,1,6,128,128]{4,3,0,2,1:T(8,128)S(1)}, f32[2,1,6,128,128]{4,3,0,2,1:T(8,128)}, u32[]{:S(2)}) copy-start(f32[2,1,6,128,128]{4,3,0,2,1:T(8,128)} %get-tuple-element.21) | copy-start | bytes 2359300
  175.5 2.6 %copy-start.7 = (f32[2,1,6,128,128]{4,3,0,2,1:T(8,128)S(1)}, f32[2,1,6,128,128]{4,3,0,2,1:T(8,128)}, u32[]{:S(2)}) copy-start(f32[2,1,6,128,128]{4,3,0,2,1:T(8,128)} %get-tuple-element.20) | copy-start | bytes 2359300
  176.1 2.6 %copy-start.9 = (f32[2,1,6,128,128]{4,3,2,0,1:T(8,128)S(1)}, f32[2,1,6,128,128]{4,3,2,0,1:T(8,128)}, u32[]{:S(2)}) copy-start(f32[2,1,6,128,128]{4,3,2,0,1:T(8,128)} %get-tuple-element.19) | copy-start | bytes 2359300
  177.4 2.6 %copy-start.17 = (f32[2,1,6,128,128]{4,3,2,0,1:T(8,128)S(1)}, f32[2,1,6,128,128]{4,3,2,0,1:T(8,128)}, u32[]{:S(2)}) copy-start(f32[2,1,6,128,128]{4,3,2,0,1:T(8,128)} %get-tuple-element.17) | copy-start | bytes 2359300
  178.1 2.6 %copy-start.15 = (f32[2,1,6,128,128]{4,3,2,0,1:T(8,128)S(1)}, f32[2,1,6,128,128]{4,3,2,0,1:T(8,128)}, u32[]{:S(2)}) copy-start(f32[2,1,6,128,128]{4,3,2,0,1:T(8,128)} %get-tuple-element.16) | copy-start | bytes 2359300
  178.8 2.6 %copy-start.16 = (f32[2,1,6,128,128]{4,3,2,0,1:T(8,128)S(1)}, f32[2,1,6,128,128]{4,3,2,0,1:T(8,128)}, u32[]{:S(2)}) copy-start(f32[2,1,6,128,128]{4,3,2,0,1:T(8,128)} %get-tuple-element.12) | copy-start | bytes 2359300
  179.4 2.6 %copy-start.14 = (f32[2,1,6,128,128]{4,3,2,0,1:T(8,128)S(1)}, f32[2,1,6,128,128]{4,3,2,0,1:T(8,128)}, u32[]{:S(2)}) copy-start(f32[2,1,6,128,128]{4,3,2,0,1:T(8,128)} %get-tuple-element.11) | copy-start | bytes 2359300
  182.9 1.3 copy-start.6
Sparse Core Ops, SparseCore 0:
  105.9 64.0 all-reduce.20
  184.3 62.9 all-reduce.22
where the time goes:
time: 258 us; the launch traced here: 257 us
  waiting for transfers between devices  171 us (66%)
  matrix products  22.4 us (9%)
  local copies, waits for them, and re-layouts  22.3 us (9%)
  other arithmetic  14.2 us (6%)
  between operations  14.1 us (5%)
  starting transfers between devices  13.3 us (5%)
    unnamed x4, waiting for transfers between devices  114 us
    ppermute x2, waiting for transfers between devices, extended(): lax.ppermute(tail, axis, [(i, (i + 1) % count) for i in range(ends)])  56.6 us
    dot_general x8, matrix products, on_device(): jnp.einsum('bxy,boyz->boxz', u_split[:, r, m], p_rows, precision=lax.Prec...  12.2 us
    slice x8, local copies, waits for them, and re-layouts, on_device(): chosen = lax.dynamic_slice_in_dim(u_padded[:, c], start, upper - lower, 1)  10.6 us
    ppermute x2, starting transfers between devices, extended(): lax.ppermute(tail, axis, [(i, (i + 1) % count) for i in range(ends)])  10.5 us
    dot_general x16, matrix products, on_device(): jnp.einsum('qmab,qmcb->qac', t_classes[:, c, lower:upper], chosen, precis...  10.2 us
    unnamed x57, local copies, waits for them, and re-layouts  7.83 us
    concatenate x2, other arithmetic, extended(): jnp.concatenate([lax.ppermute(tail, axis, [(i, (i + 1) % count) for i in...  5.5 us
  transfers between devices with their start and end apart: 6, of which 3 were waited for; matrix products, arithmetic and copies ran while one was open for 15% of the time, Pallas kernels for 0%

commit v1 on v0

v1 whole, which is shorter than its diff:
```python
import functools

import jax
import jax.numpy as jnp
from jax import lax
from jax.experimental import pallas as pl
from jax.experimental.pallas import tpu as pltpu
from jax.sharding import PartitionSpec as P

SLABS = ("row", "col")
F32 = jnp.float32
BF16 = jnp.bfloat16
VMEM = pl.BlockSpec(memory_space=pltpu.VMEM)
SMEM = pl.BlockSpec(memory_space=pltpu.SMEM)


def shape(*dims, dtype=F32):
    return jax.ShapeDtypeStruct(dims, dtype)


def call(body, outs, n_vmem, n_smem, scratch=(), flops=0):
    return pl.pallas_call(
        body,
        out_shape=outs,
        in_specs=[SMEM] * n_smem + [VMEM] * n_vmem,
        out_specs=[VMEM] * len(outs),
        scratch_shapes=list(scratch),
        cost_estimate=pl.CostEstimate(flops=flops, bytes_accessed=2 << 20, transcendentals=0),
        compiler_params=pltpu.CompilerParams(vmem_limit_bytes=40 << 20),
    )


def halves(x):
    high = x.astype(BF16)
    return high, (x - high.astype(F32)).astype(BF16)


def dot3(a, b, rhs_contract):
    one = functools.partial(
        lax.dot_general,
        dimension_numbers=(((1,), (rhs_contract,)), ((), ())),
        preferred_element_type=F32,
    )
    return one(a[0], b[0]) + (one(a[0], b[1]) + one(a[1], b[0]))


def aligned(block, size):
    return pl.multiple_of(block * size, size)


def keep_p(total_rows, where, p_mask, p, *outs):
    slab, layer = where[0], where[1]
    for a in range(2):
        row = slab * 4 + 2 * a + layer
        for o in range(8):
            col = row - 4 + o
            inside = (col >= 0) & (col < total_rows)
            keep = jnp.where(inside, p_mask[a, 0, o], 0).astype(F32)
            outs[2 * (o % 2) + a][o // 2] = p[a, 0, o] * keep


def keep_u(u_mask, u, *outs):
    for i in range(4):
        for m in range(4):
            outs[i][m] = u[i, m, 0] * u_mask[i, m, 0].astype(F32)


def slot_base(i, layer):
    return i // 2 if i % 2 == 0 else (i + 1) // 2 - layer


def product_t(size, where, t_mask, *refs):
    u_own, u_oth = refs[0:4], refs[4:8]
    pe, pc = refs[8:10], refs[10:12]
    pe_y, pc_y = refs[12:14], refs[14:16]
    pe_z, pc_z = refs[16:18], refs[18:20]
    t_hi, t_lo, ss = refs[20:23]
    own_hi, own_lo, oth_hi, oth_lo, ud_hi, ud_lo = refs[23:29]
    even, layer = where[0] % 2 == 0, where[1]
    for ref in (own_hi, own_lo, oth_hi, oth_lo, ud_hi, ud_lo):
        ref[...] = jnp.zeros_like(ref)
    for mine, other_y, other_z, hi_ref, lo_ref, shift in (
        (pe, pe_y, pe_z, own_hi, own_lo, -2),
        (pc, pc_y, pc_z, oth_hi, oth_lo, -1),
    ):
        for a in range(6):
            for e in range(4):
                c = a + e + shift
                if not 0 <= c < 6:
                    continue
                if a < 2:
                    block = jnp.where(even, other_z[a][e], other_y[a][e])
                elif a < 4:
                    block = mine[a - 2][e]
                else:
                    block = jnp.where(even, other_y[a - 4][e], other_z[a - 4][e])
                hi, lo = halves(block)
                at = (pl.ds(a * size, size), pl.ds(c * size, size))
                hi_ref[at], lo_ref[at] = hi, lo
    for i in range(4):
        left = [jnp.concatenate(x, axis=1) for x in zip(*[halves(u_own[i][m]) for m in range(4)])]
        other = [jnp.concatenate(x, axis=1) for x in zip(*[halves(u_oth[i][m]) for m in range(4)])]
        base = slot_base(i, layer)
        ud_hi[pl.ds(i * size, size), pl.ds(aligned(base, size), 4 * size)] = left[0]
        ud_lo[pl.ds(i * size, size), pl.ds(aligned(base, size), 4 * size)] = left[1]
        rows = pl.ds(aligned(base, size), 4 * size)
        band = (own_hi[rows, rows], own_lo[rows, rows])
        total = dot3(left, band, 0)
        rows = pl.ds(aligned(slot_base(i, 1 - layer), size), 4 * size)
        cols = pl.ds(aligned(i // 2 + layer if i % 2 == 0 else (i + 1) // 2, size), 4 * size)
        band = (oth_hi[rows, cols], oth_lo[rows, cols])
        total = total + dot3(other, band, 0)
        kept = jnp.concatenate(
            [total[:, m * size : (m + 1) * size] * t_mask[i, m, 0].astype(F32) for m in range(4)], axis=1
        )
        t_hi[i], t_lo[i] = halves(kept)
    for q in range(2):
        i = 2 * q + 1 - layer
        cols = pl.ds(aligned(q + 1 - layer, size), 4 * size)
        sums = dot3((t_hi[i], t_lo[i]), (ud_hi[:, cols], ud_lo[:, cols]), 1)
        for r in range(4):
            ss[q, r] = sums[:, r * size : (r + 1) * size]


def put_halo(size, even, layer, u_y, u_z, uh_hi, uh_lo):
    uh_hi[...] = jnp.zeros_like(uh_hi)
    uh_lo[...] = jnp.zeros_like(uh_lo)
    for at in range(7):
        if at < 4:
            base = slot_base(at, layer)
            pick = [jnp.where(even, u_z[at][m], u_y[at][m]) for m in range(4)]
        else:
            base = slot_base(at - 4, layer) + 4
            pick = [jnp.where(even, u_y[at - 4][m], u_z[at - 4][m]) for m in range(4)]
        both = [jnp.concatenate(x, axis=1) for x in zip(*[halves(x) for x in pick])]
        where = (pl.ds(at * size, size), pl.ds(aligned(base, size), 4 * size))
        uh_hi[where], uh_lo[where] = both


def halo_sums(size, i, base, t_hi, t_lo, uh_hi, uh_lo):
    cols = pl.ds(aligned(base + 2, size), 4 * size)
    rows = [pl.ds(aligned(jnp.where(t < i, 4 + t, t), size), size) for t in range(4)]
    hi = jnp.concatenate([uh_hi[r, cols] for r in rows], axis=0)
    lo = jnp.concatenate([uh_lo[r, cols] for r in rows], axis=0)
    return dot3((t_hi[i], t_lo[i]), (hi, lo), 1)


def send_halo(size, where, *refs):
    u_y, u_z = refs[0:4], refs[4:8]
    t_hi, t_lo, out, uh_hi, uh_lo = refs[8:13]
    layer = where[1]
    put_halo(size, where[0] % 2 == 0, layer, u_y, u_z, uh_hi, uh_lo)
    for q in range(2):
        sums = halo_sums(size, 2 * q + 1 - layer, q + 1 - layer, t_hi, t_lo, uh_hi, uh_lo)
        for t in range(4):
            out[q, t] = sums[:, t * size : (t + 1) * size]


def keep_rows(size, where, *refs):
    u_own, u_y, u_z = refs[0:4], refs[4:8], refs[8:12]
    t_hi, t_lo, out, uh_hi, uh_lo, ud_hi, ud_lo = refs[12:19]
    layer = where[1]
    put_halo(size, where[0] % 2 == 0, layer, u_y, u_z, uh_hi, uh_lo)
    ud_hi[...] = jnp.zeros_like(ud_hi)
    ud_lo[...] = jnp.zeros_like(ud_lo)
    for i in range(4):
        left = [jnp.concatenate(x, axis=1) for x in zip(*[halves(u_own[i][m]) for m in range(4)])]
        cols = pl.ds(aligned(slot_base(i, layer), size), 4 * size)
        ud_hi[pl.ds(i * size, size), cols] = left[0]
        ud_lo[pl.ds(i * size, size), cols] = left[1]
    for q in range(2):
        i = 2 * q + layer
        sums = halo_sums(size, i, q, t_hi, t_lo, uh_hi, uh_lo)
        for t in range(4):
            out[q, (8 - i + t) % 8] = sums[:, t * size : (t + 1) * size]
        cols = pl.ds(q * size, 4 * size)
        sums = dot3((t_hi[i], t_lo[i]), (ud_hi[:, cols], ud_lo[:, cols]), 1)
        for r in range(4):
            out[q, (4 - i + r) % 8] = sums[:, r * size : (r + 1) * size]


def combine(total_rows, where, o_mask, kept, ss, halo, out):
    slab, layer = where[0], where[1]
    for q in range(2):
        i = 2 * q + layer
        for t in range(8):
            o = (4 - i + t) % 8
            col = slab * 4 + i - 4 + o
            inside = (col >= 0) & (col < total_rows)
            keep = jnp.where(inside, o_mask[q, 0, o], 0).astype(F32)
            got = ss[q, t] if t < 4 else halo[q, t - 4]
            out[q, 0, o] = (kept[q, o] + got) * keep


def on_device(u_values, u_mask, p_values, p_mask, t_mask, out_mask):
    size = u_values.shape[-1]
    slabs = lax.axis_size(SLABS)
    total_rows = slabs * u_values.shape[0]
    where = jnp.stack([lax.axis_index(SLABS), lax.axis_index("layer")]).astype(jnp.int32)
    swap = [(0, 1), (1, 0)]
    pair = [(s, s ^ 1) for s in range(slabs)]
    onward = [(s, s + 2) for s in range(0, slabs - 2, 2)] + [(s, s - 2) for s in range(3, slabs, 2)]

    def over_layer(xs):
        return [lax.ppermute(x, "layer", swap) for x in xs]

    def over_pair(xs):
        return [lax.ppermute(x, SLABS, pair) for x in xs]

    def over_onward(xs):
        return [lax.ppermute(x, SLABS, onward) for x in xs]

    four = shape(4, size, size)
    wide = 6 * size
    pe0, pe1, po0, po1 = call(functools.partial(keep_p, total_rows), [four] * 4, 1, 2)(where, p_mask, p_values)
    pe = [pe0, pe1]
    pc = over_layer([po0, po1])
    pe_y = over_pair(pe)
    pe_z = over_onward(pe_y)
    u_own = call(keep_u, [four] * 4, 1, 1)(u_mask, u_values)
    u_oth = over_layer(u_own)
    pc_y = over_pair(pc)
    pc_z = over_onward(pc_y)
    late = lax.optimization_barrier((*u_own, pc[1]))[:4]
    u_y = over_pair(late)
    u_z = over_onward(u_y)
    t_hi, t_lo, ss = call(
        functools.partial(product_t, size),
        [shape(4, size, 4 * size, dtype=BF16)] * 2 + [shape(2, 4, size, size)],
        20,
        2,
        [pltpu.VMEM((wide, wide), BF16)] * 4 + [pltpu.VMEM((4 * size, wide), BF16)] * 2,
        flops=3 * (4 * 32 + 2 * 16) * 2 * size**3,
    )(where, t_mask, *u_own, *u_oth, *pe, *pc, *pe_y, *pc_y, *pe_z, *pc_z)
    ss_got = lax.ppermute(ss, "layer", swap)
    halo_scratch = [pltpu.VMEM((7 * size, 9 * size), BF16)] * 2
    (halo,) = call(
        functools.partial(send_halo, size),
        [shape(2, 4, size, size)],
        10,
        1,
        halo_scratch,
        flops=3 * 32 * 2 * size**3,
    )(where, *u_y, *u_z, t_hi, t_lo)
    halo_got = lax.ppermute(halo, "layer", swap)
    (kept,) = call(
        functools.partial(keep_rows, size),
        [shape(2, 8, size, size)],
        14,
        1,
        halo_scratch + [pltpu.VMEM((4 * size, wide), BF16)] * 2,
        flops=3 * 64 * 2 * size**3,
    )(where, *u_own, *u_y, *u_z, t_hi, t_lo)
    (out,) = call(functools.partial(combine, total_rows), [shape(2, 1, 8, size, size)], 3, 2)(
        where, out_mask, kept, ss_got, halo_got
    )
    return out


def solution(mesh):
    placed = (
        P(SLABS, None, "layer", None, None),
        P(SLABS, None, "layer"),
        P(SLABS, "layer", None, None, None),
        P(SLABS, "layer", None),
        P(SLABS, None, "layer"),
        P(SLABS, "layer", None),
    )
    return jax.shard_map(
        on_device,
        mesh=mesh,
        in_specs=placed,
        out_specs=P(SLABS, "layer", None, None, None),
        check_vma=False,
    )
```

time: 258 us -> 118 us (0.46)
  waiting for transfers between devices: 171 us -> 29.5 us
  starting transfers between devices: 13.3 us -> 52.8 us
  matrix products: 22.4 us -> 0 us
  Pallas kernels: 0 us -> 14.9 us
  other arithmetic: 14.2 us -> 0.07 us
  between operations: 14.1 us -> 0.21 us
  local copies, waits for them, and re-layouts: 22.3 us -> 19.5 us
    unnamed x4 -> x0, waiting for transfers between devices: 114 us -> none
    ppermute x4 -> x24, starting transfers between devices: 13.1 us -> 52.8 us  [the longest x8 31.3 us: over_onward(): return [lax.ppermute(x, SLABS, onward) for x in xs]]
    ppermute x4 -> x24, waiting for transfers between devices: 56.6 us -> 29.5 us  [the longest x6 9.7 us: over_layer(): return [lax.ppermute(x, 'layer', swap) for x in xs]]
    dot_general x24 -> x0, matrix products: 22.4 us -> none  [the longest x8 12.2 us: on_device(): jnp.einsum('bxy,boyz->boxz', u_split[:, r, m], p_rows, precision=lax.Prec...]
    pallas_call x0 -> x6, Pallas kernels: none -> 14.9 us  [the longest x1 5.06 us: on_device(): call(functools.partial(product_t, size), [shape(4, size, 4 * size, dtype=...]
    unnamed x57 -> x58, local copies, waits for them, and re-layouts: 7.83 us -> 19.5 us
    slice x9 -> x0, local copies, waits for them, and re-layouts: 10.7 us -> none  [the longest x8 10.6 us: on_device(): chosen = lax.dynamic_slice_in_dim(u_padded[:, c], start, upper - lower, 1)]
    concatenate x2 -> x0, other arithmetic: 5.5 us -> none  [extended(): jnp.concatenate([lax.ppermute(tail, axis, [(i, (i + 1) % count) for i in...]
  transfers between devices with their start and end apart: 6 -> 24, of which waited for: 3 -> 9; matrix products, arithmetic and copies ran while one was open for 15% -> 0% of each run, Pallas kernels for 0% -> 8%
where the time goes in v1:
time: 118 us; the launch traced here: 117 us
  starting transfers between devices  52.8 us (45%)
  waiting for transfers between devices  29.5 us (25%)
  local copies, waits for them, and re-layouts  19.5 us (17%)
  Pallas kernels  14.9 us (13%)
    ppermute x8, starting transfers between devices, over_onward(): return [lax.ppermute(x, SLABS, onward) for x in xs]  31.3 us
    unnamed x58, local copies, waits for them, and re-layouts  19.5 us
    ppermute x8, starting transfers between devices, over_pair(): return [lax.ppermute(x, SLABS, pair) for x in xs]  10.2 us
    ppermute x6, waiting for transfers between devices, over_layer(): return [lax.ppermute(x, 'layer', swap) for x in xs]  9.7 us
    ppermute x1, waiting for transfers between devices, on_device(): halo_got = lax.ppermute(halo, 'layer', swap)  9.27 us
    ppermute x6, starting transfers between devices, over_layer(): return [lax.ppermute(x, 'layer', swap) for x in xs]  9.18 us
    ppermute x1, waiting for transfers between devices, on_device(): ss_got = lax.ppermute(ss, 'layer', swap)  8.64 us
    pallas_call x1, Pallas kernels, on_device(): call(functools.partial(product_t, size), [shape(4, size, 4 * size, dtype=...  5.06 us
  transfers between devices with their start and end apart: 24, of which 9 were waited for; matrix products, arithmetic and copies ran while one was open for 0% of the time, Pallas kernels for 8%

profile of v1, /device:TPU:0, one launch (start us, length us, event | category | flops | bytes accessed | tf_op | source)
XLA Modules:
  0.0 116.9 jit_solution(3285158465459468083)
XLA Ops:
  0.7 1.2 %copy-done = f32[2,1,8,128,128]{4,3,2,1,0:T(8,128)S(1)} copy-done((f32[2,1,8,128,128]{4,3,2,1,0:T(8,128)S(1)}, f32[2,1,8,128,128]{4,3,2,1,0:T(8,128)}, u32[]{:S(2)}) %copy-start) | copy-done | bytes 1048600
  1.9 1.4 %shard_map.65 = (f32[4,128,128]{2,1,0:T(8,128)S(1)}, f32[4,128,128]{2,1,0:T(8,128)S(1)}, f32[4,128,128]{2,1,0:T(8,128)}, f32[4,128,128]{2,1,0:T(8,128)}) custom-call(s32[2]{0:T(128)S(1)} %pad_add_fusion.where, s32[2,1,8]{2,1,0:T(1,128)S(1)} %copy-done.3, f32[2,1,8,128,128]{4,3,2,1,0:T(8,128)S(1)} %copy-done), custom_call_target="tpu_custom_call" | custom-call | bytes 2097152 | tf_op jit(solution)/shard_map/pallas_call | solution.py:215
  3.3 2.9 %collective-permute-start = (f32[4,128,128]{2,1,0:T(8,128)}, f32[4,128,128]{2,1,0:T(8,128)S(1)}, u32[]{:S(2)}, u32[]{:S(2)}) collective-permute-start(f32[4,128,128]{2,1,0:T(8,128)} %get-tuple-element.24), channel_id=1, source_target_pairs={{0,1},{1,0},{2,3},{3,2},{4,5},{5,4},{6,7},{7,6},{8,9},{9,8},{10,11... | collective-permute-start | bytes 786440 | tf_op jit(solution)/shard_map/ppermute | solution.py:205
  6.3 2.0 %collective-permute-start.14 = (f32[4,128,128]{2,1,0:T(8,128)S(1)}, f32[4,128,128]{2,1,0:T(8,128)}, u32[]{:S(2)}, u32[]{:S(2)}) collective-permute-start(f32[4,128,128]{2,1,0:T(8,128)S(1)} %get-tuple-element.29.refs_8_), channel_id=1, source_target_pairs={{0,2},{2,0},{4,6},{6,4},{8,10},{10,8},{12,14},{14,12},{16,18},{18,... | collective-permute-start | bytes 786440 | tf_op jit(solution)/shard_map/ppermute | solution.py:208
  8.5 0.7 shard_map.64
  9.2 2.0 %collective-permute-start.10 = (f32[4,128,128]{2,1,0:T(8,128)S(1)}, f32[4,128,128]{2,1,0:T(8,128)S(1)}, u32[]{:S(2)}, u32[]{:S(2)}) collective-permute-start(f32[4,128,128]{2,1,0:T(8,128)S(1)} %get-tuple-element.26.refs_1_), channel_id=1, source_target_pairs={{0,1},{1,0},{2,3},{3,2},{4,5},{5,4},{6,7},{7,6},{8,9},{9,8},{10,11... | collective-permute-start | bytes 786440 | tf_op jit(solution)/shard_map/ppermute | solution.py:205
  11.3 2.3 %collective-permute-done.refs_11_ = f32[4,128,128]{2,1,0:T(8,128)S(1)} collective-permute-done((f32[4,128,128]{2,1,0:T(8,128)}, f32[4,128,128]{2,1,0:T(8,128)S(1)}, u32[]{:S(2)}, u32[]{:S(2)}) %collective-permute-start) | collective-permute-done | bytes 262176 | tf_op jit(solution)/shard_map/ppermute | solution.py:205
  13.6 2.1 %collective-permute-start.11 = (f32[4,128,128]{2,1,0:T(8,128)S(1)}, f32[4,128,128]{2,1,0:T(8,128)S(1)}, u32[]{:S(2)}, u32[]{:S(2)}) collective-permute-start(f32[4,128,128]{2,1,0:T(8,128)S(1)} %get-tuple-element.27.refs_2_), channel_id=1, source_target_pairs={{0,1},{1,0},{2,3},{3,2},{4,5},{5,4},{6,7},{7,6},{8,9},{9,8},{10,11... | collective-permute-start | bytes 786440 | tf_op jit(solution)/shard_map/ppermute | solution.py:205
  15.7 3.6 %collective-permute-done.13.refs_10_ = f32[4,128,128]{2,1,0:T(8,128)S(1)} collective-permute-done((f32[4,128,128]{2,1,0:T(8,128)}, f32[4,128,128]{2,1,0:T(8,128)S(1)}, u32[]{:S(2)}, u32[]{:S(2)}) %collective-permute-start.13) | collective-permute-done | bytes 262176 | tf_op jit(solution)/shard_map/ppermute | solution.py:205
  19.2 2.1 %collective-permute-start.12 = (f32[4,128,128]{2,1,0:T(8,128)S(1)}, f32[4,128,128]{2,1,0:T(8,128)S(1)}, u32[]{:S(2)}, u32[]{:S(2)}) collective-permute-start(f32[4,128,128]{2,1,0:T(8,128)S(1)} %get-tuple-element.28.refs_3_), channel_id=1, source_target_pairs={{0,1},{1,0},{2,3},{3,2},{4,5},{5,4},{6,7},{7,6},{8,9},{9,8},{10,11... | collective-permute-start | bytes 786440 | tf_op jit(solution)/shard_map/ppermute | solution.py:205
  21.3 2.0 %collective-permute-start.17 = (f32[4,128,128]{2,1,0:T(8,128)S(1)}, f32[4,128,128]{2,1,0:T(8,128)S(1)}, u32[]{:S(2)}, u32[]{:S(2)}) collective-permute-start(f32[4,128,128]{2,1,0:T(8,128)S(1)} %collective-permute-done.refs_11_), channel_id=1, source_target_pairs={{0,2},{2,0},{4,6},{6,4},{8,10},{10,8},{12,14},{14,12},{16,18},{18,... | collective-permute-start | bytes 786440 | tf_op jit(solution)/shard_map/ppermute | solution.py:208
  23.3 0.7 copy-done.6
  24.1 0.8 collective-permute-done.10.refs_5_
  25.5 2.1 %collective-permute-start.16 = (f32[4,128,128]{2,1,0:T(8,128)S(1)}, f32[4,128,128]{2,1,0:T(8,128)}, u32[]{:S(2)}, u32[]{:S(2)}) collective-permute-start(f32[4,128,128]{2,1,0:T(8,128)S(1)} %collective-permute-done.13.refs_10_), channel_id=1, source_target_pairs={{0,2},{2,0},{4,6},{6,4},{8,10},{10,8},{12,14},{14,12},{16,18},{18,... | collective-permute-start | bytes 786440 | tf_op jit(solution)/shard_map/ppermute | solution.py:208
  27.6 0.7 copy-done.8
  28.3 2.1 %collective-permute-done.11.refs_6_ = f32[4,128,128]{2,1,0:T(8,128)S(1)} collective-permute-done((f32[4,128,128]{2,1,0:T(8,128)S(1)}, f32[4,128,128]{2,1,0:T(8,128)S(1)}, u32[]{:S(2)}, u32[]{:S(2)}) %collective-permute-start.11) | collective-permute-done | bytes 262176 | tf_op jit(solution)/shard_map/ppermute | solution.py:205
  31.2 4.1 %collective-permute-start.18 = (f32[4,128,128]{2,1,0:T(8,128)}, f32[4,128,128]{2,1,0:T(8,128)S(1)}, u32[]{:S(2)}, u32[]{:S(2)}) collective-permute-start(f32[4,128,128]{2,1,0:T(8,128)} %collective-permute-done.14.refs_12_), channel_id=1, source_target_pairs={{0,4},{4,8},{8,12},{12,16},{16,20},{20,24},{24,28},{6,2},{10,6},{1... | collective-permute-start | bytes 786440 | tf_op jit(solution)/shard_map/ppermute | solution.py:211
  35.2 0.9 collective-permute-done.12.refs_7_
  36.8 4.1 %collective-permute-start.19 = (f32[4,128,128]{2,1,0:T(8,128)}, f32[4,128,128]{2,1,0:T(8,128)S(1)}, u32[]{:S(2)}, u32[]{:S(2)}) collective-permute-start(f32[4,128,128]{2,1,0:T(8,128)} %collective-permute-done.15.refs_13_), channel_id=1, source_target_pairs={{0,4},{4,8},{8,12},{12,16},{16,20},{20,24},{24,28},{6,2},{10,6},{1... | collective-permute-start | bytes 786440 | tf_op jit(solution)/shard_map/ppermute | solution.py:211
  41.6 1.8 %collective-permute-start.1 = (f32[4,128,128]{2,1,0:T(8,128)S(1)}, f32[4,128,128]{2,1,0:T(8,128)S(1)}, u32[]{:S(2)}, u32[]{:S(2)}) collective-permute-start(f32[4,128,128]{2,1,0:T(8,128)S(1)} %get-tuple-element.25.refs_0_), channel_id=1, source_target_pairs={{0,2},{2,0},{4,6},{6,4},{8,10},{10,8},{12,14},{14,12},{16,18},{18,... | collective-permute-start | bytes 786440 | tf_op jit(solution)/shard_map/ppermute | solution.py:208
  43.6 1.8 %collective-permute-start.3 = (f32[4,128,128]{2,1,0:T(8,128)S(1)}, f32[4,128,128]{2,1,0:T(8,128)S(1)}, u32[]{:S(2)}, u32[]{:S(2)}) collective-permute-start(f32[4,128,128]{2,1,0:T(8,128)S(1)} %get-tuple-element.27.refs_2_), channel_id=1, source_target_pairs={{0,2},{2,0},{4,6},{6,4},{8,10},{10,8},{12,14},{14,12},{16,18},{18,... | collective-permute-start | bytes 786440 | tf_op jit(solution)/shard_map/ppermute | solution.py:208
  46.3 0.7 copy-done.22
  47.1 3.7 %collective-permute-start.21 = (f32[4,128,128]{2,1,0:T(8,128)S(1)}, f32[4,128,128]{2,1,0:T(8,128)S(1)}, u32[]{:S(2)}, u32[]{:S(2)}) collective-permute-start(f32[4,128,128]{2,1,0:T(8,128)S(1)} %collective-permute-done.17.refs_15_), channel_id=1, source_target_pairs={{0,4},{4,8},{8,12},{12,16},{16,20},{20,24},{24,28},{6,2},{10,6},{1... | collective-permute-start | bytes 786440 | tf_op jit(solution)/shard_map/ppermute | solution.py:211
  51.5 4.2 %collective-permute-start.20 = (f32[4,128,128]{2,1,0:T(8,128)}, f32[4,128,128]{2,1,0:T(8,128)}, u32[]{:S(2)}, u32[]{:S(2)}) collective-permute-start(f32[4,128,128]{2,1,0:T(8,128)} %collective-permute-done.16.refs_14_), channel_id=1, source_target_pairs={{0,4},{4,8},{8,12},{12,16},{16,20},{20,24},{24,28},{6,2},{10,6},{1... | collective-permute-start | bytes 786440 | tf_op jit(solution)/shard_map/ppermute | solution.py:211
  55.7 4.5 %collective-permute-start.5 = (f32[4,128,128]{2,1,0:T(8,128)S(1)}, f32[4,128,128]{2,1,0:T(8,128)S(1)}, u32[]{:S(2)}, u32[]{:S(2)}) collective-permute-start(f32[4,128,128]{2,1,0:T(8,128)S(1)} %collective-permute-done.1.refs_4_.refs_0_), channel_id=1, source_target_pairs={{0,4},{4,8},{8,12},{12,16},{16,20},{20,24},{24,28},{6,2},{10,6},{1... | collective-permute-start | bytes 786440 | tf_op jit(solution)/shard_map/ppermute | solution.py:211
  60.2 0.9 collective-permute-done.3.refs_6_.refs_2_
  61.1 4.7 %collective-permute-start.6 = (f32[4,128,128]{2,1,0:T(8,128)S(1)}, f32[4,128,128]{2,1,0:T(8,128)S(1)}, u32[]{:S(2)}, u32[]{:S(2)}) collective-permute-start(f32[4,128,128]{2,1,0:T(8,128)S(1)} %collective-permute-done.2.refs_5_.refs_1_), channel_id=1, source_target_pairs={{0,4},{4,8},{8,12},{12,16},{16,20},{20,24},{24,28},{6,2},{10,6},{1... | collective-permute-start | bytes 786440 | tf_op jit(solution)/shard_map/ppermute | solution.py:211
  65.8 0.9 collective-permute-done.4.refs_7_.refs_3_
  66.7 2.6 %collective-permute-start.7 = (f32[4,128,128]{2,1,0:T(8,128)S(1)}, f32[4,128,128]{2,1,0:T(8,128)S(1)}, u32[]{:S(2)}, u32[]{:S(2)}) collective-permute-start(f32[4,128,128]{2,1,0:T(8,128)S(1)} %collective-permute-done.3.refs_6_.refs_2_), channel_id=1, source_target_pairs={{0,4},{4,8},{8,12},{12,16},{16,20},{20,24},{24,28},{6,2},{10,6},{1... | collective-permute-start | bytes 786440 | tf_op jit(solution)/shard_map/ppermute | solution.py:211
  70.0 3.5 %collective-permute-start.8 = (f32[4,128,128]{2,1,0:T(8,128)S(1)}, f32[4,128,128]{2,1,0:T(8,128)S(1)}, u32[]{:S(2)}, u32[]{:S(2)}) collective-permute-start(f32[4,128,128]{2,1,0:T(8,128)S(1)} %collective-permute-done.4.refs_7_.refs_3_), channel_id=1, source_target_pairs={{0,4},{4,8},{8,12},{12,16},{16,20},{20,24},{24,28},{6,2},{10,6},{1... | collective-permute-start | bytes 786440 | tf_op jit(solution)/shard_map/ppermute | solution.py:211
  73.6 0.9 copy-done.5
  74.6 0.9 copy-done.7
  75.5 0.9 copy-done.9
  76.5 0.9 copy-done.11
  77.4 0.9 copy-done.13
  78.4 0.9 copy-done.15
  79.3 0.9 copy-done.17
  80.3 0.9 copy-done.19
  81.2 0.9 copy-done.21
  82.2 0.9 copy-done.23
  83.2 0.9 copy-done.25
  84.1 5.1 %shard_map.66 = (bf16[4,128,512]{2,1,0:T(8,128)(2,1)S(1)}, bf16[4,128,512]{2,1,0:T(8,128)(2,1)S(1)}, f32[2,4,128,128]{3,2,1,0:T(8,128)S(1)}) custom-call(s32[2]{0:T(128)S(1)} %pad_add_fusion.where, s32[4,4,1]{2,1,0:T(4,128)S(1)} %copy.8.t_mask, f32[4,128,128]{2,1,0:T(8,128)S(1)} %get-tuple-element.25.refs_0_, f32[4,128,128]{2,1,0:T(8,128)S(1)} %get-tuple-element.26.refs_1_, ...), custom_call_target="tpu_custom_call" | custom-call | flops 2013265920 | bytes 2097152 | tf_op jit(solution)/shard_map/pallas_call | solution.py:227
  89.2 2.4 %shard_map.68 = f32[2,4,128,128]{3,2,1,0:T(8,128)S(1)} custom-call(s32[2]{0:T(128)S(1)} %pad_add_fusion.where, f32[4,128,128]{2,1,0:T(8,128)S(1)} %collective-permute-done.1.refs_4_.refs_0_, f32[4,128,128]{2,1,0:T(8,128)S(1)} %collective-permute-done.2.refs_5_.refs_1_, f32[4,128,128]{2,1,0:T(8,128)S(1)} %collective-permute-done.3.refs_6_.refs_2_, ...), custom_call_target="tpu_custom_call" | custom-call | flops 402653184 | bytes 2097152 | tf_op jit(solution)/shard_map/pallas_call | solution.py:237
  91.6 1.5 %collective-permute-start.23 = (f32[2,4,128,128]{3,2,1,0:T(8,128)S(1)}, f32[2,4,128,128]{3,2,1,0:T(8,128)S(1)}, u32[]{:S(2)}, u32[]{:S(2)}) collective-permute-start(f32[2,4,128,128]{3,2,1,0:T(8,128)S(1)} %shard_map.68), channel_id=1, source_target_pairs={{0,1},{1,0},{2,3},{3,2},{4,5},{5,4},{6,7},{7,6},{8,9},{9,8},{10,11... | collective-permute-start | bytes 1572872 | tf_op jit(solution)/shard_map/ppermute | solution.py:245
  93.7 3.6 %shard_map.67.kept = f32[2,8,128,128]{3,2,1,0:T(8,128)S(1)} custom-call(s32[2]{0:T(128)S(1)} %pad_add_fusion.where, f32[4,128,128]{2,1,0:T(8,128)S(1)} %get-tuple-element.25.refs_0_, f32[4,128,128]{2,1,0:T(8,128)S(1)} %get-tuple-element.26.refs_1_, f32[4,128,128]{2,1,0:T(8,128)S(1)} %get-tuple-element.27.refs_2_, ...), custom_call_target="tpu_custom_call" | custom-call | flops 805306368 | bytes 2097152 | tf_op jit(solution)/shard_map/pallas_call | solution.py:246
  97.3 9.3 %collective-permute-done.23.halo = f32[2,4,128,128]{3,2,1,0:T(8,128)S(1)} collective-permute-done((f32[2,4,128,128]{3,2,1,0:T(8,128)S(1)}, f32[2,4,128,128]{3,2,1,0:T(8,128)S(1)}, u32[]{:S(2)}, u32[]{:S(2)}) %collective-permute-start.23) | collective-permute-done | bytes 524320 | tf_op jit(solution)/shard_map/ppermute | solution.py:245
  106.5 8.6 %collective-permute-done.22.ss = f32[2,4,128,128]{3,2,1,0:T(8,128)S(1)} collective-permute-done((f32[2,4,128,128]{3,2,1,0:T(8,128)S(1)}, f32[2,4,128,128]{3,2,1,0:T(8,128)S(1)}, u32[]{:S(2)}, u32[]{:S(2)}) %collective-permute-start.22) | collective-permute-done | bytes 524320 | tf_op jit(solution)/shard_map/ppermute | solution.py:235
  115.2 1.7 %shard_map.69 = f32[2,1,8,128,128]{4,3,2,1,0:T(8,128)} custom-call(s32[2]{0:T(128)S(1)} %pad_add_fusion.where, s32[2,1,8]{2,1,0:T(1,128)S(1)} %copy-done.2, f32[2,8,128,128]{3,2,1,0:T(8,128)S(1)} %shard_map.67.kept, f32[2,4,128,128]{3,2,1,0:T(8,128)S(1)} %collective-permute-done.22.ss, f32[2,4,128,128]{3,2,1,0:T(8,128)S(1)} %collective-permute-done.23.halo), custom_call_target="tpu_custom_call" | custom-call | bytes 2097152 | tf_op jit(solution)/shard_map/pallas_call | solution.py:254
  (65 shorter events, 7.1 us)
Async XLA Ops:
  0.7 1.2 %copy-start = (f32[2,1,8,128,128]{4,3,2,1,0:T(8,128)S(1)}, f32[2,1,8,128,128]{4,3,2,1,0:T(8,128)}, u32[]{:S(2)}) copy-start(f32[2,1,8,128,128]{4,3,2,1,0:T(8,128)} %p.1) | copy-start | bytes 3145732
  1.9 6.6 %copy-start.1 = (f32[4,4,1,128,128]{4,3,2,1,0:T(8,128)S(1)}, f32[4,4,1,128,128]{4,3,2,1,0:T(8,128)}, u32[]{:S(2)}) copy-start(f32[4,4,1,128,128]{4,3,2,1,0:T(8,128)} %u.1) | copy-start | bytes 3145732
  3.3 5.9 %copy-start.4 = (f32[4,128,128]{2,1,0:T(8,128)}, f32[4,128,128]{2,1,0:T(8,128)S(1)}, u32[]{:S(2)}) copy-start(f32[4,128,128]{2,1,0:T(8,128)S(1)} %get-tuple-element.30.refs_9_) | copy-start | bytes 786436
  3.3 10.3 %collective-permute-start = (f32[4,128,128]{2,1,0:T(8,128)}, f32[4,128,128]{2,1,0:T(8,128)S(1)}, u32[]{:S(2)}, u32[]{:S(2)}) collective-permute-start(f32[4,128,128]{2,1,0:T(8,128)} %get-tuple-element.24), channel_id=1, source_target_pairs={{0,1},{1,0},{2,3},{3,2},{4,5},{5,4},{6,7},{7,6},{8,9},{9,8},{10,11... | collective-permute-start | bytes 786440 | tf_op jit(solution)/shard_map/ppermute | solution.py:205
  6.3 2.1 %copy-start.26 = (s32[4,4,1]{1,2,0:T(1,128)S(1)}, s32[4,4,1]{1,2,0:T(1,128)}, u32[]{:S(2)}) copy-start(s32[4,4,1]{1,2,0:T(1,128)} %param.7) | copy-start | bytes 196
  6.3 13.0 %collective-permute-start.13 = (f32[4,128,128]{2,1,0:T(8,128)}, f32[4,128,128]{2,1,0:T(8,128)S(1)}, u32[]{:S(2)}, u32[]{:S(2)}) collective-permute-start(f32[4,128,128]{2,1,0:T(8,128)} %get-tuple-element.31), channel_id=1, source_target_pairs={{0,1},{1,0},{2,3},{3,2},{4,5},{5,4},{6,7},{7,6},{8,9},{9,8},{10,11... | collective-permute-start | bytes 786440 | tf_op jit(solution)/shard_map/ppermute | solution.py:205
  6.3 15.0 %collective-permute-start.14 = (f32[4,128,128]{2,1,0:T(8,128)S(1)}, f32[4,128,128]{2,1,0:T(8,128)}, u32[]{:S(2)}, u32[]{:S(2)}) collective-permute-start(f32[4,128,128]{2,1,0:T(8,128)S(1)} %get-tuple-element.29.refs_8_), channel_id=1, source_target_pairs={{0,2},{2,0},{4,6},{6,4},{8,10},{10,8},{12,14},{14,12},{16,18},{18,... | collective-permute-start | bytes 786440 | tf_op jit(solution)/shard_map/ppermute | solution.py:208
  8.3 13.0 %collective-permute-start.15 = (f32[4,128,128]{2,1,0:T(8,128)S(1)}, f32[4,128,128]{2,1,0:T(8,128)}, u32[]{:S(2)}, u32[]{:S(2)}) collective-permute-start(f32[4,128,128]{2,1,0:T(8,128)S(1)} %get-tuple-element.30.refs_9_), channel_id=1, source_target_pairs={{0,2},{2,0},{4,6},{6,4},{8,10},{10,8},{12,14},{14,12},{16,18},{18,... | collective-permute-start | bytes 786440 | tf_op jit(solution)/shard_map/ppermute | solution.py:208
  9.2 15.6 %collective-permute-start.10 = (f32[4,128,128]{2,1,0:T(8,128)S(1)}, f32[4,128,128]{2,1,0:T(8,128)S(1)}, u32[]{:S(2)}, u32[]{:S(2)}) collective-permute-start(f32[4,128,128]{2,1,0:T(8,128)S(1)} %get-tuple-element.26.refs_1_), channel_id=1, source_target_pairs={{0,1},{1,0},{2,3},{3,2},{4,5},{5,4},{6,7},{7,6},{8,9},{9,8},{10,11... | collective-permute-start | bytes 786440 | tf_op jit(solution)/shard_map/ppermute | solution.py:205
  13.6 59.9 %copy-start.27 = (s32[4,4,1]{1,2,0:T(1,128)S(1)}, s32[4,4,1]{1,2,0:T(1,128)}, u32[]{:S(2)}) copy-start(s32[4,4,1]{1,2,0:T(1,128)} %param.10) | copy-start | bytes 196
  13.6 16.9 %collective-permute-start.11 = (f32[4,128,128]{2,1,0:T(8,128)S(1)}, f32[4,128,128]{2,1,0:T(8,128)S(1)}, u32[]{:S(2)}, u32[]{:S(2)}) collective-permute-start(f32[4,128,128]{2,1,0:T(8,128)S(1)} %get-tuple-element.27.refs_2_), channel_id=1, source_target_pairs={{0,1},{1,0},{2,3},{3,2},{4,5},{5,4},{6,7},{7,6},{8,9},{9,8},{10,11... | collective-permute-start | bytes 786440 | tf_op jit(solution)/shard_map/ppermute | solution.py:205
  19.2 16.9 %collective-permute-start.12 = (f32[4,128,128]{2,1,0:T(8,128)S(1)}, f32[4,128,128]{2,1,0:T(8,128)S(1)}, u32[]{:S(2)}, u32[]{:S(2)}) collective-permute-start(f32[4,128,128]{2,1,0:T(8,128)S(1)} %get-tuple-element.28.refs_3_), channel_id=1, source_target_pairs={{0,1},{1,0},{2,3},{3,2},{4,5},{5,4},{6,7},{7,6},{8,9},{9,8},{10,11... | collective-permute-start | bytes 786440 | tf_op jit(solution)/shard_map/ppermute | solution.py:205
  21.3 19.6 %collective-permute-start.9 = (f32[4,128,128]{2,1,0:T(8,128)S(1)}, f32[4,128,128]{2,1,0:T(8,128)S(1)}, u32[]{:S(2)}, u32[]{:S(2)}) collective-permute-start(f32[4,128,128]{2,1,0:T(8,128)S(1)} %get-tuple-element.25.refs_0_), channel_id=1, source_target_pairs={{0,1},{1,0},{2,3},{3,2},{4,5},{5,4},{6,7},{7,6},{8,9},{9,8},{10,11... | collective-permute-start | bytes 786440 | tf_op jit(solution)/shard_map/ppermute | solution.py:205
  21.3 22.0 %collective-permute-start.17 = (f32[4,128,128]{2,1,0:T(8,128)S(1)}, f32[4,128,128]{2,1,0:T(8,128)S(1)}, u32[]{:S(2)}, u32[]{:S(2)}) collective-permute-start(f32[4,128,128]{2,1,0:T(8,128)S(1)} %collective-permute-done.refs_11_), channel_id=1, source_target_pairs={{0,2},{2,0},{4,6},{6,4},{8,10},{10,8},{12,14},{14,12},{16,18},{18,... | collective-permute-start | bytes 786440 | tf_op jit(solution)/shard_map/ppermute | solution.py:208
  23.3 0.7 copy-start.6
  25.5 18.1 %collective-permute-start.16 = (f32[4,128,128]{2,1,0:T(8,128)S(1)}, f32[4,128,128]{2,1,0:T(8,128)}, u32[]{:S(2)}, u32[]{:S(2)}) collective-permute-start(f32[4,128,128]{2,1,0:T(8,128)S(1)} %collective-permute-done.13.refs_10_), channel_id=1, source_target_pairs={{0,2},{2,0},{4,6},{6,4},{8,10},{10,8},{12,14},{14,12},{16,18},{18,... | collective-permute-start | bytes 786440 | tf_op jit(solution)/shard_map/ppermute | solution.py:208
  27.6 0.7 copy-start.8
  30.5 0.7 copy-start.12
  31.2 14.2 %collective-permute-start.18 = (f32[4,128,128]{2,1,0:T(8,128)}, f32[4,128,128]{2,1,0:T(8,128)S(1)}, u32[]{:S(2)}, u32[]{:S(2)}) collective-permute-start(f32[4,128,128]{2,1,0:T(8,128)} %collective-permute-done.14.refs_12_), channel_id=1, source_target_pairs={{0,4},{4,8},{8,12},{12,16},{16,20},{20,24},{24,28},{6,2},{10,6},{1... | collective-permute-start | bytes 786440 | tf_op jit(solution)/shard_map/ppermute | solution.py:211
  36.8 9.6 %collective-permute-start.19 = (f32[4,128,128]{2,1,0:T(8,128)}, f32[4,128,128]{2,1,0:T(8,128)S(1)}, u32[]{:S(2)}, u32[]{:S(2)}) collective-permute-start(f32[4,128,128]{2,1,0:T(8,128)} %collective-permute-done.15.refs_13_), channel_id=1, source_target_pairs={{0,4},{4,8},{8,12},{12,16},{16,20},{20,24},{24,28},{6,2},{10,6},{1... | collective-permute-start | bytes 786440 | tf_op jit(solution)/shard_map/ppermute | solution.py:211
  40.9 0.7 copy-start.16
  41.6 9.9 %collective-permute-start.1 = (f32[4,128,128]{2,1,0:T(8,128)S(1)}, f32[4,128,128]{2,1,0:T(8,128)S(1)}, u32[]{:S(2)}, u32[]{:S(2)}) collective-permute-start(f32[4,128,128]{2,1,0:T(8,128)S(1)} %get-tuple-element.25.refs_0_), channel_id=1, source_target_pairs={{0,2},{2,0},{4,6},{6,4},{8,10},{10,8},{12,14},{14,12},{16,18},{18,... | collective-permute-start | bytes 786440 | tf_op jit(solution)/shard_map/ppermute | solution.py:208
  43.3 12.3 %collective-permute-start.2 = (f32[4,128,128]{2,1,0:T(8,128)S(1)}, f32[4,128,128]{2,1,0:T(8,128)S(1)}, u32[]{:S(2)}, u32[]{:S(2)}) collective-permute-start(f32[4,128,128]{2,1,0:T(8,128)S(1)} %get-tuple-element.26.refs_1_), channel_id=1, source_target_pairs={{0,2},{2,0},{4,6},{6,4},{8,10},{10,8},{12,14},{14,12},{16,18},{18,... | collective-permute-start | bytes 786440 | tf_op jit(solution)/shard_map/ppermute | solution.py:208
  43.6 17.5 %collective-permute-start.3 = (f32[4,128,128]{2,1,0:T(8,128)S(1)}, f32[4,128,128]{2,1,0:T(8,128)S(1)}, u32[]{:S(2)}, u32[]{:S(2)}) collective-permute-start(f32[4,128,128]{2,1,0:T(8,128)S(1)} %get-tuple-element.27.refs_2_), channel_id=1, source_target_pairs={{0,2},{2,0},{4,6},{6,4},{8,10},{10,8},{12,14},{14,12},{16,18},{18,... | collective-permute-start | bytes 786440 | tf_op jit(solution)/shard_map/ppermute | solution.py:208
  45.4 0.7 copy-start.20
  46.1 20.6 %collective-permute-start.4 = (f32[4,128,128]{2,1,0:T(8,128)S(1)}, f32[4,128,128]{2,1,0:T(8,128)S(1)}, u32[]{:S(2)}, u32[]{:S(2)}) collective-permute-start(f32[4,128,128]{2,1,0:T(8,128)S(1)} %get-tuple-element.28.refs_3_), channel_id=1, source_target_pairs={{0,2},{2,0},{4,6},{6,4},{8,10},{10,8},{12,14},{14,12},{16,18},{18,... | collective-permute-start | bytes 786440 | tf_op jit(solution)/shard_map/ppermute | solution.py:208
  46.3 0.7 copy-start.22
  47.1 22.3 %collective-permute-start.21 = (f32[4,128,128]{2,1,0:T(8,128)S(1)}, f32[4,128,128]{2,1,0:T(8,128)S(1)}, u32[]{:S(2)}, u32[]{:S(2)}) collective-permute-start(f32[4,128,128]{2,1,0:T(8,128)S(1)} %collective-permute-done.17.refs_15_), channel_id=1, source_target_pairs={{0,4},{4,8},{8,12},{12,16},{16,20},{20,24},{24,28},{6,2},{10,6},{1... | collective-permute-start | bytes 786440 | tf_op jit(solution)/shard_map/ppermute | solution.py:211
  50.8 0.7 copy-start.18
  51.5 22.1 %collective-permute-start.20 = (f32[4,128,128]{2,1,0:T(8,128)}, f32[4,128,128]{2,1,0:T(8,128)}, u32[]{:S(2)}, u32[]{:S(2)}) collective-permute-start(f32[4,128,128]{2,1,0:T(8,128)} %collective-permute-done.16.refs_14_), channel_id=1, source_target_pairs={{0,4},{4,8},{8,12},{12,16},{16,20},{20,24},{24,28},{6,2},{10,6},{1... | collective-permute-start | bytes 786440 | tf_op jit(solution)/shard_map/ppermute | solution.py:211
  55.7 33.5 %collective-permute-start.5 = (f32[4,128,128]{2,1,0:T(8,128)S(1)}, f32[4,128,128]{2,1,0:T(8,128)S(1)}, u32[]{:S(2)}, u32[]{:S(2)}) collective-permute-start(f32[4,128,128]{2,1,0:T(8,128)S(1)} %collective-permute-done.1.refs_4_.refs_0_), channel_id=1, source_target_pairs={{0,4},{4,8},{8,12},{12,16},{16,20},{20,24},{24,28},{6,2},{10,6},{1... | collective-permute-start | bytes 786440 | tf_op jit(solution)/shard_map/ppermute | solution.py:211
  61.1 28.1 %collective-permute-start.6 = (f32[4,128,128]{2,1,0:T(8,128)S(1)}, f32[4,128,128]{2,1,0:T(8,128)S(1)}, u32[]{:S(2)}, u32[]{:S(2)}) collective-permute-start(f32[4,128,128]{2,1,0:T(8,128)S(1)} %collective-permute-done.2.refs_5_.refs_1_), channel_id=1, source_target_pairs={{0,4},{4,8},{8,12},{12,16},{16,20},{20,24},{24,28},{6,2},{10,6},{1... | collective-permute-start | bytes 786440 | tf_op jit(solution)/shard_map/ppermute | solution.py:211
  66.7 22.5 %collective-permute-start.7 = (f32[4,128,128]{2,1,0:T(8,128)S(1)}, f32[4,128,128]{2,1,0:T(8,128)S(1)}, u32[]{:S(2)}, u32[]{:S(2)}) collective-permute-start(f32[4,128,128]{2,1,0:T(8,128)S(1)} %collective-permute-done.3.refs_6_.refs_2_), channel_id=1, source_target_pairs={{0,4},{4,8},{8,12},{12,16},{16,20},{20,24},{24,28},{6,2},{10,6},{1... | collective-permute-start | bytes 786440 | tf_op jit(solution)/shard_map/ppermute | solution.py:211
  70.0 19.2 %collective-permute-start.8 = (f32[4,128,128]{2,1,0:T(8,128)S(1)}, f32[4,128,128]{2,1,0:T(8,128)S(1)}, u32[]{:S(2)}, u32[]{:S(2)}) collective-permute-start(f32[4,128,128]{2,1,0:T(8,128)S(1)} %collective-permute-done.4.refs_7_.refs_3_), channel_id=1, source_target_pairs={{0,4},{4,8},{8,12},{12,16},{16,20},{20,24},{24,28},{6,2},{10,6},{1... | collective-permute-start | bytes 786440 | tf_op jit(solution)/shard_map/ppermute | solution.py:211
  73.6 1.0 copy-start.5
  74.6 0.9 copy-start.7
  75.5 0.9 copy-start.9
  76.5 0.9 copy-start.11
  77.4 0.9 copy-start.13
  78.4 0.9 copy-start.15
  79.3 0.9 copy-start.17
  80.3 0.9 copy-start.19
  81.2 0.9 copy-start.21
  82.2 0.9 copy-start.23
  83.1 0.9 copy-start.25
  91.6 14.9 %collective-permute-start.23 = (f32[2,4,128,128]{3,2,1,0:T(8,128)S(1)}, f32[2,4,128,128]{3,2,1,0:T(8,128)S(1)}, u32[]{:S(2)}, u32[]{:S(2)}) collective-permute-start(f32[2,4,128,128]{3,2,1,0:T(8,128)S(1)} %shard_map.68), channel_id=1, source_target_pairs={{0,1},{1,0},{2,3},{3,2},{4,5},{5,4},{6,7},{7,6},{8,9},{9,8},{10,11... | collective-permute-start | bytes 1572872 | tf_op jit(solution)/shard_map/ppermute | solution.py:245
  93.1 22.0 %copy-start.2 = (s32[2,1,8]{2,1,0:T(1,128)S(1)}, s32[2,1,8]{2,1,0:T(1,128)}, u32[]{:S(2)}) copy-start(s32[2,1,8]{2,1,0:T(1,128)} %o_mask.1) | copy-start | bytes 196
  93.1 22.0 %collective-permute-start.22 = (f32[2,4,128,128]{3,2,1,0:T(8,128)S(1)}, f32[2,4,128,128]{3,2,1,0:T(8,128)S(1)}, u32[]{:S(2)}, u32[]{:S(2)}) collective-permute-start(f32[2,4,128,128]{3,2,1,0:T(8,128)S(1)} %get-tuple-element.34), channel_id=1, source_target_pairs={{0,1},{1,0},{2,3},{3,2},{4,5},{5,4},{6,7},{7,6},{8,9},{9,8},{10,11... | collective-permute-start | bytes 1572872 | tf_op jit(solution)/shard_map/ppermute | solution.py:235
  (4 other events, 2.8 us)

commit v2 on v1

v2 whole, which is shorter than its diff:
```python
import functools

import jax
import jax.numpy as jnp
from jax import lax
from jax.experimental import pallas as pl
from jax.experimental.pallas import tpu as pltpu
from jax.sharding import PartitionSpec as P

SLABS = ("row", "col")
LIMIT = 63
F32 = jnp.float32
BF16 = jnp.bfloat16
VMEM = pl.BlockSpec(memory_space=pltpu.VMEM)
SMEM = pl.BlockSpec(memory_space=pltpu.SMEM)
ANY = pl.BlockSpec(memory_space=pl.ANY)

PACK = (
    [(0, 0), (0, 1), (0, 2), (0, 3), (1, 0), (1, 1), (1, 2), (2, 0), (2, 1), (2, 2), (1, 3), (2, 3)]
    + [(3, 0), (3, 1), (3, 2), (3, 3)],
    [(0, 2), (0, 3), (1, 1), (1, 2), (1, 3), (2, 1), (2, 2), (2, 3), (3, 0), (3, 1), (3, 2), (3, 3)]
    + [(0, 0), (0, 1), (1, 0), (2, 0)],
)
PIECES = (6, 6, 4)


def shape(*dims, dtype=F32):
    return jax.ShapeDtypeStruct(dims, dtype)


def call(body, outs, ins, scratch=(), flops=0, alias=None, out_spec=VMEM):
    return pl.pallas_call(
        body,
        out_shape=outs,
        in_specs=ins,
        out_specs=[out_spec] * len(outs),
        scratch_shapes=list(scratch),
        input_output_aliases=alias or {},
        cost_estimate=pl.CostEstimate(flops=flops, bytes_accessed=0, transcendentals=0),
        compiler_params=pltpu.CompilerParams(vmem_limit_bytes=LIMIT << 20),
    )


def halves(x):
    high = x.astype(BF16)
    return high, (x - high.astype(F32)).astype(BF16)


def dot3(a, b, rhs_contract):
    one = functools.partial(
        lax.dot_general,
        dimension_numbers=(((1,), (rhs_contract,)), ((), ())),
        preferred_element_type=F32,
    )
    return one(a[0], b[0]) + (one(a[0], b[1]) + one(a[1], b[0]))


def joined(blocks, axis):
    return [jnp.concatenate(x, axis=axis) for x in zip(*[halves(b) for b in blocks])]


def aligned(block, size):
    return pl.multiple_of(block * size, size)


def slot_base(i, layer):
    return i // 2 if i % 2 == 0 else (i + 1) // 2 - layer


def start(src, dst, sem):
    copy = pltpu.make_async_copy(src, dst, sem)
    copy.start()
    return copy


def keep_p(total_rows, where, p_mask_any, p_any, *refs):
    outs, (p_mask, p, sems) = refs[0:4], refs[4:]
    copies = [start(p_any.at[a], p.at[a], sems.at[a]) for a in range(2)]
    start(p_mask_any, p_mask, sems.at[2]).wait()
    slab, layer = where[0], where[1]
    for a in range(2):
        copies[a].wait()
        row = slab * 4 + 2 * a + layer
        for o in range(8):
            col = row - 4 + o
            inside = (col >= 0) & (col < total_rows)
            keep = jnp.where(inside, p_mask[a, 0, o], 0).astype(F32)
            outs[2 * (o % 2) + a][o // 2] = p[a, 0, o] * keep


def keep_u(where, u_mask, u_any, *refs):
    rows, packed, (u, sem) = refs[0], refs[1:4], refs[4:]
    start(u_any, u, sem).wait()
    even = where[0] % 2 == 0
    for i in range(4):
        for m in range(4):
            rows[i, m] = u[i, m, 0] * u_mask[i, m, 0].astype(F32)
    for par, case in ((0, even), (1, jnp.logical_not(even))):

        @pl.when(case)
        def _(par=par):
            for n, (r, m) in enumerate(PACK[par]):
                packed[n // 6][n % 6] = rows[r, m]


def fill_band(size, stage, hi_ref, lo_ref, shift, rows):
    for a in rows:
        for c in range(6):
            e = c - a - shift
            at = (pl.ds(a * size, size), pl.ds(c * size, size))
            if 0 <= e < 4:
                hi_ref[at], lo_ref[at] = halves(stage[a, e])
            else:
                hi_ref[at] = jnp.zeros((size, size), BF16)
                lo_ref[at] = jnp.zeros((size, size), BF16)


def gather_band(where, mine, other_y, other_z, stage, sems):
    even = where[0] % 2 == 0
    at_y, at_z = jnp.where(even, 4, 0), jnp.where(even, 0, 4)
    copies = []
    for a in range(2):
        copies.append(start(mine[a], stage.at[2 + a], sems.at[a]))
        copies.append(start(other_y[a], stage.at[at_y + a], sems.at[2 + a]))
        copies.append(start(other_z[a], stage.at[at_z + a], sems.at[4 + a]))
    return copies


def product_own(size, where, u_any, *refs):
    mine, other_y, other_z = refs[0:2], refs[2:4], refs[4:6]
    out, stage, u, hi, lo, sems = refs[6:]
    layer = where[1]
    copies = gather_band(where, mine, other_y, other_z, stage, sems)
    copy = start(u_any, u, sems.at[6])
    for c in copies:
        c.wait()
    fill_band(size, stage, hi, lo, -2, range(6))
    copy.wait()
    for i in range(4):
        left = joined([u[i, m] for m in range(4)], 1)
        rows = pl.ds(aligned(slot_base(i, layer), size), 4 * size)
        out[i] = dot3(left, (hi[rows, rows], lo[rows, rows]), 0)


def product_t(size, where, t_mask, u_any, t_own, u_cross, *refs):
    mine, other_y, other_z = refs[0:2], refs[2:4], refs[4:6]
    t_hi, t_lo, ss = refs[6:9]
    stage, u, u_oth, t_part, hi, lo, ud_hi, ud_lo, sems = refs[9:]
    layer = where[1]
    copies = gather_band(where, mine, other_y, other_z, stage, sems)
    u_copy = start(u_any, u, sems.at[6])
    t_copy = start(t_own, t_part, sems.at[7])
    x_copies = [start(u_cross.at[pl.ds(2 * h, 2)], u_oth.at[pl.ds(2 * h, 2)], sems.at[8 + h]) for h in range(2)]
    u_copy.wait()
    ud_hi[...] = jnp.zeros_like(ud_hi)
    ud_lo[...] = jnp.zeros_like(ud_lo)
    for i in range(4):
        cols = pl.ds(aligned(slot_base(i, layer), size), 4 * size)
        rows = pl.ds(i * size, size)
        blocks = [u[i, m] for m in range(4)]
        ud_hi[rows, cols], ud_lo[rows, cols] = joined(blocks, 1)
    for c in copies:
        c.wait()
    fill_band(size, stage, hi, lo, -1, range(6))
    t_copy.wait()
    for i in range(4):
        if i % 2 == 0:
            x_copies[i // 2].wait()
        other = joined([u_oth[i, m] for m in range(4)], 1)
        rows = pl.ds(aligned(slot_base(i, 1 - layer), size), 4 * size)
        cols = pl.ds(aligned(i // 2 + layer if i % 2 == 0 else (i + 1) // 2, size), 4 * size)
        total = t_part[i] + dot3(other, (hi[rows, cols], lo[rows, cols]), 0)
        kept = jnp.concatenate(
            [total[:, m * size : (m + 1) * size] * t_mask[i, m, 0].astype(F32) for m in range(4)], axis=1
        )
        t_hi[i], t_lo[i] = halves(kept)
    for q in range(2):
        i = 2 * q + 1 - layer
        cols = pl.ds(aligned(q + 1 - layer, size), 4 * size)
        sums = dot3((t_hi[i], t_lo[i]), (ud_hi[:, cols], ud_lo[:, cols]), 1)
        for r in range(4):
            ss[q, r] = sums[:, r * size : (r + 1) * size]


def gather_halo(u_y, u_z, stage, sems):
    spots = [stage.at[pl.ds(at, n)] for at, n in ((0, 6), (6, 6), (12, 4), (16, 6), (22, 6))]
    return [start(src, dst, sems.at[n]) for n, (src, dst) in enumerate(zip([*u_y, *u_z], spots))]


def fill_halo(size, where, stage, uh_hi, uh_lo):
    even, layer = where[0] % 2 == 0, where[1]
    uh_hi[...] = jnp.zeros_like(uh_hi)
    uh_lo[...] = jnp.zeros_like(uh_lo)
    for below_at, above_at, pack, case in ((16, 0, PACK[1], even), (0, 16, PACK[0], jnp.logical_not(even))):

        @pl.when(case)
        def _(below_at=below_at, above_at=above_at, pack=pack):
            for first, base, limit in ((below_at, 0, 4), (above_at, 4, 3)):
                for n, (r, m) in enumerate(pack[: 16 if first == 0 else 12]):
                    if r >= limit:
                        continue
                    rows = pl.ds((base + r) * size, size)
                    cols = pl.ds(aligned(slot_base(r, layer) + base + m, size), size)
                    uh_hi[rows, cols], uh_lo[rows, cols] = halves(stage[first + n])


def halo_sums(size, i, base, t_hi, t_lo, uh_hi, uh_lo):
    cols = pl.ds(aligned(base + 2, size), 4 * size)
    rows = [pl.ds(aligned(jnp.where(t < i, 4 + t, t), size), size) for t in range(4)]
    hi = jnp.concatenate([uh_hi[r, cols] for r in rows], axis=0)
    lo = jnp.concatenate([uh_lo[r, cols] for r in rows], axis=0)
    return dot3((t_hi[i], t_lo[i]), (hi, lo), 1)


def send_halo(size, where, *refs):
    u_y, u_z, t_any = refs[0:3], refs[3:5], refs[5:7]
    out, stage, t_hi, t_lo, uh_hi, uh_lo, sems = refs[7:]
    layer = where[1]
    copies = gather_halo(u_y, u_z, stage, sems)
    copies += [start(t_any[n], (t_hi, t_lo)[n], sems.at[7 + n]) for n in range(2)]
    for c in copies:
        c.wait()
    fill_halo(size, where, stage, uh_hi, uh_lo)
    for q in range(2):
        sums = halo_sums(size, 2 * q + 1 - layer, q + 1 - layer, t_hi, t_lo, uh_hi, uh_lo)
        for t in range(4):
            out[q, t] = sums[:, t * size : (t + 1) * size]


def out_keep(total_rows, where, o_mask, q, o):
    col = where[0] * 4 + 2 * q + where[1] - 4 + o
    return jnp.where((col >= 0) & (col < total_rows), o_mask[q, 0, o], 0).astype(F32)


def keep_rows(total_rows, size, where, o_mask, u_any, ss_any, *refs):
    u_y, u_z, t_any = refs[0:3], refs[3:5], refs[5:7]
    out, stage, u, ss, t_hi, t_lo, uh_hi, uh_lo, ud_hi, ud_lo, sems = refs[7:]
    layer = where[1]
    copies = gather_halo(u_y, u_z, stage, sems)
    copies += [start(t_any[n], (t_hi, t_lo)[n], sems.at[7 + n]) for n in range(2)]
    copies += [start(u_any, u, sems.at[9]), start(ss_any, ss, sems.at[10])]
    for c in copies:
        c.wait()
    fill_halo(size, where, stage, uh_hi, uh_lo)
    ud_hi[...] = jnp.zeros_like(ud_hi)
    ud_lo[...] = jnp.zeros_like(ud_lo)
    for i in range(4):
        cols = pl.ds(aligned(slot_base(i, layer), size), 4 * size)
        rows = pl.ds(i * size, size)
        blocks = [u[i, m] for m in range(4)]
        ud_hi[rows, cols], ud_lo[rows, cols] = joined(blocks, 1)
    for q in range(2):
        i = 2 * q + layer
        sums = halo_sums(size, i, q, t_hi, t_lo, uh_hi, uh_lo)
        for t in range(4):
            out[q, 0, (8 - i + t) % 8] = sums[:, t * size : (t + 1) * size]
        cols = pl.ds(q * size, 4 * size)
        sums = dot3((t_hi[i], t_lo[i]), (ud_hi[:, cols], ud_lo[:, cols]), 1)
        for r in range(4):
            o = (4 - i + r) % 8
            keep = out_keep(total_rows, where, o_mask, q, o)
            out[q, 0, o] = (sums[:, r * size : (r + 1) * size] + ss[q, r]) * keep


def combine(total_rows, where, o_mask, kept_any, halo_any, out_any, kept, halo, sems):
    layer = where[1]
    copies = []
    for q in range(2):
        i = 2 * q + layer
        first = start(halo_any.at[q], halo.at[q], sems.at[8 + q])
        rest = [start(kept_any.at[q, 0, (8 - i + t) % 8], kept.at[q, t], sems.at[4 * q + t]) for t in range(4)]
        copies.append((first, rest))
    stores = []
    for q in range(2):
        i = 2 * q + layer
        copies[q][0].wait()
        for t in range(4):
            o = (8 - i + t) % 8
            copies[q][1][t].wait()
            kept[q, t] = (kept[q, t] + halo[q, t]) * out_keep(total_rows, where, o_mask, q, o)
            stores.append(start(kept.at[q, t], out_any.at[q, 0, o], sems.at[10 + 4 * q + t]))
    for s in stores:
        s.wait()


def after(x, *others):
    return lax.optimization_barrier((x, *others))[0]


def on_device(u_values, u_mask, p_values, p_mask, t_mask, out_mask):
    size = u_values.shape[-1]
    slabs = lax.axis_size(SLABS)
    total_rows = slabs * u_values.shape[0]
    where = jnp.stack([lax.axis_index(SLABS), lax.axis_index("layer")]).astype(jnp.int32)
    swap = [(0, 1), (1, 0)]
    pair = [(s, s ^ 1) for s in range(slabs)]
    onward = [(s, s + 2) for s in range(0, slabs - 2, 2)] + [(s, s - 2) for s in range(3, slabs, 2)]

    def over_layer(x):
        return lax.ppermute(x, "layer", swap)

    def over_pair(x):
        return lax.ppermute(x, SLABS, pair)

    def onto(x):
        return lax.ppermute(x, SLABS, onward)

    def vmem(*dims, dtype=F32):
        return pltpu.VMEM(dims, dtype)

    def sems(n):
        return pltpu.SemaphoreType.DMA((n,))

    four = shape(4, size, size)
    six = shape(6, size, size)
    eight = shape(2, 4, size, size)
    sixteen = shape(4, 4, size, size)
    wide = 6 * size
    unit = 3 * 2 * (4 * size) ** 2 * size
    p_like = pltpu.VMEM(p_values.shape, F32)
    pe0, pe1, po0, po1 = call(
        functools.partial(keep_p, total_rows),
        [four] * 4,
        [SMEM, ANY, ANY],
        [pltpu.SMEM(p_mask.shape, jnp.int32), p_like, sems(3)],
    )(where, p_mask, p_values)
    pe = [pe0, pe1]
    pc = [over_layer(x) for x in (po0, po1)]
    pe_y = [over_pair(x) for x in pe]
    u_own, *packed = call(
        keep_u,
        [sixteen, six, six, four],
        [SMEM, SMEM, ANY],
        [pltpu.VMEM(u_values.shape, F32), pltpu.SemaphoreType.DMA],
    )(where, u_mask, u_values)
    u_oth = over_layer(after(u_own, pc[0]))
    pe_z = [onto(after(x, u_own)) for x in pe_y]
    pc_y = [over_pair(after(x, y)) for x, y in zip(pc, pe_y)]
    pc_z = [onto(after(x, z)) for x, z in zip(pc_y, pe_z)]
    band = [vmem(wide, wide, dtype=BF16)] * 2
    own_rows = [vmem(4 * size, wide, dtype=BF16)] * 2
    (t_own,) = call(
        functools.partial(product_own, size),
        [shape(4, size, 4 * size)],
        [SMEM] + [ANY] * 7,
        [vmem(6, 4, size, size), vmem(4, 4, size, size), *band, sems(7)],
        flops=4 * unit,
    )(where, u_own, *pe, *pe_y, *pe_z)
    u_y = [over_pair(after(x, pc[1], y)) for x, y in zip(packed[:2], pc_y)]
    u_y.append(over_pair(after(packed[2], u_y[0])))
    u_z = [onto(after(u_y[0], pc_z[0])), onto(after(u_y[1], pc_z[1], t_own))]
    t_hi, t_lo, ss = call(
        functools.partial(product_t, size),
        [shape(4, size, 4 * size, dtype=BF16)] * 2 + [eight],
        [SMEM] * 2 + [ANY] * 9,
        [vmem(6, 4, size, size)]
        + [vmem(4, 4, size, size)] * 2
        + [vmem(4, size, 4 * size), *band, *own_rows, sems(10)],
        flops=6 * unit,
    )(where, t_mask, u_own, t_own, u_oth, *pc, *pc_y, *pc_z)
    ss_got = over_layer(ss)
    halo_scratch = [vmem(7 * size, 9 * size, dtype=BF16)] * 2
    t_scratch = [vmem(4, size, 4 * size, dtype=BF16)] * 2
    (halo,) = call(
        functools.partial(send_halo, size),
        [eight],
        [SMEM] + [ANY] * 7,
        [vmem(28, size, size), *t_scratch, *halo_scratch, sems(9)],
        flops=2 * unit,
    )(where, *u_y, *u_z, t_hi, t_lo)
    halo_got = over_layer(halo)
    (kept,) = call(
        functools.partial(keep_rows, total_rows, size),
        [shape(*p_values.shape)],
        [SMEM] * 2 + [ANY] * 9,
        [vmem(28, size, size), vmem(4, 4, size, size), vmem(2, 4, size, size)]
        + [*t_scratch, *halo_scratch, *own_rows, sems(11)],
        flops=4 * unit,
    )(where, out_mask, u_own, ss_got, *u_y, *u_z, t_hi, t_lo)
    (out,) = call(
        functools.partial(combine, total_rows),
        [shape(*p_values.shape)],
        [SMEM, SMEM, ANY, ANY],
        [vmem(2, 4, size, size)] * 2 + [sems(18)],
        alias={2: 0},
        out_spec=ANY,
    )(where, out_mask, kept, halo_got)
    return out


def solution(mesh):
    placed = (
        P(SLABS, None, "layer", None, None),
        P(SLABS, None, "layer"),
        P(SLABS, "layer", None, None, None),
        P(SLABS, "layer", None),
        P(SLABS, None, "layer"),
        P(SLABS, "layer", None),
    )
    return jax.shard_map(
        on_device,
        mesh=mesh,
        in_specs=placed,
        out_specs=P(SLABS, "layer", None, None, None),
        check_vma=False,
    )
```

time: 118 us -> 90.6 us (0.77)
  local copies, waits for them, and re-layouts: 19.5 us -> 2.23 us
  Pallas kernels: 14.9 us -> 31.7 us
  starting transfers between devices: 52.8 us -> 36.7 us
  waiting for transfers between devices: 29.5 us -> 18.7 us
    unnamed x58 -> x16, local copies, waits for them, and re-layouts: 19.5 us -> 2.23 us
    ppermute x24 -> x18, starting transfers between devices: 52.8 us -> 36.7 us  [the longest x6 23.8 us: onto(): return lax.ppermute(x, SLABS, onward)]
    pallas_call x5 -> x6, Pallas kernels: 9.83 us -> 25.4 us  [the longest x1 6.8 us: on_device(): call(functools.partial(keep_rows, total_rows, size), [shape(*p_values.sha...]
    ppermute x24 -> x18, waiting for transfers between devices: 29.5 us -> 18.7 us  [the longest x5 11.4 us: over_layer(): return lax.ppermute(x, 'layer', swap)]
    pallas_call x1, Pallas kernels: 5.06 us -> 6.27 us  [on_device(): call(functools.partial(product_t, size), [shape(4, size, 4 * size, dtype=...]
  transfers between devices with their start and end apart: 24 -> 18, of which waited for: 9 -> 8; matrix products, arithmetic and copies ran while one was open for 0% -> 2% of each run, Pallas kernels for 8% -> 29%
where the time goes in v2:
time: 90.6 us; the launch traced here: 90 us
  starting transfers between devices  36.7 us (41%)
  Pallas kernels  31.7 us (35%)
  waiting for transfers between devices  18.7 us (21%)
  local copies, waits for them, and re-layouts  2.23 us (2%)
    ppermute x6, starting transfers between devices, onto(): return lax.ppermute(x, SLABS, onward)  23.8 us
    ppermute x5, waiting for transfers between devices, over_layer(): return lax.ppermute(x, 'layer', swap)  11.4 us
    pallas_call x1, Pallas kernels, on_device(): call(functools.partial(keep_rows, total_rows, size), [shape(*p_values.sha...  6.8 us
    ppermute x7, starting transfers between devices, over_pair(): return lax.ppermute(x, SLABS, pair)  6.59 us
    ppermute x5, starting transfers between devices, over_layer(): return lax.ppermute(x, 'layer', swap)  6.34 us
    pallas_call x1, Pallas kernels, on_device(): call(functools.partial(product_t, size), [shape(4, size, 4 * size, dtype=...  6.27 us
    ppermute x7, waiting for transfers between devices, over_pair(): return lax.ppermute(x, SLABS, pair)  5.75 us
    pallas_call x1, Pallas kernels, on_device(): call(functools.partial(send_halo, size), [eight], [SMEM] + [ANY] * 7, [vm...  4.97 us
  transfers between devices with their start and end apart: 18, of which 8 were waited for; matrix products, arithmetic and copies ran while one was open for 2% of the time, Pallas kernels for 29%

profile of v2, /device:TPU:0, one launch (start us, length us, event | category | flops | bytes accessed | tf_op | source)
XLA Modules:
  0.0 90.0 jit_solution(4606946826946956771)
XLA Ops:
  0.0 0.6 pad_add_fusion.where
  0.6 2.9 %shard_map.65 = (f32[4,128,128]{2,1,0:T(8,128)}, f32[4,128,128]{2,1,0:T(8,128)}, f32[4,128,128]{2,1,0:T(8,128)}, f32[4,128,128]{2,1,0:T(8,128)}) custom-call(s32[2]{0:T(128)} %pad_add_fusion.where, s32[2,1,8]{2,1,0:T(1,128)} %p_mask_any.1, f32[2,1,8,128,128]{4,3,2,1,0:T(8,128)} %p_any.1), custom_call_target="tpu_custom_call" | custom-call | tf_op jit(solution)/shard_map/pallas_call | solution.py:321
  3.5 3.0 %collective-permute-start.4 = (f32[4,128,128]{2,1,0:T(8,128)}, f32[4,128,128]{2,1,0:T(8,128)S(1)}, u32[]{:S(2)}, u32[]{:S(2)}) collective-permute-start(f32[4,128,128]{2,1,0:T(8,128)} %get-tuple-element.33), channel_id=1, source_target_pairs={{0,1},{1,0},{2,3},{3,2},{4,5},{5,4},{6,7},{7,6},{8,9},{9,8},{10,11... | collective-permute-start | bytes 786440 | tf_op jit(solution)/shard_map/ppermute | solution.py:300
  6.5 1.5 %collective-permute-start = (f32[4,128,128]{2,1,0:T(8,128)}, f32[4,128,128]{2,1,0:T(8,128)}, u32[]{:S(2)}, u32[]{:S(2)}) collective-permute-start(f32[4,128,128]{2,1,0:T(8,128)} %get-tuple-element.29.refs_0_), channel_id=1, source_target_pairs={{0,2},{2,0},{4,6},{6,4},{8,10},{10,8},{12,14},{14,12},{16,18},{18,... | collective-permute-start | bytes 786440 | tf_op jit(solution)/shard_map/ppermute | solution.py:303
  8.0 0.5 collective-permute-start.1
  8.5 0.1 collective-permute-start.6
  8.6 0.7 copy.8.u_mask
  9.3 3.6 %shard_map.64 = (f32[4,4,128,128]{3,2,1,0:T(8,128)}, f32[6,128,128]{2,1,0:T(8,128)}, f32[6,128,128]{2,1,0:T(8,128)}, f32[4,128,128]{2,1,0:T(8,128)}) custom-call(s32[2]{0:T(128)} %pad_add_fusion.where, s32[4,4,1]{2,1,0:T(4,128)} %copy.8.u_mask, f32[4,4,1,128,128]{4,3,2,1,0:T(8,128)} %u_any.1), custom_call_target="tpu_custom_call" | custom-call | tf_op jit(solution)/shard_map/pallas_call | solution.py:330
  12.9 1.0 %collective-permute-done.4.refs_0_ = f32[4,128,128]{2,1,0:T(8,128)S(1)} collective-permute-done((f32[4,128,128]{2,1,0:T(8,128)}, f32[4,128,128]{2,1,0:T(8,128)S(1)}, u32[]{:S(2)}, u32[]{:S(2)}) %collective-permute-start.4) | collective-permute-done | bytes 262176 | tf_op jit(solution)/shard_map/ppermute | solution.py:300
  13.8 2.1 %collective-permute-start.5 = (f32[4,4,128,128]{3,2,1,0:T(8,128)}, f32[4,4,128,128]{3,2,1,0:T(8,128)}, u32[]{:S(2)}, u32[]{:S(2)}) collective-permute-start(f32[4,4,128,128]{3,2,1,0:T(8,128)} %get-tuple-element.34.u_any), channel_id=1, source_target_pairs={{0,1},{1,0},{2,3},{3,2},{4,5},{5,4},{6,7},{7,6},{8,9},{9,8},{10,11... | collective-permute-start | bytes 3145736 | tf_op jit(solution)/shard_map/ppermute | solution.py:300
  15.9 0.1 collective-permute-done.refs_2_
  16.0 1.5 %collective-permute-start.7 = (f32[4,128,128]{2,1,0:T(8,128)S(1)}, f32[4,128,128]{2,1,0:T(8,128)}, u32[]{:S(2)}, u32[]{:S(2)}) collective-permute-start(f32[4,128,128]{2,1,0:T(8,128)S(1)} %collective-permute-done.4.refs_0_), channel_id=1, source_target_pairs={{0,2},{2,0},{4,6},{6,4},{8,10},{10,8},{12,14},{14,12},{16,18},{18,... | collective-permute-start | bytes 786440 | tf_op jit(solution)/shard_map/ppermute | solution.py:303
  17.5 4.1 %collective-permute-done.1.refs_3_ = f32[4,128,128]{2,1,0:T(8,128)} collective-permute-done((f32[4,128,128]{2,1,0:T(8,128)}, f32[4,128,128]{2,1,0:T(8,128)}, u32[]{:S(2)}, u32[]{:S(2)}) %collective-permute-start.1) | collective-permute-done | bytes 262176 | tf_op jit(solution)/shard_map/ppermute | solution.py:303
  21.6 0.0 collective-permute-done.6.refs_1_
  21.6 1.5 %collective-permute-start.8 = (f32[4,128,128]{2,1,0:T(8,128)S(1)}, f32[4,128,128]{2,1,0:T(8,128)}, u32[]{:S(2)}, u32[]{:S(2)}) collective-permute-start(f32[4,128,128]{2,1,0:T(8,128)S(1)} %collective-permute-done.6.refs_1_), channel_id=1, source_target_pairs={{0,2},{2,0},{4,6},{6,4},{8,10},{10,8},{12,14},{14,12},{16,18},{18,... | collective-permute-start | bytes 786440 | tf_op jit(solution)/shard_map/ppermute | solution.py:303
  23.2 4.2 %collective-permute-start.2 = (f32[4,128,128]{2,1,0:T(8,128)}, f32[4,128,128]{2,1,0:T(8,128)}, u32[]{:S(2)}, u32[]{:S(2)}) collective-permute-start(f32[4,128,128]{2,1,0:T(8,128)} %collective-permute-done.refs_2_), channel_id=1, source_target_pairs={{0,4},{4,8},{8,12},{12,16},{16,20},{20,24},{24,28},{6,2},{10,6},{1... | collective-permute-start | bytes 786440 | tf_op jit(solution)/shard_map/ppermute | solution.py:306
  27.3 3.5 %collective-permute-start.3 = (f32[4,128,128]{2,1,0:T(8,128)}, f32[4,128,128]{2,1,0:T(8,128)}, u32[]{:S(2)}, u32[]{:S(2)}) collective-permute-start(f32[4,128,128]{2,1,0:T(8,128)} %collective-permute-done.1.refs_3_), channel_id=1, source_target_pairs={{0,4},{4,8},{8,12},{12,16},{16,20},{20,24},{24,28},{6,2},{10,6},{1... | collective-permute-start | bytes 786440 | tf_op jit(solution)/shard_map/ppermute | solution.py:306
  30.8 0.0 collective-permute-done.7.refs_2_
  30.8 0.0 copy-done.3
  30.8 0.0 collective-permute-start.12
  30.9 0.6 collective-permute-done.8.refs_3_
  31.4 1.5 %collective-permute-start.13 = (f32[6,128,128]{2,1,0:T(8,128)}, f32[6,128,128]{2,1,0:T(8,128)S(1)}, u32[]{:S(2)}, u32[]{:S(2)}) collective-permute-start(f32[6,128,128]{2,1,0:T(8,128)} %get-tuple-element.44), channel_id=1, source_target_pairs={{0,2},{2,0},{4,6},{6,4},{8,10},{10,8},{12,14},{14,12},{16,18},{18,... | collective-permute-start | bytes 1179656 | tf_op jit(solution)/shard_map/ppermute | solution.py:303
  32.9 0.0 collective-permute-done.2.refs_4_
  32.9 4.9 %collective-permute-start.9 = (f32[4,128,128]{2,1,0:T(8,128)}, f32[4,128,128]{2,1,0:T(8,128)}, u32[]{:S(2)}, u32[]{:S(2)}) collective-permute-start(f32[4,128,128]{2,1,0:T(8,128)} %collective-permute-done.7.refs_2_), channel_id=1, source_target_pairs={{0,4},{4,8},{8,12},{12,16},{16,20},{20,24},{24,28},{6,2},{10,6},{1... | collective-permute-start | bytes 786440 | tf_op jit(solution)/shard_map/ppermute | solution.py:306
  37.9 0.0 collective-permute-done.3.refs_5_
  37.9 4.2 %collective-permute-start.10 = (f32[4,128,128]{2,1,0:T(8,128)}, f32[4,128,128]{2,1,0:T(8,128)}, u32[]{:S(2)}, u32[]{:S(2)}) collective-permute-start(f32[4,128,128]{2,1,0:T(8,128)} %collective-permute-done.8.refs_3_), channel_id=1, source_target_pairs={{0,4},{4,8},{8,12},{12,16},{16,20},{20,24},{24,28},{6,2},{10,6},{1... | collective-permute-start | bytes 786440 | tf_op jit(solution)/shard_map/ppermute | solution.py:306
  42.1 4.5 %shard_map.66.t_own = f32[4,128,512]{2,1,0:T(8,128)} custom-call(s32[2]{0:T(128)} %pad_add_fusion.where, f32[4,4,128,128]{3,2,1,0:T(8,128)} %get-tuple-element.34.u_any, f32[4,128,128]{2,1,0:T(8,128)} %get-tuple-element.29.refs_0_, f32[4,128,128]{2,1,0:T(8,128)} %get-tuple-element.30.refs_1_, f32[4,128,128]{2,1,0:T(8,128)} %collective-permute-done.refs_2_, ...), custom_call_target="tpu_custom_call" | custom-call | flops 805306368 | tf_op jit(solution)/shard_map/pallas_call | solution.py:342
  46.6 0.0 collective-permute-done.9.refs_4_
  46.6 0.0 collective-permute-done.12.refs_0_
  46.7 3.5 %collective-permute-start.15 = (f32[6,128,128]{2,1,0:T(8,128)S(1)}, f32[6,128,128]{2,1,0:T(8,128)}, u32[]{:S(2)}, u32[]{:S(2)}) collective-permute-start(f32[6,128,128]{2,1,0:T(8,128)S(1)} %collective-permute-done.12.refs_0_), channel_id=1, source_target_pairs={{0,4},{4,8},{8,12},{12,16},{16,20},{20,24},{24,28},{6,2},{10,6},{1... | collective-permute-start | bytes 1179656 | tf_op jit(solution)/shard_map/ppermute | solution.py:306
  50.2 0.0 collective-permute-done.10.refs_5_
  50.2 0.0 collective-permute-done.13.refs_1_
  50.2 3.4 %collective-permute-start.16 = (f32[6,128,128]{2,1,0:T(8,128)S(1)}, f32[6,128,128]{2,1,0:T(8,128)}, u32[]{:S(2)}, u32[]{:S(2)}) collective-permute-start(f32[6,128,128]{2,1,0:T(8,128)S(1)} %collective-permute-done.13.refs_1_), channel_id=1, source_target_pairs={{0,4},{4,8},{8,12},{12,16},{16,20},{20,24},{24,28},{6,2},{10,6},{1... | collective-permute-start | bytes 1179656 | tf_op jit(solution)/shard_map/ppermute | solution.py:306
  53.6 0.0 collective-permute-start.14
  53.6 0.7 copy.9.t_mask
  54.3 0.0 collective-permute-done.5.u_cross
  54.3 6.3 %shard_map.67 = (bf16[4,128,512]{2,1,0:T(8,128)(2,1)}, bf16[4,128,512]{2,1,0:T(8,128)(2,1)}, f32[2,4,128,128]{3,2,1,0:T(8,128)}) custom-call(s32[2]{0:T(128)} %pad_add_fusion.where, s32[4,4,1]{2,1,0:T(4,128)} %copy.9.t_mask, f32[4,4,128,128]{3,2,1,0:T(8,128)} %get-tuple-element.34.u_any, f32[4,128,512]{2,1,0:T(8,128)} %shard_map.66.t_own, ...), custom_call_target="tpu_custom_call" | custom-call | flops 1207959552 | tf_op jit(solution)/shard_map/pallas_call | solution.py:352
  60.6 0.6 collective-permute-start.11
  61.2 0.9 %collective-permute-done.14.refs_2_ = f32[4,128,128]{2,1,0:T(8,128)} collective-permute-done((f32[4,128,128]{2,1,0:T(8,128)}, f32[4,128,128]{2,1,0:T(8,128)}, u32[]{:S(2)}, u32[]{:S(2)}) %collective-permute-start.14) | collective-permute-done | bytes 262176 | tf_op jit(solution)/shard_map/ppermute | solution.py:303
  62.2 0.0 collective-permute-done.15.refs_3_
  62.2 1.6 %collective-permute-done.16.refs_4_ = f32[6,128,128]{2,1,0:T(8,128)} collective-permute-done((f32[6,128,128]{2,1,0:T(8,128)S(1)}, f32[6,128,128]{2,1,0:T(8,128)}, u32[]{:S(2)}, u32[]{:S(2)}) %collective-permute-start.16) | collective-permute-done | bytes 393248 | tf_op jit(solution)/shard_map/ppermute | solution.py:306
  63.7 5.0 %shard_map.69 = f32[2,4,128,128]{3,2,1,0:T(8,128)} custom-call(s32[2]{0:T(128)} %pad_add_fusion.where, f32[6,128,128]{2,1,0:T(8,128)} %copy-done, f32[6,128,128]{2,1,0:T(8,128)} %copy-done.1, f32[4,128,128]{2,1,0:T(8,128)} %collective-permute-done.14.refs_2_, f32[6,128,128]{2,1,0:T(8,128)} %collective-permute-done.15.refs_3_, ...), custom_call_target="tpu_custom_call" | custom-call | flops 402653184 | tf_op jit(solution)/shard_map/pallas_call | solution.py:364
  68.7 0.6 collective-permute-start.17
  69.3 6.1 %collective-permute-done.11.ss_any = f32[2,4,128,128]{3,2,1,0:T(8,128)} collective-permute-done((f32[2,4,128,128]{3,2,1,0:T(8,128)}, f32[2,4,128,128]{3,2,1,0:T(8,128)}, u32[]{:S(2)}, u32[]{:S(2)}) %collective-permute-start.11) | collective-permute-done | bytes 524320 | tf_op jit(solution)/shard_map/ppermute | solution.py:300
  75.4 6.8 %shard_map.68.kept_any = f32[2,1,8,128,128]{4,3,2,1,0:T(8,128)} custom-call(s32[2]{0:T(128)} %pad_add_fusion.where, s32[2,1,8]{2,1,0:T(1,128)} %o_mask.3, f32[4,4,128,128]{3,2,1,0:T(8,128)} %get-tuple-element.34.u_any, f32[2,4,128,128]{3,2,1,0:T(8,128)} %collective-permute-done.11.ss_any, f32[6,128,128]{2,1,0:T(8,128)} %copy-done, f32[6,128,128]{2,1,0:T(8,128)} %copy-done.1, ...), custom_call_target="tpu_custom_call" | custom-call | flops 805306368 | tf_op jit(solution)/shard_map/pallas_call | solution.py:372
  82.2 4.3 %collective-permute-done.17.halo_any = f32[2,4,128,128]{3,2,1,0:T(8,128)S(1)} collective-permute-done((f32[2,4,128,128]{3,2,1,0:T(8,128)}, f32[2,4,128,128]{3,2,1,0:T(8,128)S(1)}, u32[]{:S(2)}, u32[]{:S(2)}) %collective-permute-start.17) | collective-permute-done | bytes 524320 | tf_op jit(solution)/shard_map/ppermute | solution.py:300
  86.5 0.8 copy-done.2
  87.3 2.7 %shard_map.70 = f32[2,1,8,128,128]{4,3,2,1,0:T(8,128)} custom-call(s32[2]{0:T(128)} %pad_add_fusion.where, s32[2,1,8]{2,1,0:T(1,128)} %o_mask.3, f32[2,1,8,128,128]{4,3,2,1,0:T(8,128)} %shard_map.68.kept_any, f32[2,4,128,128]{3,2,1,0:T(8,128)} %copy-done.2), custom_call_target="tpu_custom_call", output_to_operand_aliasing={{}: (2, {})} | custom-call | tf_op jit(solution)/shard_map/pallas_call | solution.py:380
  (12 shorter events, 0.0 us)
Async XLA Ops:
  3.5 10.3 %collective-permute-start.4 = (f32[4,128,128]{2,1,0:T(8,128)}, f32[4,128,128]{2,1,0:T(8,128)S(1)}, u32[]{:S(2)}, u32[]{:S(2)}) collective-permute-start(f32[4,128,128]{2,1,0:T(8,128)} %get-tuple-element.33), channel_id=1, source_target_pairs={{0,1},{1,0},{2,3},{3,2},{4,5},{5,4},{6,7},{7,6},{8,9},{9,8},{10,11... | collective-permute-start | bytes 786440 | tf_op jit(solution)/shard_map/ppermute | solution.py:300
  6.5 2.1 %copy-start.5 = (s32[4,4,1]{1,2,0:T(1,128)S(1)}, s32[4,4,1]{1,2,0:T(1,128)}, u32[]{:S(2)}) copy-start(s32[4,4,1]{1,2,0:T(1,128)} %param.7) | copy-start | bytes 196
  6.5 9.5 %collective-permute-start = (f32[4,128,128]{2,1,0:T(8,128)}, f32[4,128,128]{2,1,0:T(8,128)}, u32[]{:S(2)}, u32[]{:S(2)}) collective-permute-start(f32[4,128,128]{2,1,0:T(8,128)} %get-tuple-element.29.refs_0_), channel_id=1, source_target_pairs={{0,2},{2,0},{4,6},{6,4},{8,10},{10,8},{12,14},{14,12},{16,18},{18,... | collective-permute-start | bytes 786440 | tf_op jit(solution)/shard_map/ppermute | solution.py:303
  8.0 13.6 %collective-permute-start.1 = (f32[4,128,128]{2,1,0:T(8,128)}, f32[4,128,128]{2,1,0:T(8,128)}, u32[]{:S(2)}, u32[]{:S(2)}) collective-permute-start(f32[4,128,128]{2,1,0:T(8,128)} %get-tuple-element.30.refs_1_), channel_id=1, source_target_pairs={{0,2},{2,0},{4,6},{6,4},{8,10},{10,8},{12,14},{14,12},{16,18},{18,... | collective-permute-start | bytes 786440 | tf_op jit(solution)/shard_map/ppermute | solution.py:303
  8.5 13.1 %collective-permute-start.6 = (f32[4,128,128]{2,1,0:T(8,128)}, f32[4,128,128]{2,1,0:T(8,128)S(1)}, u32[]{:S(2)}, u32[]{:S(2)}) collective-permute-start(f32[4,128,128]{2,1,0:T(8,128)} %get-tuple-element.35), channel_id=1, source_target_pairs={{0,1},{1,0},{2,3},{3,2},{4,5},{5,4},{6,7},{7,6},{8,9},{9,8},{10,11... | collective-permute-start | bytes 786440 | tf_op jit(solution)/shard_map/ppermute | solution.py:300
  13.8 17.0 %copy-start.3 = (f32[4,128,128]{2,1,0:T(8,128)}, f32[4,128,128]{2,1,0:T(8,128)S(1)}, u32[]{:S(2)}) copy-start(f32[4,128,128]{2,1,0:T(8,128)S(1)} %collective-permute-done.4.refs_0_) | copy-start | bytes 786436
  13.8 40.5 %collective-permute-start.5 = (f32[4,4,128,128]{3,2,1,0:T(8,128)}, f32[4,4,128,128]{3,2,1,0:T(8,128)}, u32[]{:S(2)}, u32[]{:S(2)}) collective-permute-start(f32[4,4,128,128]{3,2,1,0:T(8,128)} %get-tuple-element.34.u_any), channel_id=1, source_target_pairs={{0,1},{1,0},{2,3},{3,2},{4,5},{5,4},{6,7},{7,6},{8,9},{9,8},{10,11... | collective-permute-start | bytes 3145736 | tf_op jit(solution)/shard_map/ppermute | solution.py:300
  16.0 14.8 %collective-permute-start.7 = (f32[4,128,128]{2,1,0:T(8,128)S(1)}, f32[4,128,128]{2,1,0:T(8,128)}, u32[]{:S(2)}, u32[]{:S(2)}) collective-permute-start(f32[4,128,128]{2,1,0:T(8,128)S(1)} %collective-permute-done.4.refs_0_), channel_id=1, source_target_pairs={{0,2},{2,0},{4,6},{6,4},{8,10},{10,8},{12,14},{14,12},{16,18},{18,... | collective-permute-start | bytes 786440 | tf_op jit(solution)/shard_map/ppermute | solution.py:303
  21.6 9.8 %copy-start.4 = (f32[4,128,128]{2,1,0:T(8,128)}, f32[4,128,128]{2,1,0:T(8,128)S(1)}, u32[]{:S(2)}) copy-start(f32[4,128,128]{2,1,0:T(8,128)S(1)} %collective-permute-done.6.refs_1_) | copy-start | bytes 786436
  21.6 9.8 %collective-permute-start.8 = (f32[4,128,128]{2,1,0:T(8,128)S(1)}, f32[4,128,128]{2,1,0:T(8,128)}, u32[]{:S(2)}, u32[]{:S(2)}) collective-permute-start(f32[4,128,128]{2,1,0:T(8,128)S(1)} %collective-permute-done.6.refs_1_), channel_id=1, source_target_pairs={{0,2},{2,0},{4,6},{6,4},{8,10},{10,8},{12,14},{14,12},{16,18},{18,... | collective-permute-start | bytes 786440 | tf_op jit(solution)/shard_map/ppermute | solution.py:303
  23.2 9.8 %collective-permute-start.2 = (f32[4,128,128]{2,1,0:T(8,128)}, f32[4,128,128]{2,1,0:T(8,128)}, u32[]{:S(2)}, u32[]{:S(2)}) collective-permute-start(f32[4,128,128]{2,1,0:T(8,128)} %collective-permute-done.refs_2_), channel_id=1, source_target_pairs={{0,4},{4,8},{8,12},{12,16},{16,20},{20,24},{24,28},{6,2},{10,6},{1... | collective-permute-start | bytes 786440 | tf_op jit(solution)/shard_map/ppermute | solution.py:306
  27.3 10.5 %collective-permute-start.3 = (f32[4,128,128]{2,1,0:T(8,128)}, f32[4,128,128]{2,1,0:T(8,128)}, u32[]{:S(2)}, u32[]{:S(2)}) collective-permute-start(f32[4,128,128]{2,1,0:T(8,128)} %collective-permute-done.1.refs_3_), channel_id=1, source_target_pairs={{0,4},{4,8},{8,12},{12,16},{16,20},{20,24},{24,28},{6,2},{10,6},{1... | collective-permute-start | bytes 786440 | tf_op jit(solution)/shard_map/ppermute | solution.py:306
  30.8 15.8 %collective-permute-start.12 = (f32[6,128,128]{2,1,0:T(8,128)}, f32[6,128,128]{2,1,0:T(8,128)S(1)}, u32[]{:S(2)}, u32[]{:S(2)}) collective-permute-start(f32[6,128,128]{2,1,0:T(8,128)} %get-tuple-element.42), channel_id=1, source_target_pairs={{0,2},{2,0},{4,6},{6,4},{8,10},{10,8},{12,14},{14,12},{16,18},{18,... | collective-permute-start | bytes 1179656 | tf_op jit(solution)/shard_map/ppermute | solution.py:303
  31.4 18.8 %collective-permute-start.13 = (f32[6,128,128]{2,1,0:T(8,128)}, f32[6,128,128]{2,1,0:T(8,128)S(1)}, u32[]{:S(2)}, u32[]{:S(2)}) collective-permute-start(f32[6,128,128]{2,1,0:T(8,128)} %get-tuple-element.44), channel_id=1, source_target_pairs={{0,2},{2,0},{4,6},{6,4},{8,10},{10,8},{12,14},{14,12},{16,18},{18,... | collective-permute-start | bytes 1179656 | tf_op jit(solution)/shard_map/ppermute | solution.py:303
  32.9 13.7 %collective-permute-start.9 = (f32[4,128,128]{2,1,0:T(8,128)}, f32[4,128,128]{2,1,0:T(8,128)}, u32[]{:S(2)}, u32[]{:S(2)}) collective-permute-start(f32[4,128,128]{2,1,0:T(8,128)} %collective-permute-done.7.refs_2_), channel_id=1, source_target_pairs={{0,4},{4,8},{8,12},{12,16},{16,20},{20,24},{24,28},{6,2},{10,6},{1... | collective-permute-start | bytes 786440 | tf_op jit(solution)/shard_map/ppermute | solution.py:306
  37.9 12.3 %collective-permute-start.10 = (f32[4,128,128]{2,1,0:T(8,128)}, f32[4,128,128]{2,1,0:T(8,128)}, u32[]{:S(2)}, u32[]{:S(2)}) collective-permute-start(f32[4,128,128]{2,1,0:T(8,128)} %collective-permute-done.8.refs_3_), channel_id=1, source_target_pairs={{0,4},{4,8},{8,12},{12,16},{16,20},{20,24},{24,28},{6,2},{10,6},{1... | collective-permute-start | bytes 786440 | tf_op jit(solution)/shard_map/ppermute | solution.py:306
  42.1 11.5 %copy-start.6 = (s32[4,4,1]{1,2,0:T(1,128)S(1)}, s32[4,4,1]{1,2,0:T(1,128)}, u32[]{:S(2)}) copy-start(s32[4,4,1]{1,2,0:T(1,128)} %param.10) | copy-start | bytes 196
  46.7 13.9 %copy-start = (f32[6,128,128]{2,1,0:T(8,128)}, f32[6,128,128]{2,1,0:T(8,128)S(1)}, u32[]{:S(2)}) copy-start(f32[6,128,128]{2,1,0:T(8,128)S(1)} %collective-permute-done.12.refs_0_) | copy-start | bytes 1179652
  46.7 15.5 %collective-permute-start.15 = (f32[6,128,128]{2,1,0:T(8,128)S(1)}, f32[6,128,128]{2,1,0:T(8,128)}, u32[]{:S(2)}, u32[]{:S(2)}) collective-permute-start(f32[6,128,128]{2,1,0:T(8,128)S(1)} %collective-permute-done.12.refs_0_), channel_id=1, source_target_pairs={{0,4},{4,8},{8,12},{12,16},{16,20},{20,24},{24,28},{6,2},{10,6},{1... | collective-permute-start | bytes 1179656 | tf_op jit(solution)/shard_map/ppermute | solution.py:306
  50.2 10.4 %copy-start.1 = (f32[6,128,128]{2,1,0:T(8,128)}, f32[6,128,128]{2,1,0:T(8,128)S(1)}, u32[]{:S(2)}) copy-start(f32[6,128,128]{2,1,0:T(8,128)S(1)} %collective-permute-done.13.refs_1_) | copy-start | bytes 1179652
  50.2 13.5 %collective-permute-start.16 = (f32[6,128,128]{2,1,0:T(8,128)S(1)}, f32[6,128,128]{2,1,0:T(8,128)}, u32[]{:S(2)}, u32[]{:S(2)}) collective-permute-start(f32[6,128,128]{2,1,0:T(8,128)S(1)} %collective-permute-done.13.refs_1_), channel_id=1, source_target_pairs={{0,4},{4,8},{8,12},{12,16},{16,20},{20,24},{24,28},{6,2},{10,6},{1... | collective-permute-start | bytes 1179656 | tf_op jit(solution)/shard_map/ppermute | solution.py:306
  53.6 8.5 %collective-permute-start.14 = (f32[4,128,128]{2,1,0:T(8,128)}, f32[4,128,128]{2,1,0:T(8,128)}, u32[]{:S(2)}, u32[]{:S(2)}) collective-permute-start(f32[4,128,128]{2,1,0:T(8,128)} %get-tuple-element.46), channel_id=1, source_target_pairs={{0,2},{2,0},{4,6},{6,4},{8,10},{10,8},{12,14},{14,12},{16,18},{18,... | collective-permute-start | bytes 786440 | tf_op jit(solution)/shard_map/ppermute | solution.py:303
  60.6 14.8 %collective-permute-start.11 = (f32[2,4,128,128]{3,2,1,0:T(8,128)}, f32[2,4,128,128]{3,2,1,0:T(8,128)}, u32[]{:S(2)}, u32[]{:S(2)}) collective-permute-start(f32[2,4,128,128]{3,2,1,0:T(8,128)} %get-tuple-element.40), channel_id=1, source_target_pairs={{0,1},{1,0},{2,3},{3,2},{4,5},{5,4},{6,7},{7,6},{8,9},{9,8},{10,11... | collective-permute-start | bytes 1572872 | tf_op jit(solution)/shard_map/ppermute | solution.py:300
  68.7 17.8 %collective-permute-start.17 = (f32[2,4,128,128]{3,2,1,0:T(8,128)}, f32[2,4,128,128]{3,2,1,0:T(8,128)S(1)}, u32[]{:S(2)}, u32[]{:S(2)}) collective-permute-start(f32[2,4,128,128]{3,2,1,0:T(8,128)} %shard_map.69), channel_id=1, source_target_pairs={{0,1},{1,0},{2,3},{3,2},{4,5},{5,4},{6,7},{7,6},{8,9},{9,8},{10,11... | collective-permute-start | bytes 1572872 | tf_op jit(solution)/shard_map/ppermute | solution.py:300
  86.5 0.8 copy-start.2

commit v3 on v2

v3 whole, which is shorter than its diff:
```python
import functools

import jax
import jax.numpy as jnp
from jax import lax
from jax.experimental import pallas as pl
from jax.experimental.pallas import tpu as pltpu
from jax.sharding import PartitionSpec as P

SLABS = ("row", "col")
F32 = jnp.float32
BF16 = jnp.bfloat16
VMEM = pl.BlockSpec(memory_space=pltpu.VMEM)
SMEM = pl.BlockSpec(memory_space=pltpu.SMEM)
ANY = pl.BlockSpec(memory_space=pl.ANY)
HBM = object()

PACK = (
    [(0, 0), (0, 1), (0, 2), (0, 3), (1, 0), (1, 1), (1, 2), (1, 3), (2, 0), (2, 1), (2, 2), (2, 3)]
    + [(3, 0), (3, 1), (3, 2), (3, 3)],
    [(0, 2), (0, 3), (1, 1), (1, 2), (1, 3), (2, 1), (2, 2), (2, 3), (3, 0), (3, 1), (3, 2), (3, 3)]
    + [(0, 0), (0, 1), (1, 0), (2, 0)],
)
PARTS = ((0, 7), (7, 9))


def shape(*dims, dtype=F32):
    return jax.ShapeDtypeStruct(dims, dtype)


def vmem(*dims, dtype=F32):
    return pltpu.VMEM(dims, dtype)


def call(body, outs, ins, scratch=(), flops=0, alias=None, limit=24):
    def run(*args):
        placed = [pltpu.with_memory_space_constraint(x, pltpu.HBM) if spec is HBM else x for spec, x in zip(ins, args)]
        return pl.pallas_call(
            body,
            out_shape=outs,
            in_specs=[ANY if spec is HBM else spec for spec in ins],
            out_specs=[ANY if isinstance(x, jax.ShapeDtypeStruct) else VMEM for x in outs],
            scratch_shapes=list(scratch),
            input_output_aliases=alias or {},
            cost_estimate=pl.CostEstimate(flops=flops, bytes_accessed=0, transcendentals=0),
            compiler_params=pltpu.CompilerParams(vmem_limit_bytes=limit << 20),
        )(*placed)

    return run


def halves(x):
    high = x.astype(BF16)
    return high, (x - high.astype(F32)).astype(BF16)


def dot3(a, b, rhs_contract):
    one = functools.partial(
        lax.dot_general,
        dimension_numbers=(((1,), (rhs_contract,)), ((), ())),
        preferred_element_type=F32,
    )
    return one(a[0], b[0]) + (one(a[0], b[1]) + one(a[1], b[0]))


def joined(blocks, axis):
    return [jnp.concatenate(x, axis=axis) for x in zip(*[halves(b) for b in blocks])]


def aligned(block, size):
    return pl.multiple_of(block * size, size)


def slot_base(i, layer):
    return i // 2 if i % 2 == 0 else (i + 1) // 2 - layer


def start(src, dst, sem):
    copy = pltpu.make_async_copy(src, dst, sem)
    copy.start()
    return copy


def keep_p(p_mask_any, p_any, *refs):
    outs, (p_mask, p, kept, sems) = refs[0:2], refs[2:]
    copies = [start(p_any.at[a], p.at[a], sems.at[a]) for a in range(2)]
    start(p_mask_any, p_mask, sems.at[2]).wait()
    stores = []
    for a in range(2):
        copies[a].wait()
        for r in (1, 0):
            for e in range(4):
                o = 2 * e + r
                kept[r, a, e] = p[a, 0, o] * p_mask[a, 0, o].astype(F32)
            stores.append(start(kept.at[r, a], outs[r].at[a], sems.at[3 + 2 * r + a]))
    for c in stores:
        c.wait()


def keep_u(where, u_mask_any, u_any, *refs):
    outs, (u_mask, u, rows, packed, sems) = refs[0:3], refs[3:]
    copies = [start(u_any.at[i], u.at[i], sems.at[i]) for i in range(4)]
    start(u_mask_any, u_mask, sems.at[4]).wait()
    even = where[0] % 2 == 0
    stores = []
    for i in range(4):
        copies[i].wait()
        for m in range(4):
            rows[i, m] = u[i, m, 0] * u_mask[i, m].astype(F32)
        stores.append(start(rows.at[i], outs[0].at[i], sems.at[5 + i]))
    for par, case in ((0, even), (1, jnp.logical_not(even))):

        @pl.when(case)
        def _(par=par):
            for n, block in enumerate(PACK[par]):
                packed[n] = rows[block]

    for n, (first, count) in enumerate(PARTS):
        stores.append(start(packed.at[pl.ds(first, count)], outs[1 + n], sems.at[9 + n]))
    for c in stores:
        c.wait()


def fill_band(size, stage, hi_ref, lo_ref, shift, rows):
    for a in rows:
        for c in range(6):
            e = c - a - shift
            at = (pl.ds(a * size, size), pl.ds(c * size, size))
            if 0 <= e < 4:
                hi_ref[at], lo_ref[at] = halves(stage[a, e])
            else:
                hi_ref[at] = jnp.zeros((size, size), BF16)
                lo_ref[at] = jnp.zeros((size, size), BF16)


def product_own(size, where, u_any, mine, other_y, other_z, t_own, ud_hi, ud_lo, stage, u, hi, lo, sems):
    even, layer = where[0] % 2 == 0, where[1]
    copies = [
        start(u_any, u, sems.at[0]),
        start(mine, stage.at[pl.ds(2, 2)], sems.at[1]),
        start(other_y, stage.at[pl.ds(jnp.where(even, 4, 0), 2)], sems.at[2]),
        start(other_z, stage.at[pl.ds(jnp.where(even, 0, 4), 2)], sems.at[3]),
    ]
    ud_hi[...] = jnp.zeros_like(ud_hi)
    ud_lo[...] = jnp.zeros_like(ud_lo)
    copies[0].wait()
    for i in range(4):
        cols = pl.ds(aligned(slot_base(i, layer), size), 4 * size)
        rows = pl.ds(i * size, size)
        ud_hi[rows, cols], ud_lo[rows, cols] = joined([u[i, m] for m in range(4)], 1)
    for c in copies[1:]:
        c.wait()
    fill_band(size, stage, hi, lo, -2, range(6))
    for i in range(4):
        cols = pl.ds(aligned(slot_base(i, layer), size), 4 * size)
        rows = pl.ds(i * size, size)
        t_own[i] = dot3((ud_hi[rows, cols], ud_lo[rows, cols]), (hi[cols, cols], lo[cols, cols]), 0)


def product_t(total_rows, size, where, t_mask_any, t_own, ud_hi, ud_lo, u_cross, *refs):
    sides, (t_hi, t_lo, ss) = refs[0:3], refs[3:6]
    t_mask, stage, u_oth, hi, lo, sems = refs[6:]
    slab, layer = where[0], where[1]
    even = slab % 2 == 0
    spots = (2, jnp.where(even, 4, 0), jnp.where(even, 0, 4))
    x_copy = start(u_cross, u_oth, sems.at[6])
    copies = [start(sides[n], stage.at[pl.ds(spots[n], 2)], sems.at[n]) for n in range(3)]
    mask_copy = start(t_mask_any, t_mask, sems.at[7])
    x_copy.wait()
    others = [joined([u_oth[i, m] for m in range(4)], 1) for i in range(4)]
    for c in copies:
        c.wait()
    mask_copy.wait()
    fill_band(size, stage, hi, lo, -1, range(6))
    for i in range(4):
        base = slot_base(i, layer)
        rows = pl.ds(aligned(slot_base(i, 1 - layer), size), 4 * size)
        cols = pl.ds(aligned(i // 2 + layer if i % 2 == 0 else (i + 1) // 2, size), 4 * size)
        total = t_own[i] + dot3(others[i], (hi[rows, cols], lo[rows, cols]), 0)
        kept = []
        for m in range(4):
            col = slab * 4 + 2 * (base + m) - 4 + layer
            keep = jnp.where((col >= 0) & (col < total_rows), t_mask[i, m], 0).astype(F32)
            kept.append(total[:, m * size : (m + 1) * size] * keep)
        t_hi[i], t_lo[i] = joined(kept, 1)
    for q in range(2):
        i = 2 * q + 1 - layer
        cols = pl.ds(aligned(q + 1 - layer, size), 4 * size)
        sums = dot3((t_hi[i], t_lo[i]), (ud_hi[:, cols], ud_lo[:, cols]), 1)
        for r in range(4):
            ss[q, r] = sums[:, r * size : (r + 1) * size]


def gather_halo(u_y, u_z, stage, sems):
    spots = [stage.at[pl.ds(at, n)] for at, n in (*PARTS, (16, 7), (23, 5))]
    return [start(src, spot, sems.at[n]) for n, (src, spot) in enumerate(zip([*u_y, *u_z], spots))]


def fill_halo(size, where, stage, uh_hi, uh_lo, rows=(0, 1, 2, 3)):
    even, layer = where[0] % 2 == 0, where[1]
    uh_hi[...] = jnp.zeros_like(uh_hi)
    uh_lo[...] = jnp.zeros_like(uh_lo)
    for below_at, above_at, pack, case in ((16, 0, PACK[1], even), (0, 16, PACK[0], jnp.logical_not(even))):

        @pl.when(case)
        def _(below_at=below_at, above_at=above_at, pack=pack):
            for first, above in ((below_at, 0), (above_at, 1)):
                for n, (r, m) in enumerate(pack[: 16 if first == 0 else 12]):
                    if r not in rows or (above and r == 3):
                        continue
                    at = pl.ds((above * len(rows) + rows.index(r)) * size, size)
                    cols = pl.ds(aligned(slot_base(r, layer) + 4 * above + m, size), size)
                    uh_hi[at, cols], uh_lo[at, cols] = halves(stage[first + n])


def halo_sums(size, i, base, t_rows, uh_hi, uh_lo, ts=(0, 1, 2, 3)):
    cols = pl.ds(aligned(base + 2, size), 4 * size)
    rows = [pl.ds(aligned(jnp.where(t < i, len(ts) + n, n), size), size) for n, t in enumerate(ts)]
    hi = jnp.concatenate([uh_hi[r, cols] for r in rows], axis=0)
    lo = jnp.concatenate([uh_lo[r, cols] for r in rows], axis=0)
    return dot3(t_rows, (hi, lo), 1)


def send_halo(size, ts, where, *refs):
    u_y, u_z, t_any = refs[0:2], refs[2:-9], refs[-9:-7]
    out, stage, t_hi, t_lo, uh_hi, uh_lo, sems = refs[-7:]
    layer = where[1]
    copies = gather_halo(u_y, u_z, stage, sems)
    for q in range(2):
        for n in range(2):
            copies.append(start(t_any[n].at[2 * q + 1 - layer], (t_hi, t_lo)[n].at[q], sems.at[5 + 2 * q + n]))
    for c in copies:
        c.wait()
    fill_halo(size, where, stage, uh_hi, uh_lo, ts)
    for q in range(2):
        sums = halo_sums(size, 2 * q + 1 - layer, q + 1 - layer, (t_hi[q], t_lo[q]), uh_hi, uh_lo, ts)
        for n in range(len(ts)):
            out[q, n] = sums[:, n * size : (n + 1) * size]


def out_keep(total_rows, where, o_mask, q, o):
    col = where[0] * 4 + 2 * q + where[1] - 4 + o
    return jnp.where((col >= 0) & (col < total_rows), o_mask[q, 0, o], 0).astype(F32)


def keep_rows(total_rows, size, where, o_mask, u_any, ss_any, *refs):
    u_y, u_z, t_any = refs[0:2], refs[2:4], refs[4:6]
    out_any, part, out, stage, u, ss, t_hi, t_lo, uh_hi, uh_lo, ud_hi, ud_lo, sems = refs[6:]
    layer = where[1]
    copies = gather_halo(u_y, u_z, stage, sems)
    copies += [start(t_any[n], (t_hi, t_lo)[n], sems.at[7 + n]) for n in range(2)]
    copies += [start(u_any, u, sems.at[9]), start(ss_any, ss, sems.at[10])]
    for c in copies:
        c.wait()
    fill_halo(size, where, stage, uh_hi, uh_lo)
    ud_hi[...] = jnp.zeros_like(ud_hi)
    ud_lo[...] = jnp.zeros_like(ud_lo)
    for i in range(4):
        cols = pl.ds(aligned(slot_base(i, layer), size), 4 * size)
        rows = pl.ds(i * size, size)
        ud_hi[rows, cols], ud_lo[rows, cols] = joined([u[i, m] for m in range(4)], 1)
    stores = []
    for q in range(2):
        i = 2 * q + layer
        sums = halo_sums(size, i, q, (t_hi[i], t_lo[i]), uh_hi, uh_lo)
        for t in range(4):
            o = (8 - i + t) % 8
            part[q, t] = sums[:, t * size : (t + 1) * size] * out_keep(total_rows, where, o_mask, q, o)
        cols = pl.ds(q * size, 4 * size)
        sums = dot3((t_hi[i], t_lo[i]), (ud_hi[:, cols], ud_lo[:, cols]), 1)
        for r in range(4):
            o = (4 - i + r) % 8
            keep = out_keep(total_rows, where, o_mask, q, o)
            out[q, r] = (sums[:, r * size : (r + 1) * size] + ss[q, r]) * keep
            stores.append(start(out.at[q, r], out_any.at[q, 0, o], sems.at[11 + 4 * q + r]))
    for c in stores:
        c.wait()


def combine(total_rows, where, o_mask, part, halo0, halo1, kept_any, out_any, done, sems):
    stores = []
    for q in range(2):
        for t in range(4):
            o = (8 - 2 * q - where[1] + t) % 8
            done[q, t] = part[q, t] + (halo0, halo1)[t // 2][q, t % 2] * out_keep(total_rows, where, o_mask, q, o)
            stores.append(start(done.at[q, t], out_any.at[q, 0, o], sems.at[4 * q + t]))
    for s in stores:
        s.wait()


def after(x, *others):
    return lax.optimization_barrier((x, *others))[0]


def on_device(u_values, u_mask, p_values, p_mask, t_mask, out_mask):
    size = u_values.shape[-1]
    slabs = lax.axis_size(SLABS)
    total_rows = slabs * u_values.shape[0]
    where = jnp.stack([lax.axis_index(SLABS), lax.axis_index("layer")]).astype(jnp.int32)
    swap = [(0, 1), (1, 0)]
    pair = [(s, s ^ 1) for s in range(slabs)]
    onward = [(s, s + 2) for s in range(0, slabs - 2, 2)] + [(s, s - 2) for s in range(3, slabs, 2)]

    def over_layer(x):
        return lax.ppermute(x, "layer", swap)

    def over_pair(x):
        return lax.ppermute(x, SLABS, pair)

    def onto(x):
        return lax.ppermute(x, SLABS, onward)

    def sems(n):
        return pltpu.SemaphoreType.DMA((n,))

    eight = shape(2, 4, size, size)
    wide = 6 * size
    unit = 3 * 2 * (4 * size) ** 2 * size
    pe, po = call(
        keep_p,
        [eight, eight],
        [HBM, HBM],
        [pltpu.SMEM(p_mask.shape, jnp.int32), vmem(*p_values.shape), vmem(2, 2, 4, size, size), sems(7)],
    )(p_mask, p_values)
    pc = over_layer(po)
    pe_y = over_pair(pe)
    u_mask, t_mask = u_mask[:, :, 0], t_mask[:, :, 0]
    u_own, *packed = call(
        keep_u,
        [shape(4, 4, size, size)] + [shape(n, size, size) for _, n in PARTS],
        [SMEM, HBM, HBM],
        [pltpu.SMEM(u_mask.shape, jnp.int32), vmem(*u_values.shape), vmem(4, 4, size, size)]
        + [vmem(16, size, size), sems(11)],
    )(where, u_mask, u_values)
    u_oth = over_layer(after(u_own, pc))
    pe_z = onto(after(pe_y, u_own))
    pc_y = over_pair(pc)
    pc_z = onto(pc_y)
    t_like = (4, size, 4 * size)
    band = [vmem(wide, wide, dtype=BF16)] * 2
    own_rows = [vmem(4 * size, wide, dtype=BF16)] * 2
    t_own, ud_hi, ud_lo = call(
        functools.partial(product_own, size),
        [vmem(*t_like), *own_rows],
        [SMEM] + [HBM] * 4,
        [vmem(6, 4, size, size), vmem(4, 4, size, size), *band, sems(4)],
        flops=4 * unit,
    )(where, u_own, pe, pe_y, pe_z)
    u_y = [over_pair(after(x, pc)) for x in packed]
    u_z = [onto(after(u_y[0], t_own))]
    t_hi, t_lo, ss = call(
        functools.partial(product_t, total_rows, size),
        [vmem(*t_like, dtype=BF16)] * 2 + [vmem(2, 4, size, size)],
        [SMEM, HBM, VMEM, VMEM, VMEM] + [HBM] * 4,
        [pltpu.SMEM(t_mask.shape, jnp.int32), vmem(6, 4, size, size), vmem(4, 4, size, size), *band, sems(8)],
        flops=6 * unit,
    )(where, after(t_mask, u_y[0]), t_own, ud_hi, ud_lo, u_oth, pc, pc_y, pc_z)
    ss_got = over_layer(ss)
    u_z.append(onto(after(u_y[1][:5], t_hi)))
    halos = []
    for ts in ((0, 1), (2, 3)):
        nz = 1 if ts[0] == 0 else 2
        (halo,) = call(
            functools.partial(send_halo, size, ts),
            [vmem(2, 2, size, size)],
            [SMEM] + [HBM] * (2 + nz) + [ANY] * 2,
            [vmem(28, size, size)]
            + [vmem(2, size, 4 * size, dtype=BF16)] * 2
            + [vmem(4 * size, 9 * size, dtype=BF16)] * 2
            + [sems(9)],
            flops=unit,
        )(where, *u_y, *u_z[:nz], t_hi, t_lo)
        t_lo = after(t_lo, halo)
        halos.append(over_layer(after(halo, *halos)))
    halo_scratch = [vmem(8 * size, 9 * size, dtype=BF16)] * 2
    t_scratch = [vmem(*t_like, dtype=BF16)] * 2
    kept, part = call(
        functools.partial(keep_rows, total_rows, size),
        [shape(*p_values.shape), vmem(2, 4, size, size)],
        [SMEM] * 2 + [HBM] * 6 + [ANY] * 2,
        [vmem(2, 4, size, size), vmem(28, size, size), vmem(4, 4, size, size), vmem(2, 4, size, size)]
        + [*t_scratch, *halo_scratch, *own_rows, sems(19)],
        flops=40 * unit,
    )(where, out_mask, u_own, ss_got, *u_y, *u_z, t_hi, t_lo)
    (out,) = call(
        functools.partial(combine, total_rows),
        [shape(*p_values.shape)],
        [SMEM, SMEM, VMEM, VMEM, VMEM, ANY],
        [vmem(2, 4, size, size), sems(8)],
        alias={5: 0},
        limit=16,
    )(where, out_mask, part, *halos, kept)
    return out


def solution(mesh):
    placed = (
        P(SLABS, None, "layer", None, None),
        P(SLABS, None, "layer"),
        P(SLABS, "layer", None, None, None),
        P(SLABS, "layer", None),
        P(SLABS, None, "layer"),
        P(SLABS, "layer", None),
    )
    return jax.shard_map(
        on_device,
        mesh=mesh,
        in_specs=placed,
        out_specs=P(SLABS, "layer", None, None, None),
        check_vma=False,
    )
```

time: 90.6 us -> 80.4 us (0.89)
  starting transfers between devices: 36.7 us -> 29.8 us
  Pallas kernels: 31.7 us -> 25.4 us
  local copies, waits for them, and re-layouts: 2.23 us -> 4.25 us
  waiting for transfers between devices: 18.7 us -> 20.2 us
    ppermute x6 -> x4, starting transfers between devices: 23.8 us -> 16.7 us  [onto(): return lax.ppermute(x, SLABS, onward)]
    pallas_call x7 -> x8, Pallas kernels: 31.7 us -> 25.4 us  [run(): pl.pallas_call(body, out_shape=outs, in_specs=[ANY if spec is HBM else sp...]
    ppermute x5, starting transfers between devices: 6.34 us -> 9.65 us  [over_layer(): return lax.ppermute(x, 'layer', swap)]
    ppermute x7 -> x4, starting transfers between devices: 6.59 us -> 3.43 us  [over_pair(): return lax.ppermute(x, SLABS, pair)]
    ppermute x7 -> x4, waiting for transfers between devices: 5.75 us -> 8.01 us  [over_pair(): return lax.ppermute(x, SLABS, pair)]
    unnamed x16 -> x28, local copies, waits for them, and re-layouts: 2.23 us -> 4.23 us
    ppermute x6 -> x4, waiting for transfers between devices: 1.59 us -> 0.01 us  [onto(): return lax.ppermute(x, SLABS, onward)]
  transfers between devices with their start and end apart: 18 -> 13, of which waited for: 8 -> 3; matrix products, arithmetic and copies ran while one was open for 2% -> 0% of each run, Pallas kernels for 29% -> 28%
where the time goes in v3:
time: 80.4 us; the launch traced here: 80 us
  starting transfers between devices  29.8 us (37%)
  Pallas kernels  25.4 us (32%)
  waiting for transfers between devices  20.2 us (25%)
  local copies, waits for them, and re-layouts  4.25 us (5%)
    pallas_call x8, Pallas kernels, run(): pl.pallas_call(body, out_shape=outs, in_specs=[ANY if spec is HBM else sp...  25.4 us
    ppermute x4, starting transfers between devices, onto(): return lax.ppermute(x, SLABS, onward)  16.7 us
    ppermute x5, waiting for transfers between devices, over_layer(): return lax.ppermute(x, 'layer', swap)  12.2 us
    ppermute x5, starting transfers between devices, over_layer(): return lax.ppermute(x, 'layer', swap)  9.65 us
    ppermute x4, waiting for transfers between devices, over_pair(): return lax.ppermute(x, SLABS, pair)  8.01 us
    unnamed x28, local copies, waits for them, and re-layouts  4.23 us
    ppermute x4, starting transfers between devices, over_pair(): return lax.ppermute(x, SLABS, pair)  3.43 us
  transfers between devices with their start and end apart: 13, of which 3 were waited for; matrix products, arithmetic and copies ran while one was open for 0% of the time, Pallas kernels for 28%

profile of v3, /device:TPU:0, one launch (start us, length us, event | category | flops | bytes accessed | tf_op | source)
XLA Modules:
  0.0 80.0 jit_solution(16437887974102080284)
XLA Ops:
  0.0 1.3 %shard_map.65 = (f32[2,4,128,128]{3,2,1,0:T(8,128)S(1)}, f32[2,4,128,128]{3,2,1,0:T(8,128)S(1)}) custom-call(s32[2,1,8]{2,1,0:T(1,128)} %p_mask_any.1, f32[2,1,8,128,128]{4,3,2,1,0:T(8,128)} %p_any.1), custom_call_target="tpu_custom_call" | custom-call | tf_op jit(solution)/shard_map/pallas_call | solution.py:38
  1.4 0.0 copy-start.2
  1.4 3.0 %collective-permute-start = (f32[2,4,128,128]{3,2,1,0:T(8,128)S(1)}, f32[2,4,128,128]{3,2,1,0:T(8,128)S(1)}, u32[]{:S(2)}, u32[]{:S(2)}) collective-permute-start(f32[2,4,128,128]{3,2,1,0:T(8,128)S(1)} %get-tuple-element.30), channel_id=1, source_target_pairs={{0,1},{1,0},{2,3},{3,2},{4,5},{5,4},{6,7},{7,6},{8,9},{9,8},{10,11... | collective-permute-start | bytes 1572872 | tf_op jit(solution)/shard_map/ppermute | solution.py:305
  4.4 1.5 %collective-permute-start.2 = (f32[2,4,128,128]{3,2,1,0:T(8,128)S(1)}, f32[2,4,128,128]{3,2,1,0:T(8,128)S(1)}, u32[]{:S(2)}, u32[]{:S(2)}) collective-permute-start(f32[2,4,128,128]{3,2,1,0:T(8,128)S(1)} %get-tuple-element.33.mine), channel_id=1, source_target_pairs={{0,2},{2,0},{4,6},{6,4},{8,10},{10,8},{12,14},{14,12},{16,18},{18,... | collective-permute-start | bytes 1572872 | tf_op jit(solution)/shard_map/ppermute | solution.py:308
  5.9 0.1 pad_add_fusion.where
  6.0 2.3 %shard_map.64 = (f32[4,4,128,128]{3,2,1,0:T(8,128)S(1)}, f32[7,128,128]{2,1,0:T(8,128)S(1)}, f32[9,128,128]{2,1,0:T(8,128)S(1)}) custom-call(s32[2]{0:T(128)S(1)} %pad_add_fusion.where, s32[4,4]{1,0:T(4,128)} %bitcast.5, f32[4,4,1,128,128]{4,3,2,1,0:T(8,128)} %u_any.1), custom_call_target="tpu_custom_call" | custom-call | tf_op jit(solution)/shard_map/pallas_call | solution.py:38
  8.3 0.0 copy-done.2
  8.3 0.0 copy-start.1
  8.3 8.0 %collective-permute-done.refs_0_ = f32[2,4,128,128]{3,2,1,0:T(8,128)S(1)} collective-permute-done((f32[2,4,128,128]{3,2,1,0:T(8,128)S(1)}, f32[2,4,128,128]{3,2,1,0:T(8,128)S(1)}, u32[]{:S(2)}, u32[]{:S(2)}) %collective-permute-start) | collective-permute-done | bytes 524320 | tf_op jit(solution)/shard_map/ppermute | solution.py:305
  16.3 1.8 %collective-permute-start.5 = (f32[2,4,128,128]{3,2,1,0:T(8,128)S(1)}, f32[2,4,128,128]{3,2,1,0:T(8,128)S(1)}, u32[]{:S(2)}, u32[]{:S(2)}) collective-permute-start(f32[2,4,128,128]{3,2,1,0:T(8,128)S(1)} %collective-permute-done.refs_0_), channel_id=1, source_target_pairs={{0,2},{2,0},{4,6},{6,4},{8,10},{10,8},{12,14},{14,12},{16,18},{18,... | collective-permute-start | bytes 1572872 | tf_op jit(solution)/shard_map/ppermute | solution.py:308
  18.1 1.5 %collective-permute-start.4 = (f32[4,4,128,128]{3,2,1,0:T(8,128)S(1)}, f32[4,4,128,128]{3,2,1,0:T(8,128)S(1)}, u32[]{:S(2)}, u32[]{:S(2)}) collective-permute-start(f32[4,4,128,128]{3,2,1,0:T(8,128)S(1)} %get-tuple-element.38.u_any), channel_id=1, source_target_pairs={{0,1},{1,0},{2,3},{3,2},{4,5},{5,4},{6,7},{7,6},{8,9},{9,8},{10,11... | collective-permute-start | bytes 3145736 | tf_op jit(solution)/shard_map/ppermute | solution.py:305
  19.6 0.0 collective-permute-done.2.other_y
  19.6 3.5 %collective-permute-start.3 = (f32[2,4,128,128]{3,2,1,0:T(8,128)S(1)}, f32[2,4,128,128]{3,2,1,0:T(8,128)S(1)}, u32[]{:S(2)}, u32[]{:S(2)}) collective-permute-start(f32[2,4,128,128]{3,2,1,0:T(8,128)S(1)} %collective-permute-done.2.other_y), channel_id=1, source_target_pairs={{0,4},{4,8},{8,12},{12,16},{16,20},{20,24},{24,28},{6,2},{10,6},{1... | collective-permute-start | bytes 1572872 | tf_op jit(solution)/shard_map/ppermute | solution.py:311
  23.1 0.1 collective-permute-start.1
  23.2 8.0 %collective-permute-done.5.refs_1_ = f32[2,4,128,128]{3,2,1,0:T(8,128)S(1)} collective-permute-done((f32[2,4,128,128]{3,2,1,0:T(8,128)S(1)}, f32[2,4,128,128]{3,2,1,0:T(8,128)S(1)}, u32[]{:S(2)}, u32[]{:S(2)}) %collective-permute-start.5) | collective-permute-done | bytes 524320 | tf_op jit(solution)/shard_map/ppermute | solution.py:308
  31.2 3.8 %collective-permute-start.6 = (f32[2,4,128,128]{3,2,1,0:T(8,128)S(1)}, f32[2,4,128,128]{3,2,1,0:T(8,128)S(1)}, u32[]{:S(2)}, u32[]{:S(2)}) collective-permute-start(f32[2,4,128,128]{3,2,1,0:T(8,128)S(1)} %collective-permute-done.5.refs_1_), channel_id=1, source_target_pairs={{0,4},{4,8},{8,12},{12,16},{16,20},{20,24},{24,28},{6,2},{10,6},{1... | collective-permute-start | bytes 1572872 | tf_op jit(solution)/shard_map/ppermute | solution.py:311
  34.9 0.1 collective-permute-start.8
  35.0 0.0 collective-permute-done.3.other_z
  35.0 0.8 copy-done.13
  35.8 3.5 %shard_map.66 = (f32[4,128,512]{2,1,0:T(8,128)S(1)}, bf16[512,768]{1,0:T(8,128)(2,1)S(1)}, bf16[512,768]{1,0:T(8,128)(2,1)S(1)}) custom-call(s32[2]{0:T(128)S(1)} %pad_add_fusion.where, f32[4,4,128,128]{3,2,1,0:T(8,128)} %copy-done.1, f32[2,4,128,128]{3,2,1,0:T(8,128)} %copy-done.2, f32[2,4,128,128]{3,2,1,0:T(8,128)} %copy-done.11, f32[2,4,128,128]{3,2,1,0:T(8,128)} %copy-done.13), custom_call_target="tpu_custom_call" | custom-call | flops 805306368 | tf_op jit(solution)/shard_map/pallas_call | solution.py:38
  39.3 0.0 collective-permute-done.1.refs_0_
  39.3 5.4 %collective-permute-start.9 = (f32[7,128,128]{2,1,0:T(8,128)S(1)}, f32[7,128,128]{2,1,0:T(8,128)S(1)}, u32[]{:S(2)}, u32[]{:S(2)}) collective-permute-start(f32[7,128,128]{2,1,0:T(8,128)S(1)} %collective-permute-done.1.refs_0_), channel_id=1, source_target_pairs={{0,4},{4,8},{8,12},{12,16},{16,20},{20,24},{24,28},{6,2},{10,6},{1... | collective-permute-start | bytes 1376264 | tf_op jit(solution)/shard_map/ppermute | solution.py:311
  44.7 0.0 collective-permute-done.4.u_cross
  44.8 0.0 copy-start.6
  44.8 0.0 collective-permute-done.6.refs_2_
  44.8 0.0 copy-start.9
  44.8 0.9 %copy-done.6 = f32[4,4,128,128]{3,2,1,0:T(8,128)} copy-done((f32[4,4,128,128]{3,2,1,0:T(8,128)}, f32[4,4,128,128]{3,2,1,0:T(8,128)S(1)}, u32[]{:S(2)}) %copy-start.6) | copy-done | bytes 1048600
  45.7 0.2 copy-done.9
  45.9 4.8 %shard_map.67 = (bf16[4,128,512]{2,1,0:T(8,128)(2,1)S(1)}, bf16[4,128,512]{2,1,0:T(8,128)(2,1)S(1)}, f32[2,4,128,128]{3,2,1,0:T(8,128)S(1)}) custom-call(s32[2]{0:T(128)S(1)} %pad_add_fusion.where, s32[4,4]{1,0:T(4,128)} %bitcast.4, f32[4,128,512]{2,1,0:T(8,128)S(1)} %get-tuple-element.35.t_own, bf16[512,768]{1,0:T(8,128)(2,1)S(1)} %get-tuple-element.36.ud_hi, ...), custom_call_target="tpu_custom_call" | custom-call | flops 1207959552 | tf_op jit(solution)/shard_map/pallas_call | solution.py:38
  50.7 1.6 %collective-permute-start.7 = (f32[2,4,128,128]{3,2,1,0:T(8,128)S(1)}, f32[2,4,128,128]{3,2,1,0:T(8,128)S(1)}, u32[]{:S(2)}, u32[]{:S(2)}) collective-permute-start(f32[2,4,128,128]{3,2,1,0:T(8,128)S(1)} %get-tuple-element.39), channel_id=1, source_target_pairs={{0,1},{1,0},{2,3},{3,2},{4,5},{5,4},{6,7},{7,6},{8,9},{9,8},{10,11... | collective-permute-start | bytes 1572872 | tf_op jit(solution)/shard_map/ppermute | solution.py:305
  52.3 0.0 collective-permute-done.8.refs_1_
  52.3 4.1 %collective-permute-start.10 = (f32[5,128,128]{2,1,0:T(8,128)S(1)}, f32[5,128,128]{2,1,0:T(8,128)S(1)}, u32[]{:S(2)}, u32[]{:S(2)}) collective-permute-start(f32[5,128,128]{2,1,0:T(8,128)S(1)} %slice.4), channel_id=1, source_target_pairs={{0,4},{4,8},{8,12},{12,16},{16,20},{20,24},{24,28},{6,2},{10,6},{1... | collective-permute-start | bytes 983048 | tf_op jit(solution)/shard_map/ppermute | solution.py:311
  56.4 0.0 collective-permute-done.9.refs_2_
  56.4 0.8 copy-done.5
  57.2 2.9 %shard_map.68 = f32[2,2,128,128]{3,2,1,0:T(8,128)S(1)} custom-call(s32[2]{0:T(128)S(1)} %pad_add_fusion.where, f32[7,128,128]{2,1,0:T(8,128)} %copy-done.4, f32[9,128,128]{2,1,0:T(8,128)} %copy-done.3, f32[7,128,128]{2,1,0:T(8,128)} %copy-done.5, bf16[4,128,512]{2,1,0:T(8,128)(2,1)S(1)} %get-tuple-element.43.refs_3_.refs_4_, ...), custom_call_target="tpu_custom_call" | custom-call | flops 201326592 | tf_op jit(solution)/shard_map/pallas_call | solution.py:38
  60.1 0.0 copy-start
  60.1 2.1 %collective-permute-start.11 = (f32[2,2,128,128]{3,2,1,0:T(8,128)S(1)}, f32[2,2,128,128]{3,2,1,0:T(8,128)S(1)}, u32[]{:S(2)}, u32[]{:S(2)}) collective-permute-start(f32[2,2,128,128]{3,2,1,0:T(8,128)S(1)} %shard_map.68), channel_id=1, source_target_pairs={{0,1},{1,0},{2,3},{3,2},{4,5},{5,4},{6,7},{7,6},{8,9},{9,8},{10,11... | collective-permute-start | bytes 786440 | tf_op jit(solution)/shard_map/ppermute | solution.py:305
  62.2 0.0 collective-permute-done.10.refs_3_
  62.2 0.7 copy-done.10
  62.9 3.0 %shard_map.69 = f32[2,2,128,128]{3,2,1,0:T(8,128)S(1)} custom-call(s32[2]{0:T(128)S(1)} %pad_add_fusion.where, f32[7,128,128]{2,1,0:T(8,128)} %copy-done.4, f32[9,128,128]{2,1,0:T(8,128)} %copy-done.3, f32[7,128,128]{2,1,0:T(8,128)} %copy-done.5, f32[5,128,128]{2,1,0:T(8,128)} %copy-done.10, bf16[4,128,512]{2,1,0:T(8,128)(2,1)S(1)} %get-tuple-element.43.refs_3_.refs_4_, ...), custom_call_target="tpu_custom_call" | custom-call | flops 201326592 | tf_op jit(solution)/shard_map/pallas_call | solution.py:38
  65.9 4.2 %collective-permute-done.11.halo0 = f32[2,2,128,128]{3,2,1,0:T(8,128)S(1)} collective-permute-done((f32[2,2,128,128]{3,2,1,0:T(8,128)S(1)}, f32[2,2,128,128]{3,2,1,0:T(8,128)S(1)}, u32[]{:S(2)}, u32[]{:S(2)}) %collective-permute-start.11) | collective-permute-done | bytes 262176 | tf_op jit(solution)/shard_map/ppermute | solution.py:305
  70.1 1.5 %collective-permute-start.12 = (f32[2,2,128,128]{3,2,1,0:T(8,128)S(1)}, f32[2,2,128,128]{3,2,1,0:T(8,128)S(1)}, u32[]{:S(2)}, u32[]{:S(2)}) collective-permute-start(f32[2,2,128,128]{3,2,1,0:T(8,128)S(1)} %shard_map.69), channel_id=1, source_target_pairs={{0,1},{1,0},{2,3},{3,2},{4,5},{5,4},{6,7},{7,6},{8,9},{9,8},{10,11... | collective-permute-start | bytes 786440 | tf_op jit(solution)/shard_map/ppermute | solution.py:305
  71.6 0.0 collective-permute-done.7.ss_any
  71.6 0.8 copy-done.12
  72.4 0.0 copy-done
  72.4 6.2 %shard_map.70 = (f32[2,1,8,128,128]{4,3,2,1,0:T(8,128)}, f32[2,4,128,128]{3,2,1,0:T(8,128)S(1)}) custom-call(s32[2]{0:T(128)S(1)} %pad_add_fusion.where, s32[2,1,8]{2,1,0:T(1,128)S(1)} %copy-done, f32[4,4,128,128]{3,2,1,0:T(8,128)} %copy-done.1, f32[2,4,128,128]{3,2,1,0:T(8,128)} %copy-done.12, f32[7,128,128]{2,1,0:T(8,128)} %copy-done.4, ...), custom_call_target="tpu_custom_call" | custom-call | flops 8053063680 | tf_op jit(solution)/shard_map/pallas_call | solution.py:38
  78.6 0.0 collective-permute-done.12.halo1
  78.6 1.4 %shard_map.71 = f32[2,1,8,128,128]{4,3,2,1,0:T(8,128)} custom-call(s32[2]{0:T(128)S(1)} %pad_add_fusion.where, s32[2,1,8]{2,1,0:T(1,128)S(1)} %copy-done, f32[2,4,128,128]{3,2,1,0:T(8,128)S(1)} %get-tuple-element.48.part, f32[2,2,128,128]{3,2,1,0:T(8,128)S(1)} %collective-permute-done.11.halo0, ...), custom_call_target="tpu_custom_call", output_to_operand_aliasing={{}: (5, {})} | custom-call | tf_op jit(solution)/shard_map/pallas_call | solution.py:38
  (16 shorter events, 0.1 us)
Async XLA Ops:
  1.4 7.0 %copy-start.2 = (f32[2,4,128,128]{3,2,1,0:T(8,128)}, f32[2,4,128,128]{3,2,1,0:T(8,128)S(1)}, u32[]{:S(2)}) copy-start(f32[2,4,128,128]{3,2,1,0:T(8,128)S(1)} %get-tuple-element.33.mine) | copy-start | bytes 1572868
  1.4 14.9 %collective-permute-start = (f32[2,4,128,128]{3,2,1,0:T(8,128)S(1)}, f32[2,4,128,128]{3,2,1,0:T(8,128)S(1)}, u32[]{:S(2)}, u32[]{:S(2)}) collective-permute-start(f32[2,4,128,128]{3,2,1,0:T(8,128)S(1)} %get-tuple-element.30), channel_id=1, source_target_pairs={{0,1},{1,0},{2,3},{3,2},{4,5},{5,4},{6,7},{7,6},{8,9},{9,8},{10,11... | collective-permute-start | bytes 1572872 | tf_op jit(solution)/shard_map/ppermute | solution.py:305
  4.4 15.2 %collective-permute-start.2 = (f32[2,4,128,128]{3,2,1,0:T(8,128)S(1)}, f32[2,4,128,128]{3,2,1,0:T(8,128)S(1)}, u32[]{:S(2)}, u32[]{:S(2)}) collective-permute-start(f32[2,4,128,128]{3,2,1,0:T(8,128)S(1)} %get-tuple-element.33.mine), channel_id=1, source_target_pairs={{0,2},{2,0},{4,6},{6,4},{8,10},{10,8},{12,14},{14,12},{16,18},{18,... | collective-permute-start | bytes 1572872 | tf_op jit(solution)/shard_map/ppermute | solution.py:308
  8.3 26.7 %copy-start.1 = (f32[4,4,128,128]{3,2,1,0:T(8,128)}, f32[4,4,128,128]{3,2,1,0:T(8,128)S(1)}, u32[]{:S(2)}) copy-start(f32[4,4,128,128]{3,2,1,0:T(8,128)S(1)} %get-tuple-element.38.u_any) | copy-start | bytes 3145732
  16.3 23.0 %copy-start.7 = (f32[2,4,128,128]{3,2,1,0:T(8,128)}, f32[2,4,128,128]{3,2,1,0:T(8,128)S(1)}, u32[]{:S(2)}) copy-start(f32[2,4,128,128]{3,2,1,0:T(8,128)S(1)} %collective-permute-done.refs_0_) | copy-start | bytes 1572868
  16.3 14.9 %collective-permute-start.5 = (f32[2,4,128,128]{3,2,1,0:T(8,128)S(1)}, f32[2,4,128,128]{3,2,1,0:T(8,128)S(1)}, u32[]{:S(2)}, u32[]{:S(2)}) collective-permute-start(f32[2,4,128,128]{3,2,1,0:T(8,128)S(1)} %collective-permute-done.refs_0_), channel_id=1, source_target_pairs={{0,2},{2,0},{4,6},{6,4},{8,10},{10,8},{12,14},{14,12},{16,18},{18,... | collective-permute-start | bytes 1572872 | tf_op jit(solution)/shard_map/ppermute | solution.py:308
  18.1 26.7 %collective-permute-start.4 = (f32[4,4,128,128]{3,2,1,0:T(8,128)S(1)}, f32[4,4,128,128]{3,2,1,0:T(8,128)S(1)}, u32[]{:S(2)}, u32[]{:S(2)}) collective-permute-start(f32[4,4,128,128]{3,2,1,0:T(8,128)S(1)} %get-tuple-element.38.u_any), channel_id=1, source_target_pairs={{0,1},{1,0},{2,3},{3,2},{4,5},{5,4},{6,7},{7,6},{8,9},{9,8},{10,11... | collective-permute-start | bytes 3145736 | tf_op jit(solution)/shard_map/ppermute | solution.py:305
  19.6 15.5 %copy-start.11 = (f32[2,4,128,128]{3,2,1,0:T(8,128)}, f32[2,4,128,128]{3,2,1,0:T(8,128)S(1)}, u32[]{:S(2)}) copy-start(f32[2,4,128,128]{3,2,1,0:T(8,128)S(1)} %collective-permute-done.2.other_y) | copy-start | bytes 1572868
  19.6 15.4 %collective-permute-start.3 = (f32[2,4,128,128]{3,2,1,0:T(8,128)S(1)}, f32[2,4,128,128]{3,2,1,0:T(8,128)S(1)}, u32[]{:S(2)}, u32[]{:S(2)}) collective-permute-start(f32[2,4,128,128]{3,2,1,0:T(8,128)S(1)} %collective-permute-done.2.other_y), channel_id=1, source_target_pairs={{0,4},{4,8},{8,12},{12,16},{16,20},{20,24},{24,28},{6,2},{10,6},{1... | collective-permute-start | bytes 1572872 | tf_op jit(solution)/shard_map/ppermute | solution.py:311
  23.1 16.3 %collective-permute-start.1 = (f32[7,128,128]{2,1,0:T(8,128)S(1)}, f32[7,128,128]{2,1,0:T(8,128)S(1)}, u32[]{:S(2)}, u32[]{:S(2)}) collective-permute-start(f32[7,128,128]{2,1,0:T(8,128)S(1)} %get-tuple-element.31), channel_id=1, source_target_pairs={{0,2},{2,0},{4,6},{6,4},{8,10},{10,8},{12,14},{14,12},{16,18},{18,... | collective-permute-start | bytes 1376264 | tf_op jit(solution)/shard_map/ppermute | solution.py:308
  31.2 8.2 %copy-start.8 = (f32[2,4,128,128]{3,2,1,0:T(8,128)}, f32[2,4,128,128]{3,2,1,0:T(8,128)S(1)}, u32[]{:S(2)}) copy-start(f32[2,4,128,128]{3,2,1,0:T(8,128)S(1)} %collective-permute-done.5.refs_1_) | copy-start | bytes 1572868
  31.2 13.6 %collective-permute-start.6 = (f32[2,4,128,128]{3,2,1,0:T(8,128)S(1)}, f32[2,4,128,128]{3,2,1,0:T(8,128)S(1)}, u32[]{:S(2)}, u32[]{:S(2)}) collective-permute-start(f32[2,4,128,128]{3,2,1,0:T(8,128)S(1)} %collective-permute-done.5.refs_1_), channel_id=1, source_target_pairs={{0,4},{4,8},{8,12},{12,16},{16,20},{20,24},{24,28},{6,2},{10,6},{1... | collective-permute-start | bytes 1572872 | tf_op jit(solution)/shard_map/ppermute | solution.py:311
  34.9 17.4 %collective-permute-start.8 = (f32[9,128,128]{2,1,0:T(8,128)S(1)}, f32[9,128,128]{2,1,0:T(8,128)S(1)}, u32[]{:S(2)}, u32[]{:S(2)}) collective-permute-start(f32[9,128,128]{2,1,0:T(8,128)S(1)} %get-tuple-element.41), channel_id=1, source_target_pairs={{0,2},{2,0},{4,6},{6,4},{8,10},{10,8},{12,14},{14,12},{16,18},{18,... | collective-permute-start | bytes 1769480 | tf_op jit(solution)/shard_map/ppermute | solution.py:308
  35.0 0.8 copy-start.13
  39.3 11.4 %copy-start.4 = (f32[7,128,128]{2,1,0:T(8,128)}, f32[7,128,128]{2,1,0:T(8,128)S(1)}, u32[]{:S(2)}) copy-start(f32[7,128,128]{2,1,0:T(8,128)S(1)} %collective-permute-done.1.refs_0_) | copy-start | bytes 1376260
  39.3 17.1 %collective-permute-start.9 = (f32[7,128,128]{2,1,0:T(8,128)S(1)}, f32[7,128,128]{2,1,0:T(8,128)S(1)}, u32[]{:S(2)}, u32[]{:S(2)}) collective-permute-start(f32[7,128,128]{2,1,0:T(8,128)S(1)} %collective-permute-done.1.refs_0_), channel_id=1, source_target_pairs={{0,4},{4,8},{8,12},{12,16},{16,20},{20,24},{24,28},{6,2},{10,6},{1... | collective-permute-start | bytes 1376264 | tf_op jit(solution)/shard_map/ppermute | solution.py:311
  44.8 1.0 %copy-start.6 = (f32[4,4,128,128]{3,2,1,0:T(8,128)}, f32[4,4,128,128]{3,2,1,0:T(8,128)S(1)}, u32[]{:S(2)}) copy-start(f32[4,4,128,128]{3,2,1,0:T(8,128)S(1)} %collective-permute-done.4.u_cross) | copy-start | bytes 3145732
  44.8 1.1 %copy-start.9 = (f32[2,4,128,128]{3,2,1,0:T(8,128)}, f32[2,4,128,128]{3,2,1,0:T(8,128)S(1)}, u32[]{:S(2)}) copy-start(f32[2,4,128,128]{3,2,1,0:T(8,128)S(1)} %collective-permute-done.6.refs_2_) | copy-start | bytes 1572868
  50.7 20.9 %collective-permute-start.7 = (f32[2,4,128,128]{3,2,1,0:T(8,128)S(1)}, f32[2,4,128,128]{3,2,1,0:T(8,128)S(1)}, u32[]{:S(2)}, u32[]{:S(2)}) collective-permute-start(f32[2,4,128,128]{3,2,1,0:T(8,128)S(1)} %get-tuple-element.39), channel_id=1, source_target_pairs={{0,1},{1,0},{2,3},{3,2},{4,5},{5,4},{6,7},{7,6},{8,9},{9,8},{10,11... | collective-permute-start | bytes 1572872 | tf_op jit(solution)/shard_map/ppermute | solution.py:305
  52.3 4.1 %copy-start.3 = (f32[9,128,128]{2,1,0:T(8,128)}, f32[9,128,128]{2,1,0:T(8,128)S(1)}, u32[]{:S(2)}) copy-start(f32[9,128,128]{2,1,0:T(8,128)S(1)} %collective-permute-done.8.refs_1_) | copy-start | bytes 1769476
  52.3 9.9 %collective-permute-start.10 = (f32[5,128,128]{2,1,0:T(8,128)S(1)}, f32[5,128,128]{2,1,0:T(8,128)S(1)}, u32[]{:S(2)}, u32[]{:S(2)}) collective-permute-start(f32[5,128,128]{2,1,0:T(8,128)S(1)} %slice.4), channel_id=1, source_target_pairs={{0,4},{4,8},{8,12},{12,16},{16,20},{20,24},{24,28},{6,2},{10,6},{1... | collective-permute-start | bytes 983048 | tf_op jit(solution)/shard_map/ppermute | solution.py:311
  56.4 0.8 copy-start.5
  60.1 12.3 %copy-start = (s32[2,1,8]{2,1,0:T(1,128)S(1)}, s32[2,1,8]{2,1,0:T(1,128)}, u32[]{:S(2)}) copy-start(s32[2,1,8]{2,1,0:T(1,128)} %o_mask.3) | copy-start | bytes 196
  60.1 9.9 %collective-permute-start.11 = (f32[2,2,128,128]{3,2,1,0:T(8,128)S(1)}, f32[2,2,128,128]{3,2,1,0:T(8,128)S(1)}, u32[]{:S(2)}, u32[]{:S(2)}) collective-permute-start(f32[2,2,128,128]{3,2,1,0:T(8,128)S(1)} %shard_map.68), channel_id=1, source_target_pairs={{0,1},{1,0},{2,3},{3,2},{4,5},{5,4},{6,7},{7,6},{8,9},{9,8},{10,11... | collective-permute-start | bytes 786440 | tf_op jit(solution)/shard_map/ppermute | solution.py:305
  62.2 0.7 copy-start.10
  70.1 8.5 %collective-permute-start.12 = (f32[2,2,128,128]{3,2,1,0:T(8,128)S(1)}, f32[2,2,128,128]{3,2,1,0:T(8,128)S(1)}, u32[]{:S(2)}, u32[]{:S(2)}) collective-permute-start(f32[2,2,128,128]{3,2,1,0:T(8,128)S(1)} %shard_map.69), channel_id=1, source_target_pairs={{0,1},{1,0},{2,3},{3,2},{4,5},{5,4},{6,7},{7,6},{8,9},{9,8},{10,11... | collective-permute-start | bytes 786440 | tf_op jit(solution)/shard_map/ppermute | solution.py:305
  71.6 0.8 copy-start.12

commit v4 on v3

v4 whole, which is shorter than its diff:
```python
import functools

import jax
import jax.numpy as jnp
from jax import lax
from jax.experimental import pallas as pl
from jax.experimental.pallas import tpu as pltpu
from jax.sharding import PartitionSpec as P

SLABS = ("row", "col")
F32 = jnp.float32
BF16 = jnp.bfloat16
VMEM = pl.BlockSpec(memory_space=pltpu.VMEM)
SMEM = pl.BlockSpec(memory_space=pltpu.SMEM)
ANY = pl.BlockSpec(memory_space=pl.ANY)
HBM = object()

PACK = (
    [(0, 0), (0, 1), (0, 2), (0, 3), (1, 0), (1, 1), (1, 2), (1, 3), (2, 0), (2, 1), (2, 2), (2, 3)]
    + [(3, 0), (3, 1), (3, 2), (3, 3)],
    [(0, 2), (0, 3), (1, 1), (1, 2), (1, 3), (2, 1), (2, 2), (2, 3), (3, 0), (3, 1), (3, 2), (3, 3)]
    + [(0, 0), (0, 1), (1, 0), (2, 0)],
)
PARTS = ((0, 7), (7, 9))


def shape(*dims, dtype=F32):
    return jax.ShapeDtypeStruct(dims, dtype)


def vmem(*dims, dtype=F32):
    return pltpu.VMEM(dims, dtype)


def call(body, outs, ins, scratch=(), flops=0, alias=None, limit=24):
    def kernel(*refs):
        slab = lax.axis_index("row") * lax.axis_size("col") + lax.axis_index("col")
        body((slab, lax.axis_index("layer")), *refs)

    def run(*args):
        placed = [pltpu.with_memory_space_constraint(x, pltpu.HBM) if spec is HBM else x for spec, x in zip(ins, args)]
        return pl.pallas_call(
            kernel,
            out_shape=outs,
            in_specs=[ANY if spec is HBM else spec for spec in ins],
            out_specs=[ANY if isinstance(x, jax.ShapeDtypeStruct) else VMEM for x in outs],
            scratch_shapes=list(scratch),
            input_output_aliases=alias or {},
            cost_estimate=pl.CostEstimate(flops=flops, bytes_accessed=0, transcendentals=0),
            compiler_params=pltpu.CompilerParams(vmem_limit_bytes=limit << 20),
        )(*placed)

    return run


def halves(x):
    high = x.astype(BF16)
    return high, (x - high.astype(F32)).astype(BF16)


def dot3(a, b, rhs_contract):
    one = functools.partial(
        lax.dot_general,
        dimension_numbers=(((1,), (rhs_contract,)), ((), ())),
        preferred_element_type=F32,
    )
    return one(a[0], b[0]) + (one(a[0], b[1]) + one(a[1], b[0]))


def joined(blocks, axis):
    return [jnp.concatenate(x, axis=axis) for x in zip(*[halves(b) for b in blocks])]


def aligned(block, size):
    return pl.multiple_of(block * size, size)


def slot_base(i, layer):
    return i // 2 if i % 2 == 0 else (i + 1) // 2 - layer


def start(src, dst, sem):
    copy = pltpu.make_async_copy(src, dst, sem)
    copy.start()
    return copy


def keep_p(where, p_mask_any, p_any, *refs):
    outs, (p_mask, p, sems) = refs[0:2], refs[2:]
    even = where[0] % 2 == 0
    copies = [start(p_any.at[a], p.at[a], sems.at[a]) for a in range(2)]
    start(p_mask_any, p_mask, sems.at[2]).wait()
    for a in range(2):
        copies[a].wait()
        for o in range(8):
            n = 4 * a + o // 2
            outs[1 - o % 2][jnp.where(even, n, (n + 7) % 8)] = p[a, 0, o] * p_mask[a, 0, o].astype(F32)


def keep_u(where, u_mask_any, u_any, *refs):
    outs, (u_mask, u, rows, packed, sems) = refs[0:3], refs[3:]
    copies = [start(u_any.at[i], u.at[i], sems.at[i]) for i in range(4)]
    start(u_mask_any, u_mask, sems.at[4]).wait()
    even = where[0] % 2 == 0
    stores = []
    for i in range(4):
        copies[i].wait()
        for m in range(4):
            rows[i, m] = u[i, m, 0] * u_mask[i, m].astype(F32)
        stores.append(start(rows.at[i], outs[0].at[i], sems.at[5 + i]))
    for par, case in ((0, even), (1, jnp.logical_not(even))):

        @pl.when(case)
        def _(par=par):
            for n, block in enumerate(PACK[par]):
                packed[n] = rows[block]

    for n, (first, count) in enumerate(PARTS):
        stores.append(start(packed.at[pl.ds(first, count)], outs[1 + n], sems.at[9 + n]))
    for c in stores:
        c.wait()


def fill_band(size, stage, hi_ref, lo_ref, shift, rows):
    for a in rows:
        for c in range(6):
            e = c - a - shift
            at = (pl.ds(a * size, size), pl.ds(c * size, size))
            if 0 <= e < 4:
                hi_ref[at], lo_ref[at] = halves(stage[4 * a + e])
            else:
                hi_ref[at] = jnp.zeros((size, size), BF16)
                lo_ref[at] = jnp.zeros((size, size), BF16)


def gather_pair(even, packed, own, stage, sems, first):
    base = 8 if own else jnp.where(even, 16, 0)
    rotated = jnp.logical_not(even) if own else even
    places = ((base + jnp.where(rotated, 1, 0), 0, 7), (base + jnp.where(rotated, 0, 7), 7, 1))
    return [
        start(packed.at[pl.ds(n, count)], stage.at[pl.ds(at, count)], sems.at[first + k])
        for k, (at, n, count) in enumerate(places)
    ]


def gather_next(even, packed, stage, sem):
    return start(packed.at[pl.ds(0, 7)], stage.at[pl.ds(jnp.where(even, 1, 16), 7)], sem)


def product_own(size, where, u_any, p_mask_any, p_any, pe_z, pe_y, pc, pc_y, *refs):
    t_own, ud_hi, ud_lo, oth_hi, oth_lo, p_mask, p, stages, u, hi, lo, sems = refs
    even, layer = where[0] % 2 == 0, where[1]
    copies = [start(u_any, u, sems.at[0])]
    copies += [start(p_any, p, sems.at[1]), start(p_mask_any, p_mask, sems.at[2])]
    copies += gather_pair(even, pe_y, False, stages.at[0], sems, 3)
    copies += gather_pair(even, pc, True, stages.at[1], sems, 5)
    copies += gather_pair(even, pc_y, False, stages.at[1], sems, 7)
    copies += [gather_next(even, pe_z, stages.at[0], sems.at[9])]
    ud_hi[...] = jnp.zeros_like(ud_hi)
    ud_lo[...] = jnp.zeros_like(ud_lo)
    for c in copies:
        c.wait()
    for i in range(4):
        cols = pl.ds(aligned(slot_base(i, layer), size), 4 * size)
        rows = pl.ds(i * size, size)
        ud_hi[rows, cols], ud_lo[rows, cols] = joined([u[i, m] for m in range(4)], 1)
    for a in range(2):
        for e in range(4):
            stages[0, 8 + 4 * a + e] = p[a, 0, 2 * e] * p_mask[a, 0, 2 * e].astype(F32)
    fill_band(size, stages.at[0], hi, lo, -2, range(6))
    for i in range(4):
        cols = pl.ds(aligned(slot_base(i, layer), size), 4 * size)
        rows = pl.ds(i * size, size)
        t_own[i] = dot3((ud_hi[rows, cols], ud_lo[rows, cols]), (hi[cols, cols], lo[cols, cols]), 0)
    fill_band(size, stages.at[1], oth_hi, oth_lo, -1, (2, 3))
    for case, rows in ((even, (4, 5)), (jnp.logical_not(even), (0, 1))):

        @pl.when(case)
        def _(rows=rows):
            fill_band(size, stages.at[1], oth_hi, oth_lo, -1, rows)


def product_rows(total_rows, size, where, send, t_mask, t_own, others, hi, lo, t_hi, t_lo):
    slab, layer = where[0], where[1]
    for q in range(2):
        i = 2 * q + (1 - layer if send else layer)
        base = q + 1 - layer if send else q
        rows = pl.ds(aligned(q if send else q + layer, size), 4 * size)
        cols = pl.ds(aligned(q + 1 if send else q + layer, size), 4 * size)
        left = joined([others[i, m] for m in range(4)], 1)
        total = t_own[i] + dot3(left, (hi[rows, cols], lo[rows, cols]), 0)
        kept = []
        for m in range(4):
            col = slab * 4 + 2 * (base + m) - 4 + layer
            keep = jnp.where((col >= 0) & (col < total_rows), t_mask[i, m], 0).astype(F32)
            kept.append(total[:, m * size : (m + 1) * size] * keep)
        t_hi[q], t_lo[q] = joined(kept, 1)


def product_send(total_rows, size, where, t_mask_any, t_own, ud_hi, ud_lo, hi_in, lo_in, u_cross, pc_z, *refs):
    t_hi, t_lo, ss, hi, lo, t_mask, stage, u_oth, sems = refs
    even, layer = where[0] % 2 == 0, where[1]
    z_copy = gather_next(even, pc_z, stage, sems.at[1])
    x_copies = [start(u_cross.at[2 * q + 1 - layer], u_oth.at[2 * q + 1 - layer], sems.at[3 * q]) for q in range(2)]
    mask_copy = start(t_mask_any, t_mask, sems.at[2])
    z_copy.wait()
    for case, rows in ((even, (0, 1)), (jnp.logical_not(even), (4, 5))):

        @pl.when(case)
        def _(rows=rows):
            fill_band(size, stage, hi, lo, -1, rows)

    mask_copy.wait()
    for c in x_copies:
        c.wait()
    product_rows(total_rows, size, where, True, t_mask, t_own, u_oth, hi, lo, t_hi, t_lo)
    for q in range(2):
        cols = pl.ds(aligned(q + 1 - layer, size), 4 * size)
        sums = dot3((t_hi[q], t_lo[q]), (ud_hi[:, cols], ud_lo[:, cols]), 1)
        for r in range(4):
            ss[q, r] = sums[:, r * size : (r + 1) * size]


def product_keep(total_rows, size, where, t_mask_any, t_own, hi, lo, u_cross, t_hi, t_lo, t_mask, u_oth, sems):
    layer = where[1]
    copies = [start(u_cross.at[2 * q + layer], u_oth.at[2 * q + layer], sems.at[q]) for q in range(2)]
    copies.append(start(t_mask_any, t_mask, sems.at[2]))
    for c in copies:
        c.wait()
    product_rows(total_rows, size, where, False, t_mask, t_own, u_oth, hi, lo, t_hi, t_lo)


def gather_halo(u_y, u_z, stage, sems):
    spots = [stage.at[pl.ds(at, n)] for at, n in (*PARTS, (16, 7), (23, 5))]
    return [start(src, spot, sems.at[n]) for n, (src, spot) in enumerate(zip([*u_y, *u_z], spots))]


def fill_halo(size, where, stage, uh_hi, uh_lo, rows=(0, 1, 2, 3)):
    even, layer = where[0] % 2 == 0, where[1]
    uh_hi[...] = jnp.zeros_like(uh_hi)
    uh_lo[...] = jnp.zeros_like(uh_lo)
    for below_at, above_at, pack, case in ((16, 0, PACK[1], even), (0, 16, PACK[0], jnp.logical_not(even))):

        @pl.when(case)
        def _(below_at=below_at, above_at=above_at, pack=pack):
            for first, above in ((below_at, 0), (above_at, 1)):
                for n, (r, m) in enumerate(pack[: 16 if first == 0 else 12]):
                    if r not in rows or (above and r == 3):
                        continue
                    at = pl.ds((above * len(rows) + rows.index(r)) * size, size)
                    cols = pl.ds(aligned(slot_base(r, layer) + 4 * above + m, size), size)
                    uh_hi[at, cols], uh_lo[at, cols] = halves(stage[first + n])


def halo_sums(size, i, base, t_rows, uh_hi, uh_lo, ts=(0, 1, 2, 3)):
    cols = pl.ds(aligned(base + 2, size), 4 * size)
    rows = [pl.ds(aligned(jnp.where(t < i, len(ts) + n, n), size), size) for n, t in enumerate(ts)]
    hi = jnp.concatenate([uh_hi[r, cols] for r in rows], axis=0)
    lo = jnp.concatenate([uh_lo[r, cols] for r in rows], axis=0)
    return dot3(t_rows, (hi, lo), 1)


def send_halo(size, ts, where, *refs):
    u_y, u_z, t_hi, t_lo = refs[0:2], refs[2:-7], refs[-7], refs[-6]
    out, stage, uh_hi, uh_lo, sems = refs[-5:]
    layer = where[1]
    for c in gather_halo(u_y, u_z, stage, sems):
        c.wait()
    fill_halo(size, where, stage, uh_hi, uh_lo, ts)
    for q in range(2):
        sums = halo_sums(size, 2 * q + 1 - layer, q + 1 - layer, (t_hi[q], t_lo[q]), uh_hi, uh_lo, ts)
        for n in range(len(ts)):
            out[q, n] = sums[:, n * size : (n + 1) * size]


def out_keep(total_rows, where, o_mask, q, o):
    col = where[0] * 4 + 2 * q + where[1] - 4 + o
    return jnp.where((col >= 0) & (col < total_rows), o_mask[q, 0, o], 0).astype(F32)


def keep_rows(total_rows, size, where, o_mask, ss, halo, *refs):
    u_y, u_z, t_hi, t_lo, ud_hi, ud_lo = refs[0:2], refs[2:4], *refs[4:8]
    out_any, part, out, stage, uh_hi, uh_lo, sems = refs[8:]
    for c in gather_halo(u_y, u_z, stage, sems):
        c.wait()
    fill_halo(size, where, stage, uh_hi, uh_lo)
    stores = []
    for q in range(2):
        i = 2 * q + where[1]
        sums = halo_sums(size, i, q, (t_hi[q], t_lo[q]), uh_hi, uh_lo)
        for t in range(4):
            o = (8 - i + t) % 8
            keep = out_keep(total_rows, where, o_mask, q, o)
            value = sums[:, t * size : (t + 1) * size]
            if t < 2:
                out[q, 4 + t] = (value + halo[q, t]) * keep
                stores.append(start(out.at[q, 4 + t], out_any.at[q, 0, o], sems.at[4 + 2 * q + t]))
            else:
                part[q, t - 2] = value * keep
        cols = pl.ds(q * size, 4 * size)
        sums = dot3((t_hi[q], t_lo[q]), (ud_hi[:, cols], ud_lo[:, cols]), 1)
        for r in range(4):
            o = (4 - i + r) % 8
            keep = out_keep(total_rows, where, o_mask, q, o)
            out[q, r] = (sums[:, r * size : (r + 1) * size] + ss[q, r]) * keep
            stores.append(start(out.at[q, r], out_any.at[q, 0, o], sems.at[8 + 4 * q + r]))
    for c in stores:
        c.wait()


def combine(total_rows, where, o_mask, part, halo, kept_any, out_any, done, sems):
    stores = []
    for q in range(2):
        for t in range(2):
            o = (10 - 2 * q - where[1] + t) % 8
            done[q, t] = part[q, t] + halo[q, t] * out_keep(total_rows, where, o_mask, q, o)
            stores.append(start(done.at[q, t], out_any.at[q, 0, o], sems.at[2 * q + t]))
    for s in stores:
        s.wait()


def after(x, *others):
    return lax.optimization_barrier((x, *others))[0]


def on_device(u_values, u_mask, p_values, p_mask, t_mask, out_mask):
    size = u_values.shape[-1]
    slabs = lax.axis_size(SLABS)
    total_rows = slabs * u_values.shape[0]
    swap = [(0, 1), (1, 0)]
    pair = [(s, s ^ 1) for s in range(slabs)]
    onward = [(s, s + 2) for s in range(0, slabs - 2, 2)] + [(s, s - 2) for s in range(3, slabs, 2)]

    def over_layer(x):
        return lax.ppermute(x, "layer", swap)

    def over_pair(x):
        return lax.ppermute(x, SLABS, pair)

    def onto(x):
        return lax.ppermute(x, SLABS, onward)

    def sems(n):
        return pltpu.SemaphoreType.DMA((n,))

    eight = shape(2, 4, size, size)
    wide = 6 * size
    unit = 3 * 2 * (4 * size) ** 2 * size
    po, pe = call(
        keep_p,
        [vmem(8, size, size)] * 2,
        [HBM, HBM],
        [pltpu.SMEM(p_mask.shape, jnp.int32), vmem(*p_values.shape), sems(3)],
    )(p_mask, p_values)
    pc = over_layer(po)
    pe_y = over_pair(pe)
    u_mask, t_mask = u_mask[:, :, 0], t_mask[:, :, 0]
    u_own, *packed = call(
        keep_u,
        [shape(4, 4, size, size)] + [shape(n, size, size) for _, n in PARTS],
        [HBM, HBM],
        [pltpu.SMEM(u_mask.shape, jnp.int32), vmem(*u_values.shape), vmem(4, 4, size, size)]
        + [vmem(16, size, size), sems(11)],
    )(u_mask, u_values)
    u_oth = over_layer(after(u_own, pc))
    pe_z = onto(after(pe_y[:7], u_own))
    pc_y = over_pair(pc)
    pc_z = onto(pc_y)
    t_like = (4, size, 4 * size)
    band = [vmem(wide, wide, dtype=BF16)] * 2
    own_rows = [vmem(4 * size, wide, dtype=BF16)] * 2
    t_own, ud_hi, ud_lo, *oth = call(
        functools.partial(product_own, size),
        [vmem(*t_like), *own_rows, *band],
        [HBM, HBM, HBM, ANY] + [HBM] * 3,
        [pltpu.SMEM(p_mask.shape, jnp.int32), vmem(*p_values.shape)]
        + [vmem(2, 24, size, size), vmem(4, 4, size, size), *band, sems(10)],
        flops=4 * unit,
    )(u_own, p_mask, p_values, pe_z, pe_y, pc, pc_y)
    u_y = [over_pair(after(x, pc)) for x in packed]
    u_z = [onto(after(u_y[0], t_own))]
    t_mask = after(t_mask, u_y[0])
    rows = [vmem(2, size, 4 * size, dtype=BF16)] * 2
    masks = pltpu.SMEM(t_mask.shape, jnp.int32)
    *t_send, ss, hi, lo = call(
        functools.partial(product_send, total_rows, size),
        [*rows, vmem(2, 4, size, size), *band],
        [HBM] + [VMEM] * 5 + [ANY] * 2,
        [masks, vmem(24, size, size), vmem(4, 4, size, size), sems(4)],
        flops=4 * unit,
        alias={4: 3, 5: 4},
    )(t_mask, t_own, ud_hi, ud_lo, *oth, u_oth, pc_z)
    ss_got = over_layer(ss)
    t_keep = call(
        functools.partial(product_keep, total_rows, size),
        rows,
        [HBM] + [VMEM] * 3 + [ANY],
        [masks, vmem(4, 4, size, size), sems(3)],
        flops=2 * unit,
    )(t_mask, t_own, hi, lo, u_oth)
    u_z.append(onto(after(u_y[1][:5], t_send[0])))
    halos = []
    halo_scratch = [vmem(28, size, size)] + [vmem(4 * size, 9 * size, dtype=BF16)] * 2 + [sems(4)]
    for ts in ((0, 1), (2, 3)):
        nz = 1 if ts[0] == 0 else 2
        (halo,) = call(
            functools.partial(send_halo, size, ts),
            [vmem(2, 2, size, size)],
            [HBM] * 2 + [ANY] * nz + [VMEM] * 2,
            halo_scratch,
            flops=unit,
        )(*u_y, *u_z[:nz], t_send[0], after(t_send[1], *halos))
        halos.append(halo)
    halos = [over_layer(x) for x in halos]
    kept, part = call(
        functools.partial(keep_rows, total_rows, size),
        [shape(*p_values.shape), vmem(2, 2, size, size)],
        [SMEM] + [VMEM] * 2 + [HBM] * 2 + [ANY] * 2 + [VMEM] * 4,
        [vmem(2, 6, size, size), vmem(28, size, size)] + [vmem(8 * size, 9 * size, dtype=BF16)] * 2 + [sems(16)],
        flops=40 * unit,
    )(out_mask, ss_got, halos[0], *u_y, *u_z, *t_keep, ud_hi, ud_lo)
    (out,) = call(
        functools.partial(combine, total_rows),
        [shape(*p_values.shape)],
        [SMEM, VMEM, VMEM, ANY],
        [vmem(2, 2, size, size), sems(4)],
        alias={3: 0},
        limit=16,
    )(out_mask, part, halos[1], kept)
    return out


def solution(mesh):
    placed = (
        P(SLABS, None, "layer", None, None),
        P(SLABS, None, "layer"),
        P(SLABS, "layer", None, None, None),
        P(SLABS, "layer", None),
        P(SLABS, None, "layer"),
        P(SLABS, "layer", None),
    )
    return jax.shard_map(
        on_device,
        mesh=mesh,
        in_specs=placed,
        out_specs=P(SLABS, "layer", None, None, None),
        check_vma=False,
    )
```

time: 80.4 us -> 74.2 us (0.923)
  local copies, waits for them, and re-layouts: 4.25 us -> 0.08 us
  Pallas kernels: 25.4 us -> 21.7 us
  waiting for transfers between devices: 20.2 us -> 22.9 us
    unnamed x28 -> x14, local copies, waits for them, and re-layouts: 4.23 us -> 0.03 us
    pallas_call x8 -> x9, Pallas kernels: 25.4 us -> 21.7 us  [run(): pl.pallas_call(kernel, out_shape=outs, in_specs=[ANY if spec is HBM else...]
    ppermute x4, waiting for transfers between devices: 8.01 us -> 11.1 us  [over_pair(): return lax.ppermute(x, SLABS, pair)]
    ppermute x5, waiting for transfers between devices: 12.2 us -> 10.9 us  [over_layer(): return lax.ppermute(x, 'layer', swap)]
    ppermute x4, waiting for transfers between devices: 0.01 us -> 0.85 us  [onto(): return lax.ppermute(x, SLABS, onward)]
  transfers between devices with their start and end apart: 13 -> 13, of which waited for: 3 -> 7; matrix products, arithmetic and copies ran while one was open for 0% -> 0% of each run, Pallas kernels for 28% -> 26%
where the time goes in v4:
time: 74.2 us; the launch traced here: 73.9 us
  starting transfers between devices  29 us (39%)
  waiting for transfers between devices  22.9 us (31%)
  Pallas kernels  21.7 us (29%)
    pallas_call x9, Pallas kernels, run(): pl.pallas_call(kernel, out_shape=outs, in_specs=[ANY if spec is HBM else...  21.7 us
    ppermute x4, starting transfers between devices, onto(): return lax.ppermute(x, SLABS, onward)  16.5 us
    ppermute x4, waiting for transfers between devices, over_pair(): return lax.ppermute(x, SLABS, pair)  11.1 us
    ppermute x5, waiting for transfers between devices, over_layer(): return lax.ppermute(x, 'layer', swap)  10.9 us
    ppermute x5, starting transfers between devices, over_layer(): return lax.ppermute(x, 'layer', swap)  9.1 us
    ppermute x4, starting transfers between devices, over_pair(): return lax.ppermute(x, SLABS, pair)  3.43 us
  transfers between devices with their start and end apart: 13, of which 7 were waited for; matrix products, arithmetic and copies ran while one was open for 0% of the time, Pallas kernels for 26%

profile of v4, /device:TPU:0, one launch (start us, length us, event | category | flops | bytes accessed | tf_op | source)
XLA Modules:
  0.0 73.9 jit_solution(3523755371647367273)
XLA Ops:
  0.0 1.3 %shard_map.65 = (f32[8,128,128]{2,1,0:T(8,128)S(1)}, f32[8,128,128]{2,1,0:T(8,128)S(1)}) custom-call(s32[2,1,8]{2,1,0:T(1,128)} %refs_1_.5, f32[2,1,8,128,128]{4,3,2,1,0:T(8,128)} %refs_2_.1), custom_call_target="tpu_custom_call" | custom-call | tf_op jit(solution)/shard_map/pallas_call | solution.py:42
  1.3 3.0 %collective-permute-start = (f32[8,128,128]{2,1,0:T(8,128)S(1)}, f32[8,128,128]{2,1,0:T(8,128)S(1)}, u32[]{:S(2)}, u32[]{:S(2)}) collective-permute-start(f32[8,128,128]{2,1,0:T(8,128)S(1)} %get-tuple-element.33), channel_id=1, source_target_pairs={{0,1},{1,0},{2,3},{3,2},{4,5},{5,4},{6,7},{7,6},{8,9},{9,8},{10,11... | collective-permute-start | bytes 1572872 | tf_op jit(solution)/shard_map/ppermute | solution.py:335
  4.3 1.5 %collective-permute-start.2 = (f32[8,128,128]{2,1,0:T(8,128)S(1)}, f32[8,128,128]{2,1,0:T(8,128)S(1)}, u32[]{:S(2)}, u32[]{:S(2)}) collective-permute-start(f32[8,128,128]{2,1,0:T(8,128)S(1)} %get-tuple-element.37), channel_id=1, source_target_pairs={{0,2},{2,0},{4,6},{6,4},{8,10},{10,8},{12,14},{14,12},{16,18},{18,... | collective-permute-start | bytes 1572872 | tf_op jit(solution)/shard_map/ppermute | solution.py:338
  5.8 1.8 %shard_map.64 = (f32[4,4,128,128]{3,2,1,0:T(8,128)S(1)}, f32[7,128,128]{2,1,0:T(8,128)S(1)}, f32[9,128,128]{2,1,0:T(8,128)S(1)}) custom-call(s32[4,4]{1,0:T(4,128)} %bitcast.4, f32[4,4,1,128,128]{4,3,2,1,0:T(8,128)} %refs_1_.3), custom_call_target="tpu_custom_call" | custom-call | tf_op jit(solution)/shard_map/pallas_call | solution.py:42
  7.6 0.0 copy-start
  7.6 8.6 %collective-permute-done.refs_5_ = f32[8,128,128]{2,1,0:T(8,128)S(1)} collective-permute-done((f32[8,128,128]{2,1,0:T(8,128)S(1)}, f32[8,128,128]{2,1,0:T(8,128)S(1)}, u32[]{:S(2)}, u32[]{:S(2)}) %collective-permute-start) | collective-permute-done | bytes 524320 | tf_op jit(solution)/shard_map/ppermute | solution.py:335
  16.2 0.0 copy-start.5
  16.2 1.8 %collective-permute-start.4 = (f32[8,128,128]{2,1,0:T(8,128)S(1)}, f32[8,128,128]{2,1,0:T(8,128)S(1)}, u32[]{:S(2)}, u32[]{:S(2)}) collective-permute-start(f32[8,128,128]{2,1,0:T(8,128)S(1)} %collective-permute-done.refs_5_), channel_id=1, source_target_pairs={{0,2},{2,0},{4,6},{6,4},{8,10},{10,8},{12,14},{14,12},{16,18},{18,... | collective-permute-start | bytes 1572872 | tf_op jit(solution)/shard_map/ppermute | solution.py:338
  18.0 1.5 %collective-permute-start.5 = (f32[4,4,128,128]{3,2,1,0:T(8,128)S(1)}, f32[4,4,128,128]{3,2,1,0:T(8,128)S(1)}, u32[]{:S(2)}, u32[]{:S(2)}) collective-permute-start(f32[4,4,128,128]{3,2,1,0:T(8,128)S(1)} %get-tuple-element.44.refs_0_), channel_id=1, source_target_pairs={{0,1},{1,0},{2,3},{3,2},{4,5},{5,4},{6,7},{7,6},{8,9},{9,8},{10,11... | collective-permute-start | bytes 3145736 | tf_op jit(solution)/shard_map/ppermute | solution.py:335
  19.5 0.0 collective-permute-done.2.refs_4_
  19.5 0.0 copy-start.3
  19.5 3.5 %collective-permute-start.3 = (f32[7,128,128]{2,1,0:T(8,128)S(1)}, f32[7,128,128]{2,1,0:T(8,128)S(1)}, u32[]{:S(2)}, u32[]{:S(2)}) collective-permute-start(f32[7,128,128]{2,1,0:T(8,128)S(1)} %slice.8), channel_id=1, source_target_pairs={{0,4},{4,8},{8,12},{12,16},{16,20},{20,24},{24,28},{6,2},{10,6},{1... | collective-permute-start | bytes 1376264 | tf_op jit(solution)/shard_map/ppermute | solution.py:341
  23.0 0.1 collective-permute-start.1
  23.1 8.0 %collective-permute-done.4.refs_6_ = f32[8,128,128]{2,1,0:T(8,128)S(1)} collective-permute-done((f32[8,128,128]{2,1,0:T(8,128)S(1)}, f32[8,128,128]{2,1,0:T(8,128)S(1)}, u32[]{:S(2)}, u32[]{:S(2)}) %collective-permute-start.4) | collective-permute-done | bytes 524320 | tf_op jit(solution)/shard_map/ppermute | solution.py:338
  31.1 0.0 copy-start.6
  31.1 3.8 %collective-permute-start.6 = (f32[8,128,128]{2,1,0:T(8,128)S(1)}, f32[8,128,128]{2,1,0:T(8,128)S(1)}, u32[]{:S(2)}, u32[]{:S(2)}) collective-permute-start(f32[8,128,128]{2,1,0:T(8,128)S(1)} %collective-permute-done.4.refs_6_), channel_id=1, source_target_pairs={{0,4},{4,8},{8,12},{12,16},{16,20},{20,24},{24,28},{6,2},{10,6},{1... | collective-permute-start | bytes 1572872 | tf_op jit(solution)/shard_map/ppermute | solution.py:341
  34.8 0.1 collective-permute-start.8
  34.9 0.0 collective-permute-done.3.refs_3_
  34.9 0.0 copy-done
  34.9 0.0 copy-done.5
  34.9 0.0 copy-done.3
  34.9 0.0 copy-done.6
  35.0 3.6 %shard_map.66 = (f32[4,128,512]{2,1,0:T(8,128)S(1)}, bf16[512,768]{1,0:T(8,128)(2,1)S(1)}, bf16[512,768]{1,0:T(8,128)(2,1)S(1)}, bf16[768,768]{1,0:T(8,128)(2,1)S(1)}, bf16[768,768]{1,0:T(8,128)(2,1)S(1)}) custom-call(f32[4,4,128,128]{3,2,1,0:T(8,128)} %copy-done, s32[2,1,8]{2,1,0:T(1,128)} %refs_1_.5, f32[2,1,8,128,128]{4,3,2,1,0:T(8,128)} %refs_2_.1, ...), custom_call_target="tpu_custom_call" | custom-call | flops 805306368 | tf_op jit(solution)/shard_map/pallas_call | solution.py:42
  38.5 0.6 collective-permute-done.1.refs_0_.refs_3_
  39.1 0.0 copy-start.4
  39.1 5.5 %collective-permute-start.9 = (f32[7,128,128]{2,1,0:T(8,128)S(1)}, f32[7,128,128]{2,1,0:T(8,128)S(1)}, u32[]{:S(2)}, u32[]{:S(2)}) collective-permute-start(f32[7,128,128]{2,1,0:T(8,128)S(1)} %collective-permute-done.1.refs_0_.refs_3_), channel_id=1, source_target_pairs={{0,4},{4,8},{8,12},{12,16},{16,20},{20,24},{24,28},{6,2},{10,6},{1... | collective-permute-start | bytes 1376264 | tf_op jit(solution)/shard_map/ppermute | solution.py:341
  44.7 0.0 collective-permute-done.5.refs_6_.refs_4_
  44.7 0.0 collective-permute-done.6.refs_7_
  44.7 2.7 %shard_map.67 = (bf16[2,128,512]{2,1,0:T(8,128)(2,1)S(1)}, bf16[2,128,512]{2,1,0:T(8,128)(2,1)S(1)}, f32[2,4,128,128]{3,2,1,0:T(8,128)S(1)}, bf16[768,768]{1,0:T(8,128)(2,1)S(1)}, bf16[768,768]{1,0:T(8,128)(2,1)S(1)}) custom-call(s32[4,4]{1,0:T(4,128)} %bitcast.2, ...), custom_call_target="tpu_custom_call", output_to_operand_aliasing={{3}: (4, {}), {4}: (5, {})} | custom-call | flops 805306368 | tf_op jit(solution)/shard_map/pallas_call | solution.py:42
  47.3 0.0 copy-done.4
  47.3 1.6 %collective-permute-start.7 = (f32[2,4,128,128]{3,2,1,0:T(8,128)S(1)}, f32[2,4,128,128]{3,2,1,0:T(8,128)S(1)}, u32[]{:S(2)}, u32[]{:S(2)}) collective-permute-start(f32[2,4,128,128]{3,2,1,0:T(8,128)S(1)} %get-tuple-element.45), channel_id=1, source_target_pairs={{0,1},{1,0},{2,3},{3,2},{4,5},{5,4},{6,7},{7,6},{8,9},{9,8},{10,11... | collective-permute-start | bytes 1572872 | tf_op jit(solution)/shard_map/ppermute | solution.py:335
  48.9 2.6 %collective-permute-done.8.refs_1_.refs_4_ = f32[9,128,128]{2,1,0:T(8,128)S(1)} collective-permute-done((f32[9,128,128]{2,1,0:T(8,128)S(1)}, f32[9,128,128]{2,1,0:T(8,128)S(1)}, u32[]{:S(2)}, u32[]{:S(2)}) %collective-permute-start.8) | collective-permute-done | bytes 589856 | tf_op jit(solution)/shard_map/ppermute | solution.py:338
  51.5 3.7 %collective-permute-start.11 = (f32[5,128,128]{2,1,0:T(8,128)S(1)}, f32[5,128,128]{2,1,0:T(8,128)S(1)}, u32[]{:S(2)}, u32[]{:S(2)}) collective-permute-start(f32[5,128,128]{2,1,0:T(8,128)S(1)} %slice.9), channel_id=1, source_target_pairs={{0,4},{4,8},{8,12},{12,16},{16,20},{20,24},{24,28},{6,2},{10,6},{1... | collective-permute-start | bytes 983048 | tf_op jit(solution)/shard_map/ppermute | solution.py:341
  55.3 0.0 collective-permute-done.9.refs_2_.refs_5_
  55.3 0.0 copy-done.2
  55.3 2.2 %shard_map.68 = f32[2,2,128,128]{3,2,1,0:T(8,128)S(1)} custom-call(f32[7,128,128]{2,1,0:T(8,128)} %copy-done.4, f32[9,128,128]{2,1,0:T(8,128)} %copy-done.2, f32[7,128,128]{2,1,0:T(8,128)S(1)} %collective-permute-done.9.refs_2_.refs_5_, bf16[2,128,512]{2,1,0:T(8,128)(2,1)S(1)} %get-tuple-element.49.refs_3_.refs_4_, ...), custom_call_target="tpu_custom_call" | custom-call | flops 201326592 | tf_op jit(solution)/shard_map/pallas_call | solution.py:42
  57.5 1.6 %collective-permute-start.10 = (f32[2,2,128,128]{3,2,1,0:T(8,128)S(1)}, f32[2,2,128,128]{3,2,1,0:T(8,128)S(1)}, u32[]{:S(2)}, u32[]{:S(2)}) collective-permute-start(f32[2,2,128,128]{3,2,1,0:T(8,128)S(1)} %shard_map.68), channel_id=1, source_target_pairs={{0,1},{1,0},{2,3},{3,2},{4,5},{5,4},{6,7},{7,6},{8,9},{9,8},{10,11... | collective-permute-start | bytes 786440 | tf_op jit(solution)/shard_map/ppermute | solution.py:335
  59.0 1.4 %shard_map.69 = (bf16[2,128,512]{2,1,0:T(8,128)(2,1)S(1)}, bf16[2,128,512]{2,1,0:T(8,128)(2,1)S(1)}) custom-call(s32[4,4]{1,0:T(4,128)} %bitcast.3, f32[4,128,512]{2,1,0:T(8,128)S(1)} %get-tuple-element.39.refs_1_, bf16[768,768]{1,0:T(8,128)(2,1)S(1)} %get-tuple-element.52.refs_2_, bf16[768,768]{1,0:T(8,128)(2,1)S(1)} %get-tuple-element.53.refs_3_, ...), custom_call_target="tpu_custom_call" | custom-call | flops 402653184 | tf_op jit(solution)/shard_map/pallas_call | solution.py:42
  60.4 0.0 copy-start.1
  60.4 0.8 %collective-permute-done.11.refs_6_.refs_3_ = f32[5,128,128]{2,1,0:T(8,128)S(1)} collective-permute-done((f32[5,128,128]{2,1,0:T(8,128)S(1)}, f32[5,128,128]{2,1,0:T(8,128)S(1)}, u32[]{:S(2)}, u32[]{:S(2)}) %collective-permute-start.11) | collective-permute-done | bytes 327712 | tf_op jit(solution)/shard_map/ppermute | solution.py:341
  61.2 2.2 %shard_map.71 = f32[2,2,128,128]{3,2,1,0:T(8,128)S(1)} custom-call(f32[7,128,128]{2,1,0:T(8,128)} %copy-done.4, f32[9,128,128]{2,1,0:T(8,128)} %copy-done.2, f32[7,128,128]{2,1,0:T(8,128)S(1)} %collective-permute-done.9.refs_2_.refs_5_, f32[5,128,128]{2,1,0:T(8,128)S(1)} %collective-permute-done.11.refs_6_.refs_3_, ...), custom_call_target="tpu_custom_call" | custom-call | flops 201326592 | tf_op jit(solution)/shard_map/pallas_call | solution.py:42
  63.4 1.5 %collective-permute-start.12 = (f32[2,2,128,128]{3,2,1,0:T(8,128)S(1)}, f32[2,2,128,128]{3,2,1,0:T(8,128)S(1)}, u32[]{:S(2)}, u32[]{:S(2)}) collective-permute-start(f32[2,2,128,128]{3,2,1,0:T(8,128)S(1)} %shard_map.71), channel_id=1, source_target_pairs={{0,1},{1,0},{2,3},{3,2},{4,5},{5,4},{6,7},{7,6},{8,9},{9,8},{10,11... | collective-permute-start | bytes 786440 | tf_op jit(solution)/shard_map/ppermute | solution.py:335
  64.9 1.1 %collective-permute-done.10.refs_2_ = f32[2,2,128,128]{3,2,1,0:T(8,128)S(1)} collective-permute-done((f32[2,2,128,128]{3,2,1,0:T(8,128)S(1)}, f32[2,2,128,128]{3,2,1,0:T(8,128)S(1)}, u32[]{:S(2)}, u32[]{:S(2)}) %collective-permute-start.10) | collective-permute-done | bytes 262176 | tf_op jit(solution)/shard_map/ppermute | solution.py:335
  66.0 0.0 collective-permute-done.7.refs_1_
  66.0 0.0 copy-done.1
  66.0 5.3 %shard_map.70 = (f32[2,1,8,128,128]{4,3,2,1,0:T(8,128)}, f32[2,2,128,128]{3,2,1,0:T(8,128)S(1)}) custom-call(s32[2,1,8]{2,1,0:T(1,128)S(1)} %copy-done.1, f32[2,4,128,128]{3,2,1,0:T(8,128)S(1)} %collective-permute-done.7.refs_1_, f32[2,2,128,128]{3,2,1,0:T(8,128)S(1)} %collective-permute-done.10.refs_2_, f32[7,128,128]{2,1,0:T(8,128)} %copy-done.4, ...), custom_call_target="tpu_custom_call" | custom-call | flops 8053063680 | tf_op jit(solution)/shard_map/pallas_call | solution.py:42
  71.4 1.2 %collective-permute-done.12.refs_2_ = f32[2,2,128,128]{3,2,1,0:T(8,128)S(1)} collective-permute-done((f32[2,2,128,128]{3,2,1,0:T(8,128)S(1)}, f32[2,2,128,128]{3,2,1,0:T(8,128)S(1)}, u32[]{:S(2)}, u32[]{:S(2)}) %collective-permute-start.12) | collective-permute-done | bytes 262176 | tf_op jit(solution)/shard_map/ppermute | solution.py:335
  72.6 1.3 %shard_map.72 = f32[2,1,8,128,128]{4,3,2,1,0:T(8,128)} custom-call(s32[2,1,8]{2,1,0:T(1,128)S(1)} %copy-done.1, f32[2,2,128,128]{3,2,1,0:T(8,128)S(1)} %get-tuple-element.56.refs_1_, f32[2,2,128,128]{3,2,1,0:T(8,128)S(1)} %collective-permute-done.12.refs_2_, f32[2,1,8,128,128]{4,3,2,1,0:T(8,128)} %get-tuple-element.58.refs_3_), custom_call_target="tpu_custom_call", output_to_operand_aliasing={{}: (3, {})} | custom-call | tf_op jit(solution)/shard_map/pallas_call | solution.py:42
  (3 shorter events, 0.1 us)
Async XLA Ops:
  1.3 14.9 %collective-permute-start = (f32[8,128,128]{2,1,0:T(8,128)S(1)}, f32[8,128,128]{2,1,0:T(8,128)S(1)}, u32[]{:S(2)}, u32[]{:S(2)}) collective-permute-start(f32[8,128,128]{2,1,0:T(8,128)S(1)} %get-tuple-element.33), channel_id=1, source_target_pairs={{0,1},{1,0},{2,3},{3,2},{4,5},{5,4},{6,7},{7,6},{8,9},{9,8},{10,11... | collective-permute-start | bytes 1572872 | tf_op jit(solution)/shard_map/ppermute | solution.py:335
  4.3 15.2 %collective-permute-start.2 = (f32[8,128,128]{2,1,0:T(8,128)S(1)}, f32[8,128,128]{2,1,0:T(8,128)S(1)}, u32[]{:S(2)}, u32[]{:S(2)}) collective-permute-start(f32[8,128,128]{2,1,0:T(8,128)S(1)} %get-tuple-element.37), channel_id=1, source_target_pairs={{0,2},{2,0},{4,6},{6,4},{8,10},{10,8},{12,14},{14,12},{16,18},{18,... | collective-permute-start | bytes 1572872 | tf_op jit(solution)/shard_map/ppermute | solution.py:338
  7.6 27.3 %copy-start = (f32[4,4,128,128]{3,2,1,0:T(8,128)}, f32[4,4,128,128]{3,2,1,0:T(8,128)S(1)}, u32[]{:S(2)}) copy-start(f32[4,4,128,128]{3,2,1,0:T(8,128)S(1)} %get-tuple-element.44.refs_0_) | copy-start | bytes 3145732
  16.2 18.7 %copy-start.5 = (f32[8,128,128]{2,1,0:T(8,128)}, f32[8,128,128]{2,1,0:T(8,128)S(1)}, u32[]{:S(2)}) copy-start(f32[8,128,128]{2,1,0:T(8,128)S(1)} %collective-permute-done.refs_5_) | copy-start | bytes 1572868
  16.2 14.9 %collective-permute-start.4 = (f32[8,128,128]{2,1,0:T(8,128)S(1)}, f32[8,128,128]{2,1,0:T(8,128)S(1)}, u32[]{:S(2)}, u32[]{:S(2)}) collective-permute-start(f32[8,128,128]{2,1,0:T(8,128)S(1)} %collective-permute-done.refs_5_), channel_id=1, source_target_pairs={{0,2},{2,0},{4,6},{6,4},{8,10},{10,8},{12,14},{14,12},{16,18},{18,... | collective-permute-start | bytes 1572872 | tf_op jit(solution)/shard_map/ppermute | solution.py:338
  18.0 26.7 %collective-permute-start.5 = (f32[4,4,128,128]{3,2,1,0:T(8,128)S(1)}, f32[4,4,128,128]{3,2,1,0:T(8,128)S(1)}, u32[]{:S(2)}, u32[]{:S(2)}) collective-permute-start(f32[4,4,128,128]{3,2,1,0:T(8,128)S(1)} %get-tuple-element.44.refs_0_), channel_id=1, source_target_pairs={{0,1},{1,0},{2,3},{3,2},{4,5},{5,4},{6,7},{7,6},{8,9},{9,8},{10,11... | collective-permute-start | bytes 3145736 | tf_op jit(solution)/shard_map/ppermute | solution.py:335
  19.5 15.5 %copy-start.3 = (f32[8,128,128]{2,1,0:T(8,128)}, f32[8,128,128]{2,1,0:T(8,128)S(1)}, u32[]{:S(2)}) copy-start(f32[8,128,128]{2,1,0:T(8,128)S(1)} %collective-permute-done.2.refs_4_) | copy-start | bytes 1572868
  19.5 15.4 %collective-permute-start.3 = (f32[7,128,128]{2,1,0:T(8,128)S(1)}, f32[7,128,128]{2,1,0:T(8,128)S(1)}, u32[]{:S(2)}, u32[]{:S(2)}) collective-permute-start(f32[7,128,128]{2,1,0:T(8,128)S(1)} %slice.8), channel_id=1, source_target_pairs={{0,4},{4,8},{8,12},{12,16},{16,20},{20,24},{24,28},{6,2},{10,6},{1... | collective-permute-start | bytes 1376264 | tf_op jit(solution)/shard_map/ppermute | solution.py:341
  23.0 16.1 %collective-permute-start.1 = (f32[7,128,128]{2,1,0:T(8,128)S(1)}, f32[7,128,128]{2,1,0:T(8,128)S(1)}, u32[]{:S(2)}, u32[]{:S(2)}) collective-permute-start(f32[7,128,128]{2,1,0:T(8,128)S(1)} %get-tuple-element.34), channel_id=1, source_target_pairs={{0,2},{2,0},{4,6},{6,4},{8,10},{10,8},{12,14},{14,12},{16,18},{18,... | collective-permute-start | bytes 1376264 | tf_op jit(solution)/shard_map/ppermute | solution.py:338
  31.1 3.9 %copy-start.6 = (f32[8,128,128]{2,1,0:T(8,128)}, f32[8,128,128]{2,1,0:T(8,128)S(1)}, u32[]{:S(2)}) copy-start(f32[8,128,128]{2,1,0:T(8,128)S(1)} %collective-permute-done.4.refs_6_) | copy-start | bytes 1572868
  31.1 13.6 %collective-permute-start.6 = (f32[8,128,128]{2,1,0:T(8,128)S(1)}, f32[8,128,128]{2,1,0:T(8,128)S(1)}, u32[]{:S(2)}, u32[]{:S(2)}) collective-permute-start(f32[8,128,128]{2,1,0:T(8,128)S(1)} %collective-permute-done.4.refs_6_), channel_id=1, source_target_pairs={{0,4},{4,8},{8,12},{12,16},{16,20},{20,24},{24,28},{6,2},{10,6},{1... | collective-permute-start | bytes 1572872 | tf_op jit(solution)/shard_map/ppermute | solution.py:341
  34.8 16.7 %collective-permute-start.8 = (f32[9,128,128]{2,1,0:T(8,128)S(1)}, f32[9,128,128]{2,1,0:T(8,128)S(1)}, u32[]{:S(2)}, u32[]{:S(2)}) collective-permute-start(f32[9,128,128]{2,1,0:T(8,128)S(1)} %get-tuple-element.47), channel_id=1, source_target_pairs={{0,2},{2,0},{4,6},{6,4},{8,10},{10,8},{12,14},{14,12},{16,18},{18,... | collective-permute-start | bytes 1769480 | tf_op jit(solution)/shard_map/ppermute | solution.py:338
  39.1 8.2 %copy-start.4 = (f32[7,128,128]{2,1,0:T(8,128)}, f32[7,128,128]{2,1,0:T(8,128)S(1)}, u32[]{:S(2)}) copy-start(f32[7,128,128]{2,1,0:T(8,128)S(1)} %collective-permute-done.1.refs_0_.refs_3_) | copy-start | bytes 1376260
  39.1 16.1 %collective-permute-start.9 = (f32[7,128,128]{2,1,0:T(8,128)S(1)}, f32[7,128,128]{2,1,0:T(8,128)S(1)}, u32[]{:S(2)}, u32[]{:S(2)}) collective-permute-start(f32[7,128,128]{2,1,0:T(8,128)S(1)} %collective-permute-done.1.refs_0_.refs_3_), channel_id=1, source_target_pairs={{0,4},{4,8},{8,12},{12,16},{16,20},{20,24},{24,28},{6,2},{10,6},{1... | collective-permute-start | bytes 1376264 | tf_op jit(solution)/shard_map/ppermute | solution.py:341
  47.3 18.7 %collective-permute-start.7 = (f32[2,4,128,128]{3,2,1,0:T(8,128)S(1)}, f32[2,4,128,128]{3,2,1,0:T(8,128)S(1)}, u32[]{:S(2)}, u32[]{:S(2)}) collective-permute-start(f32[2,4,128,128]{3,2,1,0:T(8,128)S(1)} %get-tuple-element.45), channel_id=1, source_target_pairs={{0,1},{1,0},{2,3},{3,2},{4,5},{5,4},{6,7},{7,6},{8,9},{9,8},{10,11... | collective-permute-start | bytes 1572872 | tf_op jit(solution)/shard_map/ppermute | solution.py:335
  51.5 3.8 %copy-start.2 = (f32[9,128,128]{2,1,0:T(8,128)}, f32[9,128,128]{2,1,0:T(8,128)S(1)}, u32[]{:S(2)}) copy-start(f32[9,128,128]{2,1,0:T(8,128)S(1)} %collective-permute-done.8.refs_1_.refs_4_) | copy-start | bytes 1769476
  51.5 9.7 %collective-permute-start.11 = (f32[5,128,128]{2,1,0:T(8,128)S(1)}, f32[5,128,128]{2,1,0:T(8,128)S(1)}, u32[]{:S(2)}, u32[]{:S(2)}) collective-permute-start(f32[5,128,128]{2,1,0:T(8,128)S(1)} %slice.9), channel_id=1, source_target_pairs={{0,4},{4,8},{8,12},{12,16},{16,20},{20,24},{24,28},{6,2},{10,6},{1... | collective-permute-start | bytes 983048 | tf_op jit(solution)/shard_map/ppermute | solution.py:341
  57.5 8.6 %collective-permute-start.10 = (f32[2,2,128,128]{3,2,1,0:T(8,128)S(1)}, f32[2,2,128,128]{3,2,1,0:T(8,128)S(1)}, u32[]{:S(2)}, u32[]{:S(2)}) collective-permute-start(f32[2,2,128,128]{3,2,1,0:T(8,128)S(1)} %shard_map.68), channel_id=1, source_target_pairs={{0,1},{1,0},{2,3},{3,2},{4,5},{5,4},{6,7},{7,6},{8,9},{9,8},{10,11... | collective-permute-start | bytes 786440 | tf_op jit(solution)/shard_map/ppermute | solution.py:335
  60.4 5.6 %copy-start.1 = (s32[2,1,8]{2,1,0:T(1,128)S(1)}, s32[2,1,8]{2,1,0:T(1,128)}, u32[]{:S(2)}) copy-start(s32[2,1,8]{2,1,0:T(1,128)} %refs_0_.5) | copy-start | bytes 196
  63.4 9.1 %collective-permute-start.12 = (f32[2,2,128,128]{3,2,1,0:T(8,128)S(1)}, f32[2,2,128,128]{3,2,1,0:T(8,128)S(1)}, u32[]{:S(2)}, u32[]{:S(2)}) collective-permute-start(f32[2,2,128,128]{3,2,1,0:T(8,128)S(1)} %shard_map.71), channel_id=1, source_target_pairs={{0,1},{1,0},{2,3},{3,2},{4,5},{5,4},{6,7},{7,6},{8,9},{9,8},{10,11... | collective-permute-start | bytes 786440 | tf_op jit(solution)/shard_map/ppermute | solution.py:335

commit v5 on v4

--- a/solution.py
+++ b/solution.py
@@ -144,7 +144,7 @@
 
 
 def gather_next(even, packed, stage, sem):
-    return start(packed.at[pl.ds(0, 7)], stage.at[pl.ds(jnp.where(even, 1, 16), 7)], sem)
+    return start(packed, stage.at[pl.ds(jnp.where(even, 1, 16), 7)], sem)
 
 
 def product_own(size, where, u_any, p_mask_any, p_any, pe_z, pe_y, pc, pc_y, *refs):
@@ -364,8 +364,8 @@
     )(u_mask, u_values)
     u_oth = over_layer(after(u_own, pc))
     pe_z = onto(after(pe_y[:7], u_own))
-    pc_y = over_pair(pc)
-    pc_z = onto(pc_y)
+    pc_y = over_pair(after(pc, u_own))
+    pc_z = onto(pc_y[:7])
     t_like = (4, size, 4 * size)
     band = [vmem(wide, wide, dtype=BF16)] * 2
     own_rows = [vmem(4 * size, wide, dtype=BF16)] * 2
@@ -375,7 +375,7 @@
         [HBM, HBM, HBM, ANY] + [HBM] * 3,
         [pltpu.SMEM(p_mask.shape, jnp.int32), vmem(*p_values.shape)]
         + [vmem(2, 24, size, size), vmem(4, 4, size, size), *band, sems(10)],
-        flops=4 * unit,
+        flops=40 * unit,
     )(u_own, p_mask, p_values, pe_z, pe_y, pc, pc_y)
     u_y = [over_pair(after(x, pc)) for x in packed]
     u_z = [onto(after(u_y[0], t_own))]

time: 74.2 us -> 73 us (0.984)
  waiting for transfers between devices: 22.9 us -> 21.5 us
    ppermute x4, starting transfers between devices: 16.5 us -> 14.4 us  [onto(): return lax.ppermute(x, SLABS, onward)]
    ppermute x4, starting transfers between devices: 3.43 us -> 5.31 us  [over_pair(): return lax.ppermute(x, SLABS, pair)]
    ppermute x4, waiting for transfers between devices: 0.85 us -> 0.01 us  [onto(): return lax.ppermute(x, SLABS, onward)]
where the time goes in v5:
time: 73 us; the launch traced here: 72.5 us
  starting transfers between devices  29 us (40%)
  Pallas kernels  21.6 us (30%)
  waiting for transfers between devices  21.5 us (29%)
    pallas_call x9, Pallas kernels, run(): pl.pallas_call(kernel, out_shape=outs, in_specs=[ANY if spec is HBM else...  21.6 us
    ppermute x4, starting transfers between devices, onto(): return lax.ppermute(x, SLABS, onward)  14.4 us
    ppermute x4, waiting for transfers between devices, over_pair(): return lax.ppermute(x, SLABS, pair)  10.9 us
    ppermute x5, waiting for transfers between devices, over_layer(): return lax.ppermute(x, 'layer', swap)  10.6 us
    ppermute x5, starting transfers between devices, over_layer(): return lax.ppermute(x, 'layer', swap)  9.21 us
    ppermute x4, starting transfers between devices, over_pair(): return lax.ppermute(x, SLABS, pair)  5.31 us
  transfers between devices with their start and end apart: 13, of which 7 were waited for; matrix products, arithmetic and copies ran while one was open for 0% of the time, Pallas kernels for 26%

profile of v5, /device:TPU:0, one launch (start us, length us, event | category | flops | bytes accessed | tf_op | source)
XLA Modules:
  0.0 72.5 jit_solution(6195149395837990184)
XLA Ops:
  0.0 1.3 %shard_map.65 = (f32[8,128,128]{2,1,0:T(8,128)S(1)}, f32[8,128,128]{2,1,0:T(8,128)S(1)}) custom-call(s32[2,1,8]{2,1,0:T(1,128)} %refs_1_.5, f32[2,1,8,128,128]{4,3,2,1,0:T(8,128)} %refs_2_.1), custom_call_target="tpu_custom_call" | custom-call | tf_op jit(solution)/shard_map/pallas_call | solution.py:42
  1.3 3.0 %collective-permute-start = (f32[8,128,128]{2,1,0:T(8,128)S(1)}, f32[8,128,128]{2,1,0:T(8,128)S(1)}, u32[]{:S(2)}, u32[]{:S(2)}) collective-permute-start(f32[8,128,128]{2,1,0:T(8,128)S(1)} %get-tuple-element.34), channel_id=1, source_target_pairs={{0,1},{1,0},{2,3},{3,2},{4,5},{5,4},{6,7},{7,6},{8,9},{9,8},{10,11... | collective-permute-start | bytes 1572872 | tf_op jit(solution)/shard_map/ppermute | solution.py:335
  4.3 1.5 %collective-permute-start.2 = (f32[8,128,128]{2,1,0:T(8,128)S(1)}, f32[8,128,128]{2,1,0:T(8,128)S(1)}, u32[]{:S(2)}, u32[]{:S(2)}) collective-permute-start(f32[8,128,128]{2,1,0:T(8,128)S(1)} %get-tuple-element.38), channel_id=1, source_target_pairs={{0,2},{2,0},{4,6},{6,4},{8,10},{10,8},{12,14},{14,12},{16,18},{18,... | collective-permute-start | bytes 1572872 | tf_op jit(solution)/shard_map/ppermute | solution.py:338
  5.8 1.8 %shard_map.64 = (f32[4,4,128,128]{3,2,1,0:T(8,128)S(1)}, f32[7,128,128]{2,1,0:T(8,128)S(1)}, f32[9,128,128]{2,1,0:T(8,128)S(1)}) custom-call(s32[4,4]{1,0:T(4,128)} %bitcast.4, f32[4,4,1,128,128]{4,3,2,1,0:T(8,128)} %refs_1_.3), custom_call_target="tpu_custom_call" | custom-call | tf_op jit(solution)/shard_map/pallas_call | solution.py:42
  7.6 0.0 copy-start.1
  7.6 8.6 %collective-permute-done.refs_5_ = f32[8,128,128]{2,1,0:T(8,128)S(1)} collective-permute-done((f32[8,128,128]{2,1,0:T(8,128)S(1)}, f32[8,128,128]{2,1,0:T(8,128)S(1)}, u32[]{:S(2)}, u32[]{:S(2)}) %collective-permute-start) | collective-permute-done | bytes 524320 | tf_op jit(solution)/shard_map/ppermute | solution.py:335
  16.2 0.0 copy-start.6
  16.2 1.8 %collective-permute-start.4 = (f32[8,128,128]{2,1,0:T(8,128)S(1)}, f32[8,128,128]{2,1,0:T(8,128)S(1)}, u32[]{:S(2)}, u32[]{:S(2)}) collective-permute-start(f32[8,128,128]{2,1,0:T(8,128)S(1)} %collective-permute-done.refs_5_), channel_id=1, source_target_pairs={{0,2},{2,0},{4,6},{6,4},{8,10},{10,8},{12,14},{14,12},{16,18},{18,... | collective-permute-start | bytes 1572872 | tf_op jit(solution)/shard_map/ppermute | solution.py:338
  18.0 0.0 collective-permute-done.2.refs_4_
  18.0 0.0 copy-start.4
  18.0 3.5 %collective-permute-start.3 = (f32[7,128,128]{2,1,0:T(8,128)S(1)}, f32[7,128,128]{2,1,0:T(8,128)S(1)}, u32[]{:S(2)}, u32[]{:S(2)}) collective-permute-start(f32[7,128,128]{2,1,0:T(8,128)S(1)} %slice.12), channel_id=1, source_target_pairs={{0,4},{4,8},{8,12},{12,16},{16,20},{20,24},{24,28},{6,2},{10,6},{1... | collective-permute-start | bytes 1376264 | tf_op jit(solution)/shard_map/ppermute | solution.py:341
  21.5 1.6 %collective-permute-start.5 = (f32[4,4,128,128]{3,2,1,0:T(8,128)S(1)}, f32[4,4,128,128]{3,2,1,0:T(8,128)S(1)}, u32[]{:S(2)}, u32[]{:S(2)}) collective-permute-start(f32[4,4,128,128]{3,2,1,0:T(8,128)S(1)} %get-tuple-element.46.refs_0_), channel_id=1, source_target_pairs={{0,1},{1,0},{2,3},{3,2},{4,5},{5,4},{6,7},{7,6},{8,9},{9,8},{10,11... | collective-permute-start | bytes 3145736 | tf_op jit(solution)/shard_map/ppermute | solution.py:335
  23.1 0.0 collective-permute-start.1
  23.1 2.0 %collective-permute-start.8 = (f32[9,128,128]{2,1,0:T(8,128)S(1)}, f32[9,128,128]{2,1,0:T(8,128)S(1)}, u32[]{:S(2)}, u32[]{:S(2)}) collective-permute-start(f32[9,128,128]{2,1,0:T(8,128)S(1)} %get-tuple-element.49), channel_id=1, source_target_pairs={{0,2},{2,0},{4,6},{6,4},{8,10},{10,8},{12,14},{14,12},{16,18},{18,... | collective-permute-start | bytes 1769480 | tf_op jit(solution)/shard_map/ppermute | solution.py:338
  25.1 6.0 %collective-permute-done.4.refs_6_ = f32[8,128,128]{2,1,0:T(8,128)S(1)} collective-permute-done((f32[8,128,128]{2,1,0:T(8,128)S(1)}, f32[8,128,128]{2,1,0:T(8,128)S(1)}, u32[]{:S(2)}, u32[]{:S(2)}) %collective-permute-start.4) | collective-permute-done | bytes 524320 | tf_op jit(solution)/shard_map/ppermute | solution.py:338
  31.1 0.0 copy-start.5
  31.1 3.8 %collective-permute-start.6 = (f32[7,128,128]{2,1,0:T(8,128)S(1)}, f32[7,128,128]{2,1,0:T(8,128)S(1)}, u32[]{:S(2)}, u32[]{:S(2)}) collective-permute-start(f32[7,128,128]{2,1,0:T(8,128)S(1)} %slice.13), channel_id=1, source_target_pairs={{0,4},{4,8},{8,12},{12,16},{16,20},{20,24},{24,28},{6,2},{10,6},{1... | collective-permute-start | bytes 1376264 | tf_op jit(solution)/shard_map/ppermute | solution.py:341
  34.9 0.0 collective-permute-done.3.refs_3_
  34.9 0.0 copy-done.1
  34.9 0.0 copy-done.6
  34.9 0.0 copy-done.4
  34.9 0.0 copy-done.5
  34.9 3.6 %shard_map.66 = (f32[4,128,512]{2,1,0:T(8,128)S(1)}, bf16[512,768]{1,0:T(8,128)(2,1)S(1)}, bf16[512,768]{1,0:T(8,128)(2,1)S(1)}, bf16[768,768]{1,0:T(8,128)(2,1)S(1)}, bf16[768,768]{1,0:T(8,128)(2,1)S(1)}) custom-call(f32[4,4,128,128]{3,2,1,0:T(8,128)} %copy-done.1, s32[2,1,8]{2,1,0:T(1,128)} %refs_1_.5, f32[2,1,8,128,128]{4,3,2,1,0:T(8,128)} %refs_2_.1, ...), custom_call_target="tpu_custom_call" | custom-call | flops 8053063680 | tf_op jit(solution)/shard_map/pallas_call | solution.py:42
  38.5 2.4 %collective-permute-done.1.refs_0_.refs_3_ = f32[7,128,128]{2,1,0:T(8,128)S(1)} collective-permute-done((f32[7,128,128]{2,1,0:T(8,128)S(1)}, f32[7,128,128]{2,1,0:T(8,128)S(1)}, u32[]{:S(2)}, u32[]{:S(2)}) %collective-permute-start.1) | collective-permute-done | bytes 458784 | tf_op jit(solution)/shard_map/ppermute | solution.py:338
  40.9 0.0 copy-start.3
  40.9 3.7 %collective-permute-start.9 = (f32[7,128,128]{2,1,0:T(8,128)S(1)}, f32[7,128,128]{2,1,0:T(8,128)S(1)}, u32[]{:S(2)}, u32[]{:S(2)}) collective-permute-start(f32[7,128,128]{2,1,0:T(8,128)S(1)} %collective-permute-done.1.refs_0_.refs_3_), channel_id=1, source_target_pairs={{0,4},{4,8},{8,12},{12,16},{16,20},{20,24},{24,28},{6,2},{10,6},{1... | collective-permute-start | bytes 1376264 | tf_op jit(solution)/shard_map/ppermute | solution.py:341
  44.7 0.0 collective-permute-done.6.refs_7_
  44.7 0.4 collective-permute-done.5.refs_6_.refs_4_
  45.0 2.6 %shard_map.67 = (bf16[2,128,512]{2,1,0:T(8,128)(2,1)S(1)}, bf16[2,128,512]{2,1,0:T(8,128)(2,1)S(1)}, f32[2,4,128,128]{3,2,1,0:T(8,128)S(1)}, bf16[768,768]{1,0:T(8,128)(2,1)S(1)}, bf16[768,768]{1,0:T(8,128)(2,1)S(1)}) custom-call(s32[4,4]{1,0:T(4,128)} %bitcast.2, ...), custom_call_target="tpu_custom_call", output_to_operand_aliasing={{3}: (4, {}), {4}: (5, {})} | custom-call | flops 805306368 | tf_op jit(solution)/shard_map/pallas_call | solution.py:42
  47.7 0.0 copy-done.3
  47.7 1.6 %collective-permute-start.7 = (f32[2,4,128,128]{3,2,1,0:T(8,128)S(1)}, f32[2,4,128,128]{3,2,1,0:T(8,128)S(1)}, u32[]{:S(2)}, u32[]{:S(2)}) collective-permute-start(f32[2,4,128,128]{3,2,1,0:T(8,128)S(1)} %get-tuple-element.47), channel_id=1, source_target_pairs={{0,1},{1,0},{2,3},{3,2},{4,5},{5,4},{6,7},{7,6},{8,9},{9,8},{10,11... | collective-permute-start | bytes 1572872 | tf_op jit(solution)/shard_map/ppermute | solution.py:335
  49.2 2.5 %collective-permute-done.8.refs_1_.refs_4_ = f32[9,128,128]{2,1,0:T(8,128)S(1)} collective-permute-done((f32[9,128,128]{2,1,0:T(8,128)S(1)}, f32[9,128,128]{2,1,0:T(8,128)S(1)}, u32[]{:S(2)}, u32[]{:S(2)}) %collective-permute-start.8) | collective-permute-done | bytes 589856 | tf_op jit(solution)/shard_map/ppermute | solution.py:338
  51.8 3.4 %collective-permute-start.11 = (f32[5,128,128]{2,1,0:T(8,128)S(1)}, f32[5,128,128]{2,1,0:T(8,128)S(1)}, u32[]{:S(2)}, u32[]{:S(2)}) collective-permute-start(f32[5,128,128]{2,1,0:T(8,128)S(1)} %slice.14), channel_id=1, source_target_pairs={{0,4},{4,8},{8,12},{12,16},{16,20},{20,24},{24,28},{6,2},{10,6},{1... | collective-permute-start | bytes 983048 | tf_op jit(solution)/shard_map/ppermute | solution.py:341
  55.3 0.0 collective-permute-done.9.refs_2_.refs_5_
  55.3 0.0 copy-done.2
  55.3 2.2 %shard_map.68 = f32[2,2,128,128]{3,2,1,0:T(8,128)S(1)} custom-call(f32[7,128,128]{2,1,0:T(8,128)} %copy-done.3, f32[9,128,128]{2,1,0:T(8,128)} %copy-done.2, f32[7,128,128]{2,1,0:T(8,128)S(1)} %collective-permute-done.9.refs_2_.refs_5_, bf16[2,128,512]{2,1,0:T(8,128)(2,1)S(1)} %get-tuple-element.51.refs_3_.refs_4_, ...), custom_call_target="tpu_custom_call" | custom-call | flops 201326592 | tf_op jit(solution)/shard_map/pallas_call | solution.py:42
  57.5 1.6 %collective-permute-start.10 = (f32[2,2,128,128]{3,2,1,0:T(8,128)S(1)}, f32[2,2,128,128]{3,2,1,0:T(8,128)S(1)}, u32[]{:S(2)}, u32[]{:S(2)}) collective-permute-start(f32[2,2,128,128]{3,2,1,0:T(8,128)S(1)} %shard_map.68), channel_id=1, source_target_pairs={{0,1},{1,0},{2,3},{3,2},{4,5},{5,4},{6,7},{7,6},{8,9},{9,8},{10,11... | collective-permute-start | bytes 786440 | tf_op jit(solution)/shard_map/ppermute | solution.py:335
  59.0 1.4 %shard_map.69 = (bf16[2,128,512]{2,1,0:T(8,128)(2,1)S(1)}, bf16[2,128,512]{2,1,0:T(8,128)(2,1)S(1)}) custom-call(s32[4,4]{1,0:T(4,128)} %bitcast.3, f32[4,128,512]{2,1,0:T(8,128)S(1)} %get-tuple-element.41.refs_1_, bf16[768,768]{1,0:T(8,128)(2,1)S(1)} %get-tuple-element.54.refs_2_, bf16[768,768]{1,0:T(8,128)(2,1)S(1)} %get-tuple-element.55.refs_3_, ...), custom_call_target="tpu_custom_call" | custom-call | flops 402653184 | tf_op jit(solution)/shard_map/pallas_call | solution.py:42
  60.4 0.0 copy-start
  60.4 0.0 collective-permute-done.11.refs_6_.refs_3_
  60.4 2.2 %shard_map.71 = f32[2,2,128,128]{3,2,1,0:T(8,128)S(1)} custom-call(f32[7,128,128]{2,1,0:T(8,128)} %copy-done.3, f32[9,128,128]{2,1,0:T(8,128)} %copy-done.2, f32[7,128,128]{2,1,0:T(8,128)S(1)} %collective-permute-done.9.refs_2_.refs_5_, f32[5,128,128]{2,1,0:T(8,128)S(1)} %collective-permute-done.11.refs_6_.refs_3_, ...), custom_call_target="tpu_custom_call" | custom-call | flops 201326592 | tf_op jit(solution)/shard_map/pallas_call | solution.py:42
  62.6 1.5 %collective-permute-start.12 = (f32[2,2,128,128]{3,2,1,0:T(8,128)S(1)}, f32[2,2,128,128]{3,2,1,0:T(8,128)S(1)}, u32[]{:S(2)}, u32[]{:S(2)}) collective-permute-start(f32[2,2,128,128]{3,2,1,0:T(8,128)S(1)} %shard_map.71), channel_id=1, source_target_pairs={{0,1},{1,0},{2,3},{3,2},{4,5},{5,4},{6,7},{7,6},{8,9},{9,8},{10,11... | collective-permute-start | bytes 786440 | tf_op jit(solution)/shard_map/ppermute | solution.py:335
  64.1 1.2 %collective-permute-done.10.refs_2_ = f32[2,2,128,128]{3,2,1,0:T(8,128)S(1)} collective-permute-done((f32[2,2,128,128]{3,2,1,0:T(8,128)S(1)}, f32[2,2,128,128]{3,2,1,0:T(8,128)S(1)}, u32[]{:S(2)}, u32[]{:S(2)}) %collective-permute-start.10) | collective-permute-done | bytes 262176 | tf_op jit(solution)/shard_map/ppermute | solution.py:335
  65.3 0.0 collective-permute-done.7.refs_1_
  65.3 0.0 copy-done
  65.3 5.4 %shard_map.70 = (f32[2,1,8,128,128]{4,3,2,1,0:T(8,128)}, f32[2,2,128,128]{3,2,1,0:T(8,128)S(1)}) custom-call(s32[2,1,8]{2,1,0:T(1,128)S(1)} %copy-done, f32[2,4,128,128]{3,2,1,0:T(8,128)S(1)} %collective-permute-done.7.refs_1_, f32[2,2,128,128]{3,2,1,0:T(8,128)S(1)} %collective-permute-done.10.refs_2_, f32[7,128,128]{2,1,0:T(8,128)} %copy-done.3, ...), custom_call_target="tpu_custom_call" | custom-call | flops 8053063680 | tf_op jit(solution)/shard_map/pallas_call | solution.py:42
  70.7 0.5 collective-permute-done.12.refs_2_
  71.1 1.3 %shard_map.72 = f32[2,1,8,128,128]{4,3,2,1,0:T(8,128)} custom-call(s32[2,1,8]{2,1,0:T(1,128)S(1)} %copy-done, f32[2,2,128,128]{3,2,1,0:T(8,128)S(1)} %get-tuple-element.58.refs_1_, f32[2,2,128,128]{3,2,1,0:T(8,128)S(1)} %collective-permute-done.12.refs_2_, f32[2,1,8,128,128]{4,3,2,1,0:T(8,128)} %get-tuple-element.60.refs_3_), custom_call_target="tpu_custom_call", output_to_operand_aliasing={{}: (3, {})} | custom-call | tf_op jit(solution)/shard_map/pallas_call | solution.py:42
  (4 shorter events, 0.1 us)
Async XLA Ops:
  1.3 14.9 %collective-permute-start = (f32[8,128,128]{2,1,0:T(8,128)S(1)}, f32[8,128,128]{2,1,0:T(8,128)S(1)}, u32[]{:S(2)}, u32[]{:S(2)}) collective-permute-start(f32[8,128,128]{2,1,0:T(8,128)S(1)} %get-tuple-element.34), channel_id=1, source_target_pairs={{0,1},{1,0},{2,3},{3,2},{4,5},{5,4},{6,7},{7,6},{8,9},{9,8},{10,11... | collective-permute-start | bytes 1572872 | tf_op jit(solution)/shard_map/ppermute | solution.py:335
  4.3 13.7 %collective-permute-start.2 = (f32[8,128,128]{2,1,0:T(8,128)S(1)}, f32[8,128,128]{2,1,0:T(8,128)S(1)}, u32[]{:S(2)}, u32[]{:S(2)}) collective-permute-start(f32[8,128,128]{2,1,0:T(8,128)S(1)} %get-tuple-element.38), channel_id=1, source_target_pairs={{0,2},{2,0},{4,6},{6,4},{8,10},{10,8},{12,14},{14,12},{16,18},{18,... | collective-permute-start | bytes 1572872 | tf_op jit(solution)/shard_map/ppermute | solution.py:338
  7.6 27.3 %copy-start.1 = (f32[4,4,128,128]{3,2,1,0:T(8,128)}, f32[4,4,128,128]{3,2,1,0:T(8,128)S(1)}, u32[]{:S(2)}) copy-start(f32[4,4,128,128]{3,2,1,0:T(8,128)S(1)} %get-tuple-element.46.refs_0_) | copy-start | bytes 3145732
  16.2 18.7 %copy-start.6 = (f32[8,128,128]{2,1,0:T(8,128)}, f32[8,128,128]{2,1,0:T(8,128)S(1)}, u32[]{:S(2)}) copy-start(f32[8,128,128]{2,1,0:T(8,128)S(1)} %collective-permute-done.refs_5_) | copy-start | bytes 1572868
  16.2 14.9 %collective-permute-start.4 = (f32[8,128,128]{2,1,0:T(8,128)S(1)}, f32[8,128,128]{2,1,0:T(8,128)S(1)}, u32[]{:S(2)}, u32[]{:S(2)}) collective-permute-start(f32[8,128,128]{2,1,0:T(8,128)S(1)} %collective-permute-done.refs_5_), channel_id=1, source_target_pairs={{0,2},{2,0},{4,6},{6,4},{8,10},{10,8},{12,14},{14,12},{16,18},{18,... | collective-permute-start | bytes 1572872 | tf_op jit(solution)/shard_map/ppermute | solution.py:338
  18.0 16.9 %copy-start.4 = (f32[8,128,128]{2,1,0:T(8,128)}, f32[8,128,128]{2,1,0:T(8,128)S(1)}, u32[]{:S(2)}) copy-start(f32[8,128,128]{2,1,0:T(8,128)S(1)} %collective-permute-done.2.refs_4_) | copy-start | bytes 1572868
  18.0 16.9 %collective-permute-start.3 = (f32[7,128,128]{2,1,0:T(8,128)S(1)}, f32[7,128,128]{2,1,0:T(8,128)S(1)}, u32[]{:S(2)}, u32[]{:S(2)}) collective-permute-start(f32[7,128,128]{2,1,0:T(8,128)S(1)} %slice.12), channel_id=1, source_target_pairs={{0,4},{4,8},{8,12},{12,16},{16,20},{20,24},{24,28},{6,2},{10,6},{1... | collective-permute-start | bytes 1376264 | tf_op jit(solution)/shard_map/ppermute | solution.py:341
  21.5 23.5 %collective-permute-start.5 = (f32[4,4,128,128]{3,2,1,0:T(8,128)S(1)}, f32[4,4,128,128]{3,2,1,0:T(8,128)S(1)}, u32[]{:S(2)}, u32[]{:S(2)}) collective-permute-start(f32[4,4,128,128]{3,2,1,0:T(8,128)S(1)} %get-tuple-element.46.refs_0_), channel_id=1, source_target_pairs={{0,1},{1,0},{2,3},{3,2},{4,5},{5,4},{6,7},{7,6},{8,9},{9,8},{10,11... | collective-permute-start | bytes 3145736 | tf_op jit(solution)/shard_map/ppermute | solution.py:335
  23.1 17.8 %collective-permute-start.1 = (f32[7,128,128]{2,1,0:T(8,128)S(1)}, f32[7,128,128]{2,1,0:T(8,128)S(1)}, u32[]{:S(2)}, u32[]{:S(2)}) collective-permute-start(f32[7,128,128]{2,1,0:T(8,128)S(1)} %get-tuple-element.35), channel_id=1, source_target_pairs={{0,2},{2,0},{4,6},{6,4},{8,10},{10,8},{12,14},{14,12},{16,18},{18,... | collective-permute-start | bytes 1376264 | tf_op jit(solution)/shard_map/ppermute | solution.py:338
  23.1 28.7 %collective-permute-start.8 = (f32[9,128,128]{2,1,0:T(8,128)S(1)}, f32[9,128,128]{2,1,0:T(8,128)S(1)}, u32[]{:S(2)}, u32[]{:S(2)}) collective-permute-start(f32[9,128,128]{2,1,0:T(8,128)S(1)} %get-tuple-element.49), channel_id=1, source_target_pairs={{0,2},{2,0},{4,6},{6,4},{8,10},{10,8},{12,14},{14,12},{16,18},{18,... | collective-permute-start | bytes 1769480 | tf_op jit(solution)/shard_map/ppermute | solution.py:338
  31.1 3.8 %copy-start.5 = (f32[8,128,128]{2,1,0:T(8,128)}, f32[8,128,128]{2,1,0:T(8,128)S(1)}, u32[]{:S(2)}) copy-start(f32[8,128,128]{2,1,0:T(8,128)S(1)} %collective-permute-done.4.refs_6_) | copy-start | bytes 1572868
  31.1 13.6 %collective-permute-start.6 = (f32[7,128,128]{2,1,0:T(8,128)S(1)}, f32[7,128,128]{2,1,0:T(8,128)S(1)}, u32[]{:S(2)}, u32[]{:S(2)}) collective-permute-start(f32[7,128,128]{2,1,0:T(8,128)S(1)} %slice.13), channel_id=1, source_target_pairs={{0,4},{4,8},{8,12},{12,16},{16,20},{20,24},{24,28},{6,2},{10,6},{1... | collective-permute-start | bytes 1376264 | tf_op jit(solution)/shard_map/ppermute | solution.py:341
  40.9 6.8 %copy-start.3 = (f32[7,128,128]{2,1,0:T(8,128)}, f32[7,128,128]{2,1,0:T(8,128)S(1)}, u32[]{:S(2)}) copy-start(f32[7,128,128]{2,1,0:T(8,128)S(1)} %collective-permute-done.1.refs_0_.refs_3_) | copy-start | bytes 1376260
  40.9 14.4 %collective-permute-start.9 = (f32[7,128,128]{2,1,0:T(8,128)S(1)}, f32[7,128,128]{2,1,0:T(8,128)S(1)}, u32[]{:S(2)}, u32[]{:S(2)}) collective-permute-start(f32[7,128,128]{2,1,0:T(8,128)S(1)} %collective-permute-done.1.refs_0_.refs_3_), channel_id=1, source_target_pairs={{0,4},{4,8},{8,12},{12,16},{16,20},{20,24},{24,28},{6,2},{10,6},{1... | collective-permute-start | bytes 1376264 | tf_op jit(solution)/shard_map/ppermute | solution.py:341
  47.7 17.6 %collective-permute-start.7 = (f32[2,4,128,128]{3,2,1,0:T(8,128)S(1)}, f32[2,4,128,128]{3,2,1,0:T(8,128)S(1)}, u32[]{:S(2)}, u32[]{:S(2)}) collective-permute-start(f32[2,4,128,128]{3,2,1,0:T(8,128)S(1)} %get-tuple-element.47), channel_id=1, source_target_pairs={{0,1},{1,0},{2,3},{3,2},{4,5},{5,4},{6,7},{7,6},{8,9},{9,8},{10,11... | collective-permute-start | bytes 1572872 | tf_op jit(solution)/shard_map/ppermute | solution.py:335
  51.8 3.5 %copy-start.2 = (f32[9,128,128]{2,1,0:T(8,128)}, f32[9,128,128]{2,1,0:T(8,128)S(1)}, u32[]{:S(2)}) copy-start(f32[9,128,128]{2,1,0:T(8,128)S(1)} %collective-permute-done.8.refs_1_.refs_4_) | copy-start | bytes 1769476
  51.8 8.6 %collective-permute-start.11 = (f32[5,128,128]{2,1,0:T(8,128)S(1)}, f32[5,128,128]{2,1,0:T(8,128)S(1)}, u32[]{:S(2)}, u32[]{:S(2)}) collective-permute-start(f32[5,128,128]{2,1,0:T(8,128)S(1)} %slice.14), channel_id=1, source_target_pairs={{0,4},{4,8},{8,12},{12,16},{16,20},{20,24},{24,28},{6,2},{10,6},{1... | collective-permute-start | bytes 983048 | tf_op jit(solution)/shard_map/ppermute | solution.py:341
  57.5 7.8 %collective-permute-start.10 = (f32[2,2,128,128]{3,2,1,0:T(8,128)S(1)}, f32[2,2,128,128]{3,2,1,0:T(8,128)S(1)}, u32[]{:S(2)}, u32[]{:S(2)}) collective-permute-start(f32[2,2,128,128]{3,2,1,0:T(8,128)S(1)} %shard_map.68), channel_id=1, source_target_pairs={{0,1},{1,0},{2,3},{3,2},{4,5},{5,4},{6,7},{7,6},{8,9},{9,8},{10,11... | collective-permute-start | bytes 786440 | tf_op jit(solution)/shard_map/ppermute | solution.py:335
  60.4 4.9 %copy-start = (s32[2,1,8]{2,1,0:T(1,128)S(1)}, s32[2,1,8]{2,1,0:T(1,128)}, u32[]{:S(2)}) copy-start(s32[2,1,8]{2,1,0:T(1,128)} %refs_0_.5) | copy-start | bytes 196
  62.6 8.6 %collective-permute-start.12 = (f32[2,2,128,128]{3,2,1,0:T(8,128)S(1)}, f32[2,2,128,128]{3,2,1,0:T(8,128)S(1)}, u32[]{:S(2)}, u32[]{:S(2)}) collective-permute-start(f32[2,2,128,128]{3,2,1,0:T(8,128)S(1)} %shard_map.71), channel_id=1, source_target_pairs={{0,1},{1,0},{2,3},{3,2},{4,5},{5,4},{6,7},{7,6},{8,9},{9,8},{10,11... | collective-permute-start | bytes 786440 | tf_op jit(solution)/shard_map/ppermute | solution.py:335

commit v6 on v5

--- a/solution.py
+++ b/solution.py
@@ -121,13 +121,13 @@
         c.wait()
 
 
-def fill_band(size, stage, hi_ref, lo_ref, shift, rows):
+def fill_band(size, stage, hi_ref, lo_ref, shift, rows, first=0):
     for a in rows:
         for c in range(6):
             e = c - a - shift
             at = (pl.ds(a * size, size), pl.ds(c * size, size))
             if 0 <= e < 4:
-                hi_ref[at], lo_ref[at] = halves(stage[4 * a + e])
+                hi_ref[at], lo_ref[at] = halves(stage[4 * a + e - first])
             else:
                 hi_ref[at] = jnp.zeros((size, size), BF16)
                 lo_ref[at] = jnp.zeros((size, size), BF16)
@@ -198,22 +198,17 @@
 
 
 def product_send(total_rows, size, where, t_mask_any, t_own, ud_hi, ud_lo, hi_in, lo_in, u_cross, pc_z, *refs):
-    t_hi, t_lo, ss, hi, lo, t_mask, stage, u_oth, sems = refs
+    t_hi, t_lo, ss, hi, lo, t_mask, sem = refs
     even, layer = where[0] % 2 == 0, where[1]
-    z_copy = gather_next(even, pc_z, stage, sems.at[1])
-    x_copies = [start(u_cross.at[2 * q + 1 - layer], u_oth.at[2 * q + 1 - layer], sems.at[3 * q]) for q in range(2)]
-    mask_copy = start(t_mask_any, t_mask, sems.at[2])
-    z_copy.wait()
-    for case, rows in ((even, (0, 1)), (jnp.logical_not(even), (4, 5))):
+    mask_copy = start(t_mask_any, t_mask, sem)
+    for case, rows, first in ((even, (0, 1), 1), (jnp.logical_not(even), (4, 5), 16)):
 
         @pl.when(case)
-        def _(rows=rows):
-            fill_band(size, stage, hi, lo, -1, rows)
+        def _(rows=rows, first=first):
+            fill_band(size, pc_z, hi, lo, -1, rows, first)
 
     mask_copy.wait()
-    for c in x_copies:
-        c.wait()
-    product_rows(total_rows, size, where, True, t_mask, t_own, u_oth, hi, lo, t_hi, t_lo)
+    product_rows(total_rows, size, where, True, t_mask, t_own, u_cross, hi, lo, t_hi, t_lo)
     for q in range(2):
         cols = pl.ds(aligned(q + 1 - layer, size), 4 * size)
         sums = dot3((t_hi[q], t_lo[q]), (ud_hi[:, cols], ud_lo[:, cols]), 1)
@@ -221,31 +216,25 @@
             ss[q, r] = sums[:, r * size : (r + 1) * size]
 
 
-def product_keep(total_rows, size, where, t_mask_any, t_own, hi, lo, u_cross, t_hi, t_lo, t_mask, u_oth, sems):
-    layer = where[1]
-    copies = [start(u_cross.at[2 * q + layer], u_oth.at[2 * q + layer], sems.at[q]) for q in range(2)]
-    copies.append(start(t_mask_any, t_mask, sems.at[2]))
-    for c in copies:
-        c.wait()
-    product_rows(total_rows, size, where, False, t_mask, t_own, u_oth, hi, lo, t_hi, t_lo)
-
-
-def gather_halo(u_y, u_z, stage, sems):
+def product_keep(total_rows, size, where, t_mask_any, t_own, hi, lo, u_cross, t_hi, t_lo, t_mask, sem):
+    start(t_mask_any, t_mask, sem).wait()
+    product_rows(total_rows, size, where, False, t_mask, t_own, u_cross, hi, lo, t_hi, t_lo)
+
+
+def gather_halo(pieces, stage, sems):
     spots = [stage.at[pl.ds(at, n)] for at, n in (*PARTS, (16, 7), (23, 5))]
-    return [start(src, spot, sems.at[n]) for n, (src, spot) in enumerate(zip([*u_y, *u_z], spots))]
-
-
-def fill_halo(size, where, stage, uh_hi, uh_lo, rows=(0, 1, 2, 3)):
+    return [start(x, spot, sems.at[n]) for n, (x, spot) in enumerate(zip(pieces, spots)) if x is not None]
+
+
+def fill_halo(size, where, stage, uh_hi, uh_lo, rows, blocks):
     even, layer = where[0] % 2 == 0, where[1]
-    uh_hi[...] = jnp.zeros_like(uh_hi)
-    uh_lo[...] = jnp.zeros_like(uh_lo)
     for below_at, above_at, pack, case in ((16, 0, PACK[1], even), (0, 16, PACK[0], jnp.logical_not(even))):
 
         @pl.when(case)
         def _(below_at=below_at, above_at=above_at, pack=pack):
             for first, above in ((below_at, 0), (above_at, 1)):
-                for n, (r, m) in enumerate(pack[: 16 if first == 0 else 12]):
-                    if r not in rows or (above and r == 3):
+                for n, (r, m) in enumerate(pack):
+                    if first + n not in blocks or r not in rows or (above and r == 3):
                         continue
                     at = pl.ds((above * len(rows) + rows.index(r)) * size, size)
                     cols = pl.ds(aligned(slot_base(r, layer) + 4 * above + m, size), size)
@@ -260,17 +249,38 @@
     return dot3(t_rows, (hi, lo), 1)
 
 
-def send_halo(size, ts, where, *refs):
-    u_y, u_z, t_hi, t_lo = refs[0:2], refs[2:-7], refs[-7], refs[-6]
-    out, stage, uh_hi, uh_lo, sems = refs[-5:]
-    layer = where[1]
-    for c in gather_halo(u_y, u_z, stage, sems):
-        c.wait()
-    fill_halo(size, where, stage, uh_hi, uh_lo, ts)
+def send_sums(size, ts, where, t_hi, t_lo, uh_hi, uh_lo, out):
     for q in range(2):
-        sums = halo_sums(size, 2 * q + 1 - layer, q + 1 - layer, (t_hi[q], t_lo[q]), uh_hi, uh_lo, ts)
+        i, base = 2 * q + 1 - where[1], q + 1 - where[1]
+        sums = halo_sums(size, i, base, (t_hi[q], t_lo[q]), uh_hi, uh_lo, ts)
         for n in range(len(ts)):
             out[q, n] = sums[:, n * size : (n + 1) * size]
+
+
+def first_halo(size, where, y0, y1, z0, t_hi, t_lo, out, uh_hi, uh_lo, stage, sems):
+    copies = gather_halo((y0, y1, z0), stage, sems)
+    uh_hi[...] = jnp.zeros_like(uh_hi)
+    uh_lo[...] = jnp.zeros_like(uh_lo)
+    for c in copies:
+        c.wait()
+    fill_halo(size, where, stage, uh_hi, uh_lo, (0, 1), range(23))
+    send_sums(size, (0, 1), where, t_hi, t_lo, uh_hi, uh_lo, out)
+
+
+def halo_matrix(size, where, y0, y1, z0, uh_hi, uh_lo, stage, sems):
+    copies = gather_halo((y0, y1, z0), stage, sems)
+    uh_hi[...] = jnp.zeros_like(uh_hi)
+    uh_lo[...] = jnp.zeros_like(uh_lo)
+    for c in copies:
+        c.wait()
+    fill_halo(size, where, stage, uh_hi, uh_lo, (2, 3), range(23))
+
+
+def last_halo(size, where, z1, t_hi, t_lo, hi_in, lo_in, out, uh_hi, uh_lo, stage, sems):
+    for c in gather_halo((None, None, None, z1), stage, sems):
+        c.wait()
+    fill_halo(size, where, stage, uh_hi, uh_lo, (2, 3), range(23, 28))
+    send_sums(size, (2, 3), where, t_hi, t_lo, uh_hi, uh_lo, out)
 
 
 def out_keep(total_rows, where, o_mask, q, o):
@@ -279,31 +289,27 @@
 
 
 def keep_rows(total_rows, size, where, o_mask, ss, halo, *refs):
-    u_y, u_z, t_hi, t_lo, ud_hi, ud_lo = refs[0:2], refs[2:4], *refs[4:8]
-    out_any, part, out, stage, uh_hi, uh_lo, sems = refs[8:]
-    for c in gather_halo(u_y, u_z, stage, sems):
-        c.wait()
-    fill_halo(size, where, stage, uh_hi, uh_lo)
+    (t_hi, t_lo), (ud_hi, ud_lo), first, last = (refs[2 * n : 2 * n + 2] for n in range(4))
+    out_any, part, out, sems = refs[8:]
     stores = []
     for q in range(2):
         i = 2 * q + where[1]
-        sums = halo_sums(size, i, q, (t_hi[q], t_lo[q]), uh_hi, uh_lo)
-        for t in range(4):
-            o = (8 - i + t) % 8
+        t_rows = (t_hi[q], t_lo[q])
+        cols = pl.ds(q * size, 4 * size)
+        own = dot3(t_rows, (ud_hi[:, cols], ud_lo[:, cols]), 1)
+        near = halo_sums(size, i, q, t_rows, *first, (0, 1))
+        for n in range(6):
+            o = (4 - i + n) % 8
             keep = out_keep(total_rows, where, o_mask, q, o)
-            value = sums[:, t * size : (t + 1) * size]
-            if t < 2:
-                out[q, 4 + t] = (value + halo[q, t]) * keep
-                stores.append(start(out.at[q, 4 + t], out_any.at[q, 0, o], sems.at[4 + 2 * q + t]))
+            if n < 4:
+                out[q, n] = (own[:, n * size : (n + 1) * size] + ss[q, n]) * keep
             else:
-                part[q, t - 2] = value * keep
-        cols = pl.ds(q * size, 4 * size)
-        sums = dot3((t_hi[q], t_lo[q]), (ud_hi[:, cols], ud_lo[:, cols]), 1)
-        for r in range(4):
-            o = (4 - i + r) % 8
-            keep = out_keep(total_rows, where, o_mask, q, o)
-            out[q, r] = (sums[:, r * size : (r + 1) * size] + ss[q, r]) * keep
-            stores.append(start(out.at[q, r], out_any.at[q, 0, o], sems.at[8 + 4 * q + r]))
+                out[q, n] = (near[:, (n - 4) * size : (n - 3) * size] + halo[q, n - 4]) * keep
+            stores.append(start(out.at[q, n], out_any.at[q, 0, o], sems.at[6 * q + n]))
+        sums = halo_sums(size, i, q, t_rows, *last, (2, 3))
+        for n in range(2):
+            keep = out_keep(total_rows, where, o_mask, q, (10 - i + n) % 8)
+            part[q, n] = sums[:, n * size : (n + 1) * size] * keep
     for c in stores:
         c.wait()
 
@@ -385,8 +391,8 @@
     *t_send, ss, hi, lo = call(
         functools.partial(product_send, total_rows, size),
         [*rows, vmem(2, 4, size, size), *band],
-        [HBM] + [VMEM] * 5 + [ANY] * 2,
-        [masks, vmem(24, size, size), vmem(4, 4, size, size), sems(4)],
+        [HBM] + [VMEM] * 7,
+        [masks, pltpu.SemaphoreType.DMA],
         flops=4 * unit,
         alias={4: 3, 5: 4},
     )(t_mask, t_own, ud_hi, ud_lo, *oth, u_oth, pc_z)
@@ -394,31 +400,41 @@
     t_keep = call(
         functools.partial(product_keep, total_rows, size),
         rows,
-        [HBM] + [VMEM] * 3 + [ANY],
-        [masks, vmem(4, 4, size, size), sems(3)],
+        [HBM] + [VMEM] * 4,
+        [masks, pltpu.SemaphoreType.DMA],
         flops=2 * unit,
     )(t_mask, t_own, hi, lo, u_oth)
     u_z.append(onto(after(u_y[1][:5], t_send[0])))
-    halos = []
-    halo_scratch = [vmem(28, size, size)] + [vmem(4 * size, 9 * size, dtype=BF16)] * 2 + [sems(4)]
-    for ts in ((0, 1), (2, 3)):
-        nz = 1 if ts[0] == 0 else 2
-        (halo,) = call(
-            functools.partial(send_halo, size, ts),
-            [vmem(2, 2, size, size)],
-            [HBM] * 2 + [ANY] * nz + [VMEM] * 2,
-            halo_scratch,
-            flops=unit,
-        )(*u_y, *u_z[:nz], t_send[0], after(t_send[1], *halos))
-        halos.append(halo)
-    halos = [over_layer(x) for x in halos]
+    uh = [vmem(4 * size, 9 * size, dtype=BF16)] * 2
+    pair_sums = vmem(2, 2, size, size)
+    stage = vmem(28, size, size)
+    halo, *uh_first = call(
+        functools.partial(first_halo, size),
+        [pair_sums, *uh],
+        [HBM, HBM, ANY, VMEM, VMEM],
+        [stage, sems(3)],
+        flops=unit,
+    )(*u_y, u_z[0], *t_send)
+    halo_got = over_layer(halo)
+    uh_last = call(functools.partial(halo_matrix, size), uh, [HBM, HBM, ANY], [stage, sems(3)])(
+        after(u_y[0], halo), u_y[1], u_z[0]
+    )
+    last, *uh_last = call(
+        functools.partial(last_halo, size),
+        [pair_sums, *uh],
+        [ANY] + [VMEM] * 4,
+        [stage, sems(4)],
+        flops=unit,
+        alias={3: 1, 4: 2},
+    )(u_z[1], *t_send, *uh_last)
+    last_got = over_layer(last)
     kept, part = call(
         functools.partial(keep_rows, total_rows, size),
-        [shape(*p_values.shape), vmem(2, 2, size, size)],
-        [SMEM] + [VMEM] * 2 + [HBM] * 2 + [ANY] * 2 + [VMEM] * 4,
-        [vmem(2, 6, size, size), vmem(28, size, size)] + [vmem(8 * size, 9 * size, dtype=BF16)] * 2 + [sems(16)],
+        [shape(*p_values.shape), pair_sums],
+        [SMEM] + [VMEM] * 10,
+        [vmem(2, 6, size, size), sems(12)],
         flops=40 * unit,
-    )(out_mask, ss_got, halos[0], *u_y, *u_z, *t_keep, ud_hi, ud_lo)
+    )(out_mask, ss_got, halo_got, *t_keep, ud_hi, ud_lo, *uh_first, *uh_last)
     (out,) = call(
         functools.partial(combine, total_rows),
         [shape(*p_values.shape)],
@@ -426,7 +442,7 @@
         [vmem(2, 2, size, size), sems(4)],
         alias={3: 0},
         limit=16,
-    )(out_mask, part, halos[1], kept)
+    )(out_mask, part, last_got, kept)
     return out
 
 

time: 73 us -> 72.9 us (level)
  waiting for transfers between devices: 21.5 us -> 25 us
  Pallas kernels: 21.6 us -> 19.2 us
  starting transfers between devices: 29 us -> 28 us
    ppermute x5, waiting for transfers between devices: 10.6 us -> 13.7 us  [over_layer(): return lax.ppermute(x, 'layer', swap)]
    pallas_call x9 -> x10, Pallas kernels: 21.6 us -> 19.2 us  [run(): pl.pallas_call(kernel, out_shape=outs, in_specs=[ANY if spec is HBM else...]
    ppermute x5, starting transfers between devices: 9.21 us -> 8.28 us  [over_layer(): return lax.ppermute(x, 'layer', swap)]
  transfers between devices with their start and end apart: 13 -> 13, of which waited for: 7 -> 7; matrix products, arithmetic and copies ran while one was open for 0% -> 0% of each run, Pallas kernels for 26% -> 23%
where the time goes in v6:
time: 72.9 us; the launch traced here: 72.5 us
  starting transfers between devices  28 us (38%)
  waiting for transfers between devices  25 us (34%)
  Pallas kernels  19.2 us (26%)
    pallas_call x10, Pallas kernels, run(): pl.pallas_call(kernel, out_shape=outs, in_specs=[ANY if spec is HBM else...  19.2 us
    ppermute x4, starting transfers between devices, onto(): return lax.ppermute(x, SLABS, onward)  14.4 us
    ppermute x5, waiting for transfers between devices, over_layer(): return lax.ppermute(x, 'layer', swap)  13.7 us
    ppermute x4, waiting for transfers between devices, over_pair(): return lax.ppermute(x, SLABS, pair)  11.2 us
    ppermute x5, starting transfers between devices, over_layer(): return lax.ppermute(x, 'layer', swap)  8.28 us
    ppermute x4, starting transfers between devices, over_pair(): return lax.ppermute(x, SLABS, pair)  5.31 us
  transfers between devices with their start and end apart: 13, of which 7 were waited for; matrix products, arithmetic and copies ran while one was open for 0% of the time, Pallas kernels for 23%

profile of v6, /device:TPU:0, one launch (start us, length us, event | category | flops | bytes accessed | tf_op | source)
XLA Modules:
  0.0 72.5 jit_solution(1372673921810755988)
XLA Ops:
  0.0 1.3 %shard_map.65 = (f32[8,128,128]{2,1,0:T(8,128)S(1)}, f32[8,128,128]{2,1,0:T(8,128)S(1)}) custom-call(s32[2,1,8]{2,1,0:T(1,128)} %refs_1_.5, f32[2,1,8,128,128]{4,3,2,1,0:T(8,128)} %refs_2_.1), custom_call_target="tpu_custom_call" | custom-call | tf_op jit(solution)/shard_map/pallas_call | solution.py:42
  1.3 3.0 %collective-permute-start = (f32[8,128,128]{2,1,0:T(8,128)S(1)}, f32[8,128,128]{2,1,0:T(8,128)S(1)}, u32[]{:S(2)}, u32[]{:S(2)}) collective-permute-start(f32[8,128,128]{2,1,0:T(8,128)S(1)} %get-tuple-element.42), channel_id=1, source_target_pairs={{0,1},{1,0},{2,3},{3,2},{4,5},{5,4},{6,7},{7,6},{8,9},{9,8},{10,11... | collective-permute-start | bytes 1572872 | tf_op jit(solution)/shard_map/ppermute | solution.py:341
  4.3 1.5 %collective-permute-start.2 = (f32[8,128,128]{2,1,0:T(8,128)S(1)}, f32[8,128,128]{2,1,0:T(8,128)S(1)}, u32[]{:S(2)}, u32[]{:S(2)}) collective-permute-start(f32[8,128,128]{2,1,0:T(8,128)S(1)} %get-tuple-element.46), channel_id=1, source_target_pairs={{0,2},{2,0},{4,6},{6,4},{8,10},{10,8},{12,14},{14,12},{16,18},{18,... | collective-permute-start | bytes 1572872 | tf_op jit(solution)/shard_map/ppermute | solution.py:344
  5.8 1.8 %shard_map.64 = (f32[4,4,128,128]{3,2,1,0:T(8,128)S(1)}, f32[7,128,128]{2,1,0:T(8,128)S(1)}, f32[9,128,128]{2,1,0:T(8,128)S(1)}) custom-call(s32[4,4]{1,0:T(4,128)} %bitcast.4, f32[4,4,1,128,128]{4,3,2,1,0:T(8,128)} %refs_1_.3), custom_call_target="tpu_custom_call" | custom-call | tf_op jit(solution)/shard_map/pallas_call | solution.py:42
  7.6 0.0 copy-start.1
  7.6 8.6 %collective-permute-done.refs_5_ = f32[8,128,128]{2,1,0:T(8,128)S(1)} collective-permute-done((f32[8,128,128]{2,1,0:T(8,128)S(1)}, f32[8,128,128]{2,1,0:T(8,128)S(1)}, u32[]{:S(2)}, u32[]{:S(2)}) %collective-permute-start) | collective-permute-done | bytes 524320 | tf_op jit(solution)/shard_map/ppermute | solution.py:341
  16.2 0.0 copy-start.6
  16.2 1.8 %collective-permute-start.4 = (f32[8,128,128]{2,1,0:T(8,128)S(1)}, f32[8,128,128]{2,1,0:T(8,128)S(1)}, u32[]{:S(2)}, u32[]{:S(2)}) collective-permute-start(f32[8,128,128]{2,1,0:T(8,128)S(1)} %collective-permute-done.refs_5_), channel_id=1, source_target_pairs={{0,2},{2,0},{4,6},{6,4},{8,10},{10,8},{12,14},{14,12},{16,18},{18,... | collective-permute-start | bytes 1572872 | tf_op jit(solution)/shard_map/ppermute | solution.py:344
  18.0 0.0 collective-permute-done.2.refs_4_
  18.0 0.0 copy-start.4
  18.0 3.5 %collective-permute-start.3 = (f32[7,128,128]{2,1,0:T(8,128)S(1)}, f32[7,128,128]{2,1,0:T(8,128)S(1)}, u32[]{:S(2)}, u32[]{:S(2)}) collective-permute-start(f32[7,128,128]{2,1,0:T(8,128)S(1)} %slice.12), channel_id=1, source_target_pairs={{0,4},{4,8},{8,12},{12,16},{16,20},{20,24},{24,28},{6,2},{10,6},{1... | collective-permute-start | bytes 1376264 | tf_op jit(solution)/shard_map/ppermute | solution.py:347
  21.5 1.6 %collective-permute-start.5 = (f32[4,4,128,128]{3,2,1,0:T(8,128)S(1)}, f32[4,4,128,128]{3,2,1,0:T(8,128)S(1)}, u32[]{:S(2)}, u32[]{:S(2)}) collective-permute-start(f32[4,4,128,128]{3,2,1,0:T(8,128)S(1)} %get-tuple-element.54.refs_0_), channel_id=1, source_target_pairs={{0,1},{1,0},{2,3},{3,2},{4,5},{5,4},{6,7},{7,6},{8,9},{9,8},{10,11... | collective-permute-start | bytes 3145736 | tf_op jit(solution)/shard_map/ppermute | solution.py:341
  23.1 0.0 collective-permute-start.1
  23.1 2.0 %collective-permute-start.8 = (f32[9,128,128]{2,1,0:T(8,128)S(1)}, f32[9,128,128]{2,1,0:T(8,128)S(1)}, u32[]{:S(2)}, u32[]{:S(2)}) collective-permute-start(f32[9,128,128]{2,1,0:T(8,128)S(1)} %get-tuple-element.57), channel_id=1, source_target_pairs={{0,2},{2,0},{4,6},{6,4},{8,10},{10,8},{12,14},{14,12},{16,18},{18,... | collective-permute-start | bytes 1769480 | tf_op jit(solution)/shard_map/ppermute | solution.py:344
  25.1 6.0 %collective-permute-done.4.refs_6_ = f32[8,128,128]{2,1,0:T(8,128)S(1)} collective-permute-done((f32[8,128,128]{2,1,0:T(8,128)S(1)}, f32[8,128,128]{2,1,0:T(8,128)S(1)}, u32[]{:S(2)}, u32[]{:S(2)}) %collective-permute-start.4) | collective-permute-done | bytes 524320 | tf_op jit(solution)/shard_map/ppermute | solution.py:344
  31.1 0.0 copy-start.5
  31.1 3.8 %collective-permute-start.6 = (f32[7,128,128]{2,1,0:T(8,128)S(1)}, f32[7,128,128]{2,1,0:T(8,128)S(1)}, u32[]{:S(2)}, u32[]{:S(2)}) collective-permute-start(f32[7,128,128]{2,1,0:T(8,128)S(1)} %slice.13), channel_id=1, source_target_pairs={{0,4},{4,8},{8,12},{12,16},{16,20},{20,24},{24,28},{6,2},{10,6},{1... | collective-permute-start | bytes 1376264 | tf_op jit(solution)/shard_map/ppermute | solution.py:347
  34.9 0.0 collective-permute-done.3.refs_3_
  34.9 0.0 copy-done.1
  34.9 0.0 copy-done.6
  34.9 0.0 copy-done.4
  34.9 0.0 copy-done.5
  34.9 3.6 %shard_map.66 = (f32[4,128,512]{2,1,0:T(8,128)S(1)}, bf16[512,768]{1,0:T(8,128)(2,1)S(1)}, bf16[512,768]{1,0:T(8,128)(2,1)S(1)}, bf16[768,768]{1,0:T(8,128)(2,1)S(1)}, bf16[768,768]{1,0:T(8,128)(2,1)S(1)}) custom-call(f32[4,4,128,128]{3,2,1,0:T(8,128)} %copy-done.1, s32[2,1,8]{2,1,0:T(1,128)} %refs_1_.5, f32[2,1,8,128,128]{4,3,2,1,0:T(8,128)} %refs_2_.1, ...), custom_call_target="tpu_custom_call" | custom-call | flops 8053063680 | tf_op jit(solution)/shard_map/pallas_call | solution.py:42
  38.5 2.4 %collective-permute-done.1.refs_0_ = f32[7,128,128]{2,1,0:T(8,128)S(1)} collective-permute-done((f32[7,128,128]{2,1,0:T(8,128)S(1)}, f32[7,128,128]{2,1,0:T(8,128)S(1)}, u32[]{:S(2)}, u32[]{:S(2)}) %collective-permute-start.1) | collective-permute-done | bytes 458784 | tf_op jit(solution)/shard_map/ppermute | solution.py:344
  40.9 3.7 %collective-permute-start.9 = (f32[7,128,128]{2,1,0:T(8,128)S(1)}, f32[7,128,128]{2,1,0:T(8,128)S(1)}, u32[]{:S(2)}, u32[]{:S(2)}) collective-permute-start(f32[7,128,128]{2,1,0:T(8,128)S(1)} %collective-permute-done.1.refs_0_), channel_id=1, source_target_pairs={{0,4},{4,8},{8,12},{12,16},{16,20},{20,24},{24,28},{6,2},{10,6},{1... | collective-permute-start | bytes 1376264 | tf_op jit(solution)/shard_map/ppermute | solution.py:347
  44.6 0.0 collective-permute-done.6.refs_7_
  44.7 0.4 collective-permute-done.5.refs_6_.refs_4_
  45.0 2.3 %shard_map.67 = (bf16[2,128,512]{2,1,0:T(8,128)(2,1)S(1)}, bf16[2,128,512]{2,1,0:T(8,128)(2,1)S(1)}, f32[2,4,128,128]{3,2,1,0:T(8,128)S(1)}, bf16[768,768]{1,0:T(8,128)(2,1)S(1)}, bf16[768,768]{1,0:T(8,128)(2,1)S(1)}) custom-call(s32[4,4]{1,0:T(4,128)} %bitcast.2, ...), custom_call_target="tpu_custom_call", output_to_operand_aliasing={{3}: (4, {}), {4}: (5, {})} | custom-call | flops 805306368 | tf_op jit(solution)/shard_map/pallas_call | solution.py:42
  47.3 0.0 copy-done.3
  47.3 1.6 %collective-permute-start.7 = (f32[2,4,128,128]{3,2,1,0:T(8,128)S(1)}, f32[2,4,128,128]{3,2,1,0:T(8,128)S(1)}, u32[]{:S(2)}, u32[]{:S(2)}) collective-permute-start(f32[2,4,128,128]{3,2,1,0:T(8,128)S(1)} %get-tuple-element.55), channel_id=1, source_target_pairs={{0,1},{1,0},{2,3},{3,2},{4,5},{5,4},{6,7},{7,6},{8,9},{9,8},{10,11... | collective-permute-start | bytes 1572872 | tf_op jit(solution)/shard_map/ppermute | solution.py:341
  48.9 2.9 %collective-permute-done.8.refs_1_ = f32[9,128,128]{2,1,0:T(8,128)S(1)} collective-permute-done((f32[9,128,128]{2,1,0:T(8,128)S(1)}, f32[9,128,128]{2,1,0:T(8,128)S(1)}, u32[]{:S(2)}, u32[]{:S(2)}) %collective-permute-start.8) | collective-permute-done | bytes 589856 | tf_op jit(solution)/shard_map/ppermute | solution.py:344
  51.8 3.4 %collective-permute-start.11 = (f32[5,128,128]{2,1,0:T(8,128)S(1)}, f32[5,128,128]{2,1,0:T(8,128)S(1)}, u32[]{:S(2)}, u32[]{:S(2)}) collective-permute-start(f32[5,128,128]{2,1,0:T(8,128)S(1)} %slice.14), channel_id=1, source_target_pairs={{0,4},{4,8},{8,12},{12,16},{16,20},{20,24},{24,28},{6,2},{10,6},{1... | collective-permute-start | bytes 983048 | tf_op jit(solution)/shard_map/ppermute | solution.py:347
  55.2 0.0 collective-permute-done.9.refs_2_
  55.3 0.0 copy-done.2
  55.3 2.0 %shard_map.68 = (f32[2,2,128,128]{3,2,1,0:T(8,128)S(1)}, bf16[512,1152]{1,0:T(8,128)(2,1)S(1)}, bf16[512,1152]{1,0:T(8,128)(2,1)S(1)}) custom-call(f32[7,128,128]{2,1,0:T(8,128)} %copy-done.3, f32[9,128,128]{2,1,0:T(8,128)} %copy-done.2, f32[7,128,128]{2,1,0:T(8,128)S(1)} %collective-permute-done.9.refs_2_, ...), custom_call_target="tpu_custom_call" | custom-call | flops 201326592 | tf_op jit(solution)/shard_map/pallas_call | solution.py:42
  57.3 1.6 %collective-permute-start.10 = (f32[2,2,128,128]{3,2,1,0:T(8,128)S(1)}, f32[2,2,128,128]{3,2,1,0:T(8,128)S(1)}, u32[]{:S(2)}, u32[]{:S(2)}) collective-permute-start(f32[2,2,128,128]{3,2,1,0:T(8,128)S(1)} %get-tuple-element.61), channel_id=1, source_target_pairs={{0,1},{1,0},{2,3},{3,2},{4,5},{5,4},{6,7},{7,6},{8,9},{9,8},{10,11... | collective-permute-start | bytes 786440 | tf_op jit(solution)/shard_map/ppermute | solution.py:341
  58.9 1.3 %shard_map.70 = (bf16[512,1152]{1,0:T(8,128)(2,1)S(1)}, bf16[512,1152]{1,0:T(8,128)(2,1)S(1)}) custom-call(f32[7,128,128]{2,1,0:T(8,128)} %copy-done.3, f32[9,128,128]{2,1,0:T(8,128)} %copy-done.2, f32[7,128,128]{2,1,0:T(8,128)S(1)} %collective-permute-done.9.refs_2_), custom_call_target="tpu_custom_call" | custom-call | tf_op jit(solution)/shard_map/pallas_call | solution.py:42
  60.2 1.3 %shard_map.69 = (bf16[2,128,512]{2,1,0:T(8,128)(2,1)S(1)}, bf16[2,128,512]{2,1,0:T(8,128)(2,1)S(1)}) custom-call(s32[4,4]{1,0:T(4,128)} %bitcast.3, f32[4,128,512]{2,1,0:T(8,128)S(1)} %get-tuple-element.49.refs_1_, bf16[768,768]{1,0:T(8,128)(2,1)S(1)} %get-tuple-element.62.refs_2_, bf16[768,768]{1,0:T(8,128)(2,1)S(1)} %get-tuple-element.63.refs_3_, ...), custom_call_target="tpu_custom_call" | custom-call | flops 402653184 | tf_op jit(solution)/shard_map/pallas_call | solution.py:42
  61.5 0.0 collective-permute-done.11.refs_0_
  61.5 0.0 copy-start
  61.5 0.9 %shard_map.71 = (f32[2,2,128,128]{3,2,1,0:T(8,128)S(1)}, bf16[512,1152]{1,0:T(8,128)(2,1)S(1)}, bf16[512,1152]{1,0:T(8,128)(2,1)S(1)}) custom-call(f32[5,128,128]{2,1,0:T(8,128)S(1)} %collective-permute-done.11.refs_0_, bf16[2,128,512]{2,1,0:T(8,128)(2,1)S(1)} %get-tuple-element.59.refs_3_.refs_1_, ...), custom_call_target="tpu_custom_call", output_to_operand_aliasing={{1}: (3, {}), {2}: (4, {})} | custom-call | flops 201326592 | tf_op jit(solution)/shard_map/pallas_call | solution.py:42
  62.4 0.6 collective-permute-start.12
  63.0 2.0 %collective-permute-done.10.refs_2_ = f32[2,2,128,128]{3,2,1,0:T(8,128)S(1)} collective-permute-done((f32[2,2,128,128]{3,2,1,0:T(8,128)S(1)}, f32[2,2,128,128]{3,2,1,0:T(8,128)S(1)}, u32[]{:S(2)}, u32[]{:S(2)}) %collective-permute-start.10) | collective-permute-done | bytes 262176 | tf_op jit(solution)/shard_map/ppermute | solution.py:341
  65.0 0.0 collective-permute-done.7.refs_1_
  65.0 0.0 copy-done
  65.0 3.5 %shard_map.72 = (f32[2,1,8,128,128]{4,3,2,1,0:T(8,128)}, f32[2,2,128,128]{3,2,1,0:T(8,128)S(1)}) custom-call(s32[2,1,8]{2,1,0:T(1,128)S(1)} %copy-done, f32[2,4,128,128]{3,2,1,0:T(8,128)S(1)} %collective-permute-done.7.refs_1_, f32[2,2,128,128]{3,2,1,0:T(8,128)S(1)} %collective-permute-done.10.refs_2_, bf16[2,128,512]{2,1,0:T(8,128)(2,1)S(1)} %get-tuple-element.64.refs_3_, ...), custom_call_target="tpu_custom_call" | custom-call | flops 8053063680 | tf_op jit(solution)/shard_map/pallas_call | solution.py:42
  68.4 2.8 %collective-permute-done.12.refs_2_ = f32[2,2,128,128]{3,2,1,0:T(8,128)S(1)} collective-permute-done((f32[2,2,128,128]{3,2,1,0:T(8,128)S(1)}, f32[2,2,128,128]{3,2,1,0:T(8,128)S(1)}, u32[]{:S(2)}, u32[]{:S(2)}) %collective-permute-start.12) | collective-permute-done | bytes 262176 | tf_op jit(solution)/shard_map/ppermute | solution.py:341
  71.2 1.3 %shard_map.73 = f32[2,1,8,128,128]{4,3,2,1,0:T(8,128)} custom-call(s32[2,1,8]{2,1,0:T(1,128)S(1)} %copy-done, f32[2,2,128,128]{3,2,1,0:T(8,128)S(1)} %get-tuple-element.74.refs_1_, f32[2,2,128,128]{3,2,1,0:T(8,128)S(1)} %collective-permute-done.12.refs_2_, f32[2,1,8,128,128]{4,3,2,1,0:T(8,128)} %get-tuple-element.76.refs_3_), custom_call_target="tpu_custom_call", output_to_operand_aliasing={{}: (3, {})} | custom-call | tf_op jit(solution)/shard_map/pallas_call | solution.py:42
  (5 shorter events, 0.1 us)
Async XLA Ops:
  1.3 14.9 %collective-permute-start = (f32[8,128,128]{2,1,0:T(8,128)S(1)}, f32[8,128,128]{2,1,0:T(8,128)S(1)}, u32[]{:S(2)}, u32[]{:S(2)}) collective-permute-start(f32[8,128,128]{2,1,0:T(8,128)S(1)} %get-tuple-element.42), channel_id=1, source_target_pairs={{0,1},{1,0},{2,3},{3,2},{4,5},{5,4},{6,7},{7,6},{8,9},{9,8},{10,11... | collective-permute-start | bytes 1572872 | tf_op jit(solution)/shard_map/ppermute | solution.py:341
  4.3 13.7 %collective-permute-start.2 = (f32[8,128,128]{2,1,0:T(8,128)S(1)}, f32[8,128,128]{2,1,0:T(8,128)S(1)}, u32[]{:S(2)}, u32[]{:S(2)}) collective-permute-start(f32[8,128,128]{2,1,0:T(8,128)S(1)} %get-tuple-element.46), channel_id=1, source_target_pairs={{0,2},{2,0},{4,6},{6,4},{8,10},{10,8},{12,14},{14,12},{16,18},{18,... | collective-permute-start | bytes 1572872 | tf_op jit(solution)/shard_map/ppermute | solution.py:344
  7.6 27.3 %copy-start.1 = (f32[4,4,128,128]{3,2,1,0:T(8,128)}, f32[4,4,128,128]{3,2,1,0:T(8,128)S(1)}, u32[]{:S(2)}) copy-start(f32[4,4,128,128]{3,2,1,0:T(8,128)S(1)} %get-tuple-element.54.refs_0_) | copy-start | bytes 3145732
  16.2 18.7 %copy-start.6 = (f32[8,128,128]{2,1,0:T(8,128)}, f32[8,128,128]{2,1,0:T(8,128)S(1)}, u32[]{:S(2)}) copy-start(f32[8,128,128]{2,1,0:T(8,128)S(1)} %collective-permute-done.refs_5_) | copy-start | bytes 1572868
  16.2 14.9 %collective-permute-start.4 = (f32[8,128,128]{2,1,0:T(8,128)S(1)}, f32[8,128,128]{2,1,0:T(8,128)S(1)}, u32[]{:S(2)}, u32[]{:S(2)}) collective-permute-start(f32[8,128,128]{2,1,0:T(8,128)S(1)} %collective-permute-done.refs_5_), channel_id=1, source_target_pairs={{0,2},{2,0},{4,6},{6,4},{8,10},{10,8},{12,14},{14,12},{16,18},{18,... | collective-permute-start | bytes 1572872 | tf_op jit(solution)/shard_map/ppermute | solution.py:344
  18.0 16.9 %copy-start.4 = (f32[8,128,128]{2,1,0:T(8,128)}, f32[8,128,128]{2,1,0:T(8,128)S(1)}, u32[]{:S(2)}) copy-start(f32[8,128,128]{2,1,0:T(8,128)S(1)} %collective-permute-done.2.refs_4_) | copy-start | bytes 1572868
  18.0 16.9 %collective-permute-start.3 = (f32[7,128,128]{2,1,0:T(8,128)S(1)}, f32[7,128,128]{2,1,0:T(8,128)S(1)}, u32[]{:S(2)}, u32[]{:S(2)}) collective-permute-start(f32[7,128,128]{2,1,0:T(8,128)S(1)} %slice.12), channel_id=1, source_target_pairs={{0,4},{4,8},{8,12},{12,16},{16,20},{20,24},{24,28},{6,2},{10,6},{1... | collective-permute-start | bytes 1376264 | tf_op jit(solution)/shard_map/ppermute | solution.py:347
  21.5 23.5 %collective-permute-start.5 = (f32[4,4,128,128]{3,2,1,0:T(8,128)S(1)}, f32[4,4,128,128]{3,2,1,0:T(8,128)S(1)}, u32[]{:S(2)}, u32[]{:S(2)}) collective-permute-start(f32[4,4,128,128]{3,2,1,0:T(8,128)S(1)} %get-tuple-element.54.refs_0_), channel_id=1, source_target_pairs={{0,1},{1,0},{2,3},{3,2},{4,5},{5,4},{6,7},{7,6},{8,9},{9,8},{10,11... | collective-permute-start | bytes 3145736 | tf_op jit(solution)/shard_map/ppermute | solution.py:341
  23.1 17.8 %collective-permute-start.1 = (f32[7,128,128]{2,1,0:T(8,128)S(1)}, f32[7,128,128]{2,1,0:T(8,128)S(1)}, u32[]{:S(2)}, u32[]{:S(2)}) collective-permute-start(f32[7,128,128]{2,1,0:T(8,128)S(1)} %get-tuple-element.43), channel_id=1, source_target_pairs={{0,2},{2,0},{4,6},{6,4},{8,10},{10,8},{12,14},{14,12},{16,18},{18,... | collective-permute-start | bytes 1376264 | tf_op jit(solution)/shard_map/ppermute | solution.py:344
  23.1 28.7 %collective-permute-start.8 = (f32[9,128,128]{2,1,0:T(8,128)S(1)}, f32[9,128,128]{2,1,0:T(8,128)S(1)}, u32[]{:S(2)}, u32[]{:S(2)}) collective-permute-start(f32[9,128,128]{2,1,0:T(8,128)S(1)} %get-tuple-element.57), channel_id=1, source_target_pairs={{0,2},{2,0},{4,6},{6,4},{8,10},{10,8},{12,14},{14,12},{16,18},{18,... | collective-permute-start | bytes 1769480 | tf_op jit(solution)/shard_map/ppermute | solution.py:344
  31.1 3.8 %copy-start.5 = (f32[8,128,128]{2,1,0:T(8,128)}, f32[8,128,128]{2,1,0:T(8,128)S(1)}, u32[]{:S(2)}) copy-start(f32[8,128,128]{2,1,0:T(8,128)S(1)} %collective-permute-done.4.refs_6_) | copy-start | bytes 1572868
  31.1 13.6 %collective-permute-start.6 = (f32[7,128,128]{2,1,0:T(8,128)S(1)}, f32[7,128,128]{2,1,0:T(8,128)S(1)}, u32[]{:S(2)}, u32[]{:S(2)}) collective-permute-start(f32[7,128,128]{2,1,0:T(8,128)S(1)} %slice.13), channel_id=1, source_target_pairs={{0,4},{4,8},{8,12},{12,16},{16,20},{20,24},{24,28},{6,2},{10,6},{1... | collective-permute-start | bytes 1376264 | tf_op jit(solution)/shard_map/ppermute | solution.py:347
  40.9 6.4 %copy-start.3 = (f32[7,128,128]{2,1,0:T(8,128)}, f32[7,128,128]{2,1,0:T(8,128)S(1)}, u32[]{:S(2)}) copy-start(f32[7,128,128]{2,1,0:T(8,128)S(1)} %collective-permute-done.1.refs_0_) | copy-start | bytes 1376260
  40.9 14.4 %collective-permute-start.9 = (f32[7,128,128]{2,1,0:T(8,128)S(1)}, f32[7,128,128]{2,1,0:T(8,128)S(1)}, u32[]{:S(2)}, u32[]{:S(2)}) collective-permute-start(f32[7,128,128]{2,1,0:T(8,128)S(1)} %collective-permute-done.1.refs_0_), channel_id=1, source_target_pairs={{0,4},{4,8},{8,12},{12,16},{16,20},{20,24},{24,28},{6,2},{10,6},{1... | collective-permute-start | bytes 1376264 | tf_op jit(solution)/shard_map/ppermute | solution.py:347
  47.3 17.6 %collective-permute-start.7 = (f32[2,4,128,128]{3,2,1,0:T(8,128)S(1)}, f32[2,4,128,128]{3,2,1,0:T(8,128)S(1)}, u32[]{:S(2)}, u32[]{:S(2)}) collective-permute-start(f32[2,4,128,128]{3,2,1,0:T(8,128)S(1)} %get-tuple-element.55), channel_id=1, source_target_pairs={{0,1},{1,0},{2,3},{3,2},{4,5},{5,4},{6,7},{7,6},{8,9},{9,8},{10,11... | collective-permute-start | bytes 1572872 | tf_op jit(solution)/shard_map/ppermute | solution.py:341
  51.8 3.5 %copy-start.2 = (f32[9,128,128]{2,1,0:T(8,128)}, f32[9,128,128]{2,1,0:T(8,128)S(1)}, u32[]{:S(2)}) copy-start(f32[9,128,128]{2,1,0:T(8,128)S(1)} %collective-permute-done.8.refs_1_) | copy-start | bytes 1769476
  51.8 9.7 %collective-permute-start.11 = (f32[5,128,128]{2,1,0:T(8,128)S(1)}, f32[5,128,128]{2,1,0:T(8,128)S(1)}, u32[]{:S(2)}, u32[]{:S(2)}) collective-permute-start(f32[5,128,128]{2,1,0:T(8,128)S(1)} %slice.14), channel_id=1, source_target_pairs={{0,4},{4,8},{8,12},{12,16},{16,20},{20,24},{24,28},{6,2},{10,6},{1... | collective-permute-start | bytes 983048 | tf_op jit(solution)/shard_map/ppermute | solution.py:347
  57.3 7.7 %collective-permute-start.10 = (f32[2,2,128,128]{3,2,1,0:T(8,128)S(1)}, f32[2,2,128,128]{3,2,1,0:T(8,128)S(1)}, u32[]{:S(2)}, u32[]{:S(2)}) collective-permute-start(f32[2,2,128,128]{3,2,1,0:T(8,128)S(1)} %get-tuple-element.61), channel_id=1, source_target_pairs={{0,1},{1,0},{2,3},{3,2},{4,5},{5,4},{6,7},{7,6},{8,9},{9,8},{10,11... | collective-permute-start | bytes 786440 | tf_op jit(solution)/shard_map/ppermute | solution.py:341
  61.5 3.5 %copy-start = (s32[2,1,8]{2,1,0:T(1,128)S(1)}, s32[2,1,8]{2,1,0:T(1,128)}, u32[]{:S(2)}) copy-start(s32[2,1,8]{2,1,0:T(1,128)} %refs_0_.5) | copy-start | bytes 196
  62.4 8.9 %collective-permute-start.12 = (f32[2,2,128,128]{3,2,1,0:T(8,128)S(1)}, f32[2,2,128,128]{3,2,1,0:T(8,128)S(1)}, u32[]{:S(2)}, u32[]{:S(2)}) collective-permute-start(f32[2,2,128,128]{3,2,1,0:T(8,128)S(1)} %get-tuple-element.75), channel_id=1, source_target_pairs={{0,1},{1,0},{2,3},{3,2},{4,5},{5,4},{6,7},{7,6},{8,9},{9,8},{10,11... | collective-permute-start | bytes 786440 | tf_op jit(solution)/shard_map/ppermute | solution.py:341

commit v7 on v6

--- a/solution.py
+++ b/solution.py
@@ -147,11 +147,13 @@
     return start(packed, stage.at[pl.ds(jnp.where(even, 1, 16), 7)], sem)
 
 
-def product_own(size, where, u_any, p_mask_any, p_any, pe_z, pe_y, pc, pc_y, *refs):
-    t_own, ud_hi, ud_lo, oth_hi, oth_lo, p_mask, p, stages, u, hi, lo, sems = refs
-    even, layer = where[0] % 2 == 0, where[1]
+def product_own(total_rows, size, where, u_any, p_mask_any, p_any, t_mask_any, pe_z, pe_y, pc, pc_y, *refs):
+    t_own, ud_hi, ud_lo, oth_hi, oth_lo, keeps, p_mask, t_mask, p, stages, u, hi, lo, sems = refs
+    slab, layer = where[0], where[1]
+    even = slab % 2 == 0
     copies = [start(u_any, u, sems.at[0])]
     copies += [start(p_any, p, sems.at[1]), start(p_mask_any, p_mask, sems.at[2])]
+    copies += [start(t_mask_any, t_mask, sems.at[10])]
     copies += gather_pair(even, pe_y, False, stages.at[0], sems, 3)
     copies += gather_pair(even, pc, True, stages.at[1], sems, 5)
     copies += gather_pair(even, pc_y, False, stages.at[1], sems, 7)
@@ -164,6 +166,10 @@
         cols = pl.ds(aligned(slot_base(i, layer), size), 4 * size)
         rows = pl.ds(i * size, size)
         ud_hi[rows, cols], ud_lo[rows, cols] = joined([u[i, m] for m in range(4)], 1)
+        for m in range(4):
+            col = slab * 4 + 2 * (slot_base(i, layer) + m) - 4 + layer
+            keep = jnp.where((col >= 0) & (col < total_rows), t_mask[i, m], 0).astype(F32)
+            keeps[i, m] = jnp.full(keeps.shape[2:], keep, F32)
     for a in range(2):
         for e in range(4):
             stages[0, 8 + 4 * a + e] = p[a, 0, 2 * e] * p_mask[a, 0, 2 * e].astype(F32)
@@ -180,35 +186,27 @@
             fill_band(size, stages.at[1], oth_hi, oth_lo, -1, rows)
 
 
-def product_rows(total_rows, size, where, send, t_mask, t_own, others, hi, lo, t_hi, t_lo):
-    slab, layer = where[0], where[1]
+def product_rows(size, where, send, keeps, t_own, others, hi, lo, t_hi, t_lo):
+    layer = where[1]
     for q in range(2):
         i = 2 * q + (1 - layer if send else layer)
-        base = q + 1 - layer if send else q
         rows = pl.ds(aligned(q if send else q + layer, size), 4 * size)
         cols = pl.ds(aligned(q + 1 if send else q + layer, size), 4 * size)
         left = joined([others[i, m] for m in range(4)], 1)
         total = t_own[i] + dot3(left, (hi[rows, cols], lo[rows, cols]), 0)
-        kept = []
-        for m in range(4):
-            col = slab * 4 + 2 * (base + m) - 4 + layer
-            keep = jnp.where((col >= 0) & (col < total_rows), t_mask[i, m], 0).astype(F32)
-            kept.append(total[:, m * size : (m + 1) * size] * keep)
+        kept = [total[:, m * size : (m + 1) * size] * keeps[i, m, 0:1] for m in range(4)]
         t_hi[q], t_lo[q] = joined(kept, 1)
 
 
-def product_send(total_rows, size, where, t_mask_any, t_own, ud_hi, ud_lo, hi_in, lo_in, u_cross, pc_z, *refs):
-    t_hi, t_lo, ss, hi, lo, t_mask, sem = refs
+def product_send(size, where, keeps, t_own, ud_hi, ud_lo, hi_in, lo_in, u_cross, pc_z, t_hi, t_lo, ss, hi, lo):
     even, layer = where[0] % 2 == 0, where[1]
-    mask_copy = start(t_mask_any, t_mask, sem)
     for case, rows, first in ((even, (0, 1), 1), (jnp.logical_not(even), (4, 5), 16)):
 
         @pl.when(case)
         def _(rows=rows, first=first):
             fill_band(size, pc_z, hi, lo, -1, rows, first)
 
-    mask_copy.wait()
-    product_rows(total_rows, size, where, True, t_mask, t_own, u_cross, hi, lo, t_hi, t_lo)
+    product_rows(size, where, True, keeps, t_own, u_cross, hi, lo, t_hi, t_lo)
     for q in range(2):
         cols = pl.ds(aligned(q + 1 - layer, size), 4 * size)
         sums = dot3((t_hi[q], t_lo[q]), (ud_hi[:, cols], ud_lo[:, cols]), 1)
@@ -216,9 +214,8 @@
             ss[q, r] = sums[:, r * size : (r + 1) * size]
 
 
-def product_keep(total_rows, size, where, t_mask_any, t_own, hi, lo, u_cross, t_hi, t_lo, t_mask, sem):
-    start(t_mask_any, t_mask, sem).wait()
-    product_rows(total_rows, size, where, False, t_mask, t_own, u_cross, hi, lo, t_hi, t_lo)
+def product_keep(size, where, keeps, t_own, hi, lo, u_cross, t_hi, t_lo):
+    product_rows(size, where, False, keeps, t_own, u_cross, hi, lo, t_hi, t_lo)
 
 
 def gather_halo(pieces, stage, sems):
@@ -290,7 +287,7 @@
 
 def keep_rows(total_rows, size, where, o_mask, ss, halo, *refs):
     (t_hi, t_lo), (ud_hi, ud_lo), first, last = (refs[2 * n : 2 * n + 2] for n in range(4))
-    out_any, part, out, sems = refs[8:]
+    out_any, part, keeps, out, sems = refs[8:]
     stores = []
     for q in range(2):
         i = 2 * q + where[1]
@@ -310,19 +307,20 @@
         for n in range(2):
             keep = out_keep(total_rows, where, o_mask, q, (10 - i + n) % 8)
             part[q, n] = sums[:, n * size : (n + 1) * size] * keep
+            keeps[q, n] = jnp.full(keeps.shape[2:], keep, F32)
     for c in stores:
         c.wait()
 
 
-def combine(total_rows, where, o_mask, part, halo, kept_any, out_any, done, sems):
+def combine(where, keeps, part, halo, kept_any, out_any, out, sems):
     stores = []
     for q in range(2):
-        for t in range(2):
-            o = (10 - 2 * q - where[1] + t) % 8
-            done[q, t] = part[q, t] + halo[q, t] * out_keep(total_rows, where, o_mask, q, o)
-            stores.append(start(done.at[q, t], out_any.at[q, 0, o], sems.at[2 * q + t]))
-    for s in stores:
-        s.wait()
+        for n in range(2):
+            o = (10 - 2 * q - where[1] + n) % 8
+            out[q, n] = part[q, n] + halo[q, n] * keeps[q, n, 0:1]
+            stores.append(start(out.at[q, n], out_any.at[q, 0, o], sems.at[2 * q + n]))
+    for c in stores:
+        c.wait()
 
 
 def after(x, *others):
@@ -375,35 +373,33 @@
     t_like = (4, size, 4 * size)
     band = [vmem(wide, wide, dtype=BF16)] * 2
     own_rows = [vmem(4 * size, wide, dtype=BF16)] * 2
-    t_own, ud_hi, ud_lo, *oth = call(
-        functools.partial(product_own, size),
-        [vmem(*t_like), *own_rows, *band],
-        [HBM, HBM, HBM, ANY] + [HBM] * 3,
-        [pltpu.SMEM(p_mask.shape, jnp.int32), vmem(*p_values.shape)]
-        + [vmem(2, 24, size, size), vmem(4, 4, size, size), *band, sems(10)],
+    t_own, ud_hi, ud_lo, *oth, keeps = call(
+        functools.partial(product_own, total_rows, size),
+        [vmem(*t_like), *own_rows, *band, vmem(4, 4, 8, size)],
+        [HBM, HBM, HBM, HBM, ANY] + [HBM] * 3,
+        [pltpu.SMEM(x.shape, jnp.int32) for x in (p_mask, t_mask)]
+        + [vmem(*p_values.shape)]
+        + [vmem(2, 24, size, size), vmem(4, 4, size, size), *band, sems(11)],
         flops=40 * unit,
-    )(u_own, p_mask, p_values, pe_z, pe_y, pc, pc_y)
+    )(u_own, p_mask, p_values, t_mask, pe_z, pe_y, pc, pc_y)
     u_y = [over_pair(after(x, pc)) for x in packed]
     u_z = [onto(after(u_y[0], t_own))]
-    t_mask = after(t_mask, u_y[0])
+    keeps = after(keeps, u_y[0])
     rows = [vmem(2, size, 4 * size, dtype=BF16)] * 2
-    masks = pltpu.SMEM(t_mask.shape, jnp.int32)
     *t_send, ss, hi, lo = call(
-        functools.partial(product_send, total_rows, size),
+        functools.partial(product_send, size),
         [*rows, vmem(2, 4, size, size), *band],
-        [HBM] + [VMEM] * 7,
-        [masks, pltpu.SemaphoreType.DMA],
+        [VMEM] * 8,
         flops=4 * unit,
         alias={4: 3, 5: 4},
-    )(t_mask, t_own, ud_hi, ud_lo, *oth, u_oth, pc_z)
+    )(keeps, t_own, ud_hi, ud_lo, *oth, u_oth, pc_z)
     ss_got = over_layer(ss)
     t_keep = call(
-        functools.partial(product_keep, total_rows, size),
+        functools.partial(product_keep, size),
         rows,
-        [HBM] + [VMEM] * 4,
-        [masks, pltpu.SemaphoreType.DMA],
+        [VMEM] * 5,
         flops=2 * unit,
-    )(t_mask, t_own, hi, lo, u_oth)
+    )(keeps, t_own, hi, lo, u_oth)
     u_z.append(onto(after(u_y[1][:5], t_send[0])))
     uh = [vmem(4 * size, 9 * size, dtype=BF16)] * 2
     pair_sums = vmem(2, 2, size, size)
@@ -428,21 +424,21 @@
         alias={3: 1, 4: 2},
     )(u_z[1], *t_send, *uh_last)
     last_got = over_layer(last)
-    kept, part = call(
+    kept, part, keeps = call(
         functools.partial(keep_rows, total_rows, size),
-        [shape(*p_values.shape), pair_sums],
+        [shape(*p_values.shape), pair_sums, vmem(2, 2, 8, size)],
         [SMEM] + [VMEM] * 10,
         [vmem(2, 6, size, size), sems(12)],
         flops=40 * unit,
     )(out_mask, ss_got, halo_got, *t_keep, ud_hi, ud_lo, *uh_first, *uh_last)
     (out,) = call(
-        functools.partial(combine, total_rows),
+        combine,
         [shape(*p_values.shape)],
-        [SMEM, VMEM, VMEM, ANY],
+        [VMEM, VMEM, VMEM, ANY],
         [vmem(2, 2, size, size), sems(4)],
         alias={3: 0},
         limit=16,
-    )(out_mask, part, last_got, kept)
+    )(keeps, part, last_got, kept)
     return out
 
 

time: 72.9 us -> 72.1 us (0.989)
  Pallas kernels: 19.2 us -> 17.4 us
    pallas_call x10, Pallas kernels: 19.2 us -> 17.4 us  [run(): pl.pallas_call(kernel, out_shape=outs, in_specs=[ANY if spec is HBM else...]
  transfers between devices with their start and end apart: 13 -> 13, of which waited for: 7 -> 7; matrix products, arithmetic and copies ran while one was open for 0% -> 0% of each run, Pallas kernels for 23% -> 22%
where the time goes in v7:
time: 72.1 us; the launch traced here: 71.4 us
  starting transfers between devices  28.5 us (40%)
  waiting for transfers between devices  25.1 us (35%)
  Pallas kernels  17.4 us (24%)
    pallas_call x10, Pallas kernels, run(): pl.pallas_call(kernel, out_shape=outs, in_specs=[ANY if spec is HBM else...  17.4 us
    ppermute x4, starting transfers between devices, onto(): return lax.ppermute(x, SLABS, onward)  14.4 us
    ppermute x5, waiting for transfers between devices, over_layer(): return lax.ppermute(x, 'layer', swap)  13.3 us
    ppermute x4, waiting for transfers between devices, over_pair(): return lax.ppermute(x, SLABS, pair)  11.8 us
    ppermute x5, starting transfers between devices, over_layer(): return lax.ppermute(x, 'layer', swap)  8.78 us
    ppermute x4, starting transfers between devices, over_pair(): return lax.ppermute(x, SLABS, pair)  5.31 us
  transfers between devices with their start and end apart: 13, of which 7 were waited for; matrix products, arithmetic and copies ran while one was open for 0% of the time, Pallas kernels for 22%

profile of v7, /device:TPU:0, one launch (start us, length us, event | category | flops | bytes accessed | tf_op | source)
XLA Modules:
  0.0 71.4 jit_solution(17286944695586864753)
XLA Ops:
  0.0 1.3 %shard_map.65 = (f32[8,128,128]{2,1,0:T(8,128)S(1)}, f32[8,128,128]{2,1,0:T(8,128)S(1)}) custom-call(s32[2,1,8]{2,1,0:T(1,128)} %refs_1_.5, f32[2,1,8,128,128]{4,3,2,1,0:T(8,128)} %refs_2_.1), custom_call_target="tpu_custom_call" | custom-call | tf_op jit(solution)/shard_map/pallas_call | solution.py:42
  1.3 3.0 %collective-permute-start.2 = (f32[8,128,128]{2,1,0:T(8,128)S(1)}, f32[8,128,128]{2,1,0:T(8,128)S(1)}, u32[]{:S(2)}, u32[]{:S(2)}) collective-permute-start(f32[8,128,128]{2,1,0:T(8,128)S(1)} %get-tuple-element.46), channel_id=1, source_target_pairs={{0,1},{1,0},{2,3},{3,2},{4,5},{5,4},{6,7},{7,6},{8,9},{9,8},{10,11... | collective-permute-start | bytes 1572872 | tf_op jit(solution)/shard_map/ppermute | solution.py:339
  4.3 1.5 %collective-permute-start = (f32[8,128,128]{2,1,0:T(8,128)S(1)}, f32[8,128,128]{2,1,0:T(8,128)S(1)}, u32[]{:S(2)}, u32[]{:S(2)}) collective-permute-start(f32[8,128,128]{2,1,0:T(8,128)S(1)} %get-tuple-element.44), channel_id=1, source_target_pairs={{0,2},{2,0},{4,6},{6,4},{8,10},{10,8},{12,14},{14,12},{16,18},{18,... | collective-permute-start | bytes 1572872 | tf_op jit(solution)/shard_map/ppermute | solution.py:342
  5.8 1.8 %shard_map.64 = (f32[4,4,128,128]{3,2,1,0:T(8,128)S(1)}, f32[7,128,128]{2,1,0:T(8,128)S(1)}, f32[9,128,128]{2,1,0:T(8,128)S(1)}) custom-call(s32[4,4]{1,0:T(4,128)} %bitcast.2, f32[4,4,1,128,128]{4,3,2,1,0:T(8,128)} %refs_1_.3), custom_call_target="tpu_custom_call" | custom-call | tf_op jit(solution)/shard_map/pallas_call | solution.py:42
  7.6 0.0 copy-start
  7.6 8.6 %collective-permute-done.2.refs_6_ = f32[8,128,128]{2,1,0:T(8,128)S(1)} collective-permute-done((f32[8,128,128]{2,1,0:T(8,128)S(1)}, f32[8,128,128]{2,1,0:T(8,128)S(1)}, u32[]{:S(2)}, u32[]{:S(2)}) %collective-permute-start.2) | collective-permute-done | bytes 524320 | tf_op jit(solution)/shard_map/ppermute | solution.py:339
  16.2 0.0 copy-start.6
  16.2 1.8 %collective-permute-start.3 = (f32[8,128,128]{2,1,0:T(8,128)S(1)}, f32[8,128,128]{2,1,0:T(8,128)S(1)}, u32[]{:S(2)}, u32[]{:S(2)}) collective-permute-start(f32[8,128,128]{2,1,0:T(8,128)S(1)} %collective-permute-done.2.refs_6_), channel_id=1, source_target_pairs={{0,2},{2,0},{4,6},{6,4},{8,10},{10,8},{12,14},{14,12},{16,18},{18,... | collective-permute-start | bytes 1572872 | tf_op jit(solution)/shard_map/ppermute | solution.py:342
  18.0 0.0 collective-permute-done.refs_5_
  18.0 0.0 copy-start.4
  18.0 3.5 %collective-permute-start.1 = (f32[7,128,128]{2,1,0:T(8,128)S(1)}, f32[7,128,128]{2,1,0:T(8,128)S(1)}, u32[]{:S(2)}, u32[]{:S(2)}) collective-permute-start(f32[7,128,128]{2,1,0:T(8,128)S(1)} %slice.12), channel_id=1, source_target_pairs={{0,4},{4,8},{8,12},{12,16},{16,20},{20,24},{24,28},{6,2},{10,6},{1... | collective-permute-start | bytes 1376264 | tf_op jit(solution)/shard_map/ppermute | solution.py:345
  21.5 1.6 %collective-permute-start.5 = (f32[4,4,128,128]{3,2,1,0:T(8,128)S(1)}, f32[4,4,128,128]{3,2,1,0:T(8,128)S(1)}, u32[]{:S(2)}, u32[]{:S(2)}) collective-permute-start(f32[4,4,128,128]{3,2,1,0:T(8,128)S(1)} %get-tuple-element.57.refs_0_), channel_id=1, source_target_pairs={{0,1},{1,0},{2,3},{3,2},{4,5},{5,4},{6,7},{7,6},{8,9},{9,8},{10,11... | collective-permute-start | bytes 3145736 | tf_op jit(solution)/shard_map/ppermute | solution.py:339
  23.1 0.0 collective-permute-start.4
  23.1 2.0 %collective-permute-start.8 = (f32[9,128,128]{2,1,0:T(8,128)S(1)}, f32[9,128,128]{2,1,0:T(8,128)S(1)}, u32[]{:S(2)}, u32[]{:S(2)}) collective-permute-start(f32[9,128,128]{2,1,0:T(8,128)S(1)} %get-tuple-element.60), channel_id=1, source_target_pairs={{0,2},{2,0},{4,6},{6,4},{8,10},{10,8},{12,14},{14,12},{16,18},{18,... | collective-permute-start | bytes 1769480 | tf_op jit(solution)/shard_map/ppermute | solution.py:342
  25.1 6.0 %collective-permute-done.3.refs_7_ = f32[8,128,128]{2,1,0:T(8,128)S(1)} collective-permute-done((f32[8,128,128]{2,1,0:T(8,128)S(1)}, f32[8,128,128]{2,1,0:T(8,128)S(1)}, u32[]{:S(2)}, u32[]{:S(2)}) %collective-permute-start.3) | collective-permute-done | bytes 524320 | tf_op jit(solution)/shard_map/ppermute | solution.py:342
  31.1 0.0 copy-start.5
  31.1 3.8 %collective-permute-start.6 = (f32[7,128,128]{2,1,0:T(8,128)S(1)}, f32[7,128,128]{2,1,0:T(8,128)S(1)}, u32[]{:S(2)}, u32[]{:S(2)}) collective-permute-start(f32[7,128,128]{2,1,0:T(8,128)S(1)} %slice.13), channel_id=1, source_target_pairs={{0,4},{4,8},{8,12},{12,16},{16,20},{20,24},{24,28},{6,2},{10,6},{1... | collective-permute-start | bytes 1376264 | tf_op jit(solution)/shard_map/ppermute | solution.py:345
  34.9 0.0 collective-permute-done.1.refs_4_
  34.9 0.0 copy-done
  34.9 0.0 copy-done.6
  34.9 0.0 copy-done.4
  34.9 0.0 copy-done.5
  34.9 3.6 %shard_map.66 = (f32[4,128,512]{2,1,0:T(8,128)S(1)}, bf16[512,768]{1,0:T(8,128)(2,1)S(1)}, bf16[512,768]{1,0:T(8,128)(2,1)S(1)}, bf16[768,768]{1,0:T(8,128)(2,1)...) custom-call(f32[4,4,128,128]{3,2,1,0:T(8,128)} %copy-done, s32[2,1,8]{2,1,0:T(1,128)} %refs_1_.5, ...), custom_call_target="tpu_custom_call" | custom-call | flops 8053063680 | tf_op jit(solution)/shard_map/pallas_call | solution.py:42
  38.5 2.4 %collective-permute-done.4.refs_0_ = f32[7,128,128]{2,1,0:T(8,128)S(1)} collective-permute-done((f32[7,128,128]{2,1,0:T(8,128)S(1)}, f32[7,128,128]{2,1,0:T(8,128)S(1)}, u32[]{:S(2)}, u32[]{:S(2)}) %collective-permute-start.4) | collective-permute-done | bytes 458784 | tf_op jit(solution)/shard_map/ppermute | solution.py:342
  40.9 3.7 %collective-permute-start.9 = (f32[7,128,128]{2,1,0:T(8,128)S(1)}, f32[7,128,128]{2,1,0:T(8,128)S(1)}, u32[]{:S(2)}, u32[]{:S(2)}) collective-permute-start(f32[7,128,128]{2,1,0:T(8,128)S(1)} %collective-permute-done.4.refs_0_), channel_id=1, source_target_pairs={{0,4},{4,8},{8,12},{12,16},{16,20},{20,24},{24,28},{6,2},{10,6},{1... | collective-permute-start | bytes 1376264 | tf_op jit(solution)/shard_map/ppermute | solution.py:345
  44.6 0.0 collective-permute-done.6.refs_7_
  44.7 0.4 collective-permute-done.5.refs_6_.refs_4_
  45.0 1.7 %shard_map.67 = (bf16[2,128,512]{2,1,0:T(8,128)(2,1)S(1)}, bf16[2,128,512]{2,1,0:T(8,128)(2,1)S(1)}, f32[2,4,128,128]{3,2,1,0:T(8,128)S(1)}, bf16[768,768]{1,0:T(8,128)(2,1)S(1)}, bf16[768,768]{1,0:T(8,128)(2,1)S(1)}) custom-call(f32[4,4,8,128]{3,2,1,0:T(8,128)S(1)} %get-tuple-element.51.refs_0_, ...), custom_call_target="tpu_custom_call", output_to_operand_aliasing={{3}: (4, {}), {4}: (5, {})} | custom-call | flops 805306368 | tf_op jit(solution)/shard_map/pallas_call | solution.py:42
  46.7 0.0 copy-done.3
  46.8 1.6 %collective-permute-start.7 = (f32[2,4,128,128]{3,2,1,0:T(8,128)S(1)}, f32[2,4,128,128]{3,2,1,0:T(8,128)S(1)}, u32[]{:S(2)}, u32[]{:S(2)}) collective-permute-start(f32[2,4,128,128]{3,2,1,0:T(8,128)S(1)} %get-tuple-element.58), channel_id=1, source_target_pairs={{0,1},{1,0},{2,3},{3,2},{4,5},{5,4},{6,7},{7,6},{8,9},{9,8},{10,11... | collective-permute-start | bytes 1572872 | tf_op jit(solution)/shard_map/ppermute | solution.py:339
  48.3 3.5 %collective-permute-done.8.refs_1_ = f32[9,128,128]{2,1,0:T(8,128)S(1)} collective-permute-done((f32[9,128,128]{2,1,0:T(8,128)S(1)}, f32[9,128,128]{2,1,0:T(8,128)S(1)}, u32[]{:S(2)}, u32[]{:S(2)}) %collective-permute-start.8) | collective-permute-done | bytes 589856 | tf_op jit(solution)/shard_map/ppermute | solution.py:342
  51.8 3.4 %collective-permute-start.11 = (f32[5,128,128]{2,1,0:T(8,128)S(1)}, f32[5,128,128]{2,1,0:T(8,128)S(1)}, u32[]{:S(2)}, u32[]{:S(2)}) collective-permute-start(f32[5,128,128]{2,1,0:T(8,128)S(1)} %slice.14), channel_id=1, source_target_pairs={{0,4},{4,8},{8,12},{12,16},{16,20},{20,24},{24,28},{6,2},{10,6},{1... | collective-permute-start | bytes 983048 | tf_op jit(solution)/shard_map/ppermute | solution.py:345
  55.2 0.0 collective-permute-done.9.refs_2_
  55.3 0.0 copy-done.2
  55.3 2.0 %shard_map.68 = (f32[2,2,128,128]{3,2,1,0:T(8,128)S(1)}, bf16[512,1152]{1,0:T(8,128)(2,1)S(1)}, bf16[512,1152]{1,0:T(8,128)(2,1)S(1)}) custom-call(f32[7,128,128]{2,1,0:T(8,128)} %copy-done.3, f32[9,128,128]{2,1,0:T(8,128)} %copy-done.2, f32[7,128,128]{2,1,0:T(8,128)S(1)} %collective-permute-done.9.refs_2_, ...), custom_call_target="tpu_custom_call" | custom-call | flops 201326592 | tf_op jit(solution)/shard_map/pallas_call | solution.py:42
  57.3 1.6 %collective-permute-start.10 = (f32[2,2,128,128]{3,2,1,0:T(8,128)S(1)}, f32[2,2,128,128]{3,2,1,0:T(8,128)S(1)}, u32[]{:S(2)}, u32[]{:S(2)}) collective-permute-start(f32[2,2,128,128]{3,2,1,0:T(8,128)S(1)} %get-tuple-element.64), channel_id=1, source_target_pairs={{0,1},{1,0},{2,3},{3,2},{4,5},{5,4},{6,7},{7,6},{8,9},{9,8},{10,11... | collective-permute-start | bytes 786440 | tf_op jit(solution)/shard_map/ppermute | solution.py:339
  58.9 1.3 %shard_map.70 = (bf16[512,1152]{1,0:T(8,128)(2,1)S(1)}, bf16[512,1152]{1,0:T(8,128)(2,1)S(1)}) custom-call(f32[7,128,128]{2,1,0:T(8,128)} %copy-done.3, f32[9,128,128]{2,1,0:T(8,128)} %copy-done.2, f32[7,128,128]{2,1,0:T(8,128)S(1)} %collective-permute-done.9.refs_2_), custom_call_target="tpu_custom_call" | custom-call | tf_op jit(solution)/shard_map/pallas_call | solution.py:42
  60.2 0.6 shard_map.69
  60.8 0.0 collective-permute-done.11.refs_0_
  60.8 0.0 copy-start.1
  60.8 0.9 %shard_map.71 = (f32[2,2,128,128]{3,2,1,0:T(8,128)S(1)}, bf16[512,1152]{1,0:T(8,128)(2,1)S(1)}, bf16[512,1152]{1,0:T(8,128)(2,1)S(1)}) custom-call(f32[5,128,128]{2,1,0:T(8,128)S(1)} %collective-permute-done.11.refs_0_, bf16[2,128,512]{2,1,0:T(8,128)(2,1)S(1)} %get-tuple-element.62.refs_3_.refs_1_, ...), custom_call_target="tpu_custom_call", output_to_operand_aliasing={{1}: (3, {}), {2}: (4, {})} | custom-call | flops 201326592 | tf_op jit(solution)/shard_map/pallas_call | solution.py:42
  61.7 1.1 %collective-permute-start.12 = (f32[2,2,128,128]{3,2,1,0:T(8,128)S(1)}, f32[2,2,128,128]{3,2,1,0:T(8,128)S(1)}, u32[]{:S(2)}, u32[]{:S(2)}) collective-permute-start(f32[2,2,128,128]{3,2,1,0:T(8,128)S(1)} %get-tuple-element.79), channel_id=1, source_target_pairs={{0,1},{1,0},{2,3},{3,2},{4,5},{5,4},{6,7},{7,6},{8,9},{9,8},{10,11... | collective-permute-start | bytes 786440 | tf_op jit(solution)/shard_map/ppermute | solution.py:339
  62.8 1.6 %collective-permute-done.10.refs_2_ = f32[2,2,128,128]{3,2,1,0:T(8,128)S(1)} collective-permute-done((f32[2,2,128,128]{3,2,1,0:T(8,128)S(1)}, f32[2,2,128,128]{3,2,1,0:T(8,128)S(1)}, u32[]{:S(2)}, u32[]{:S(2)}) %collective-permute-start.10) | collective-permute-done | bytes 262176 | tf_op jit(solution)/shard_map/ppermute | solution.py:339
  64.4 0.0 collective-permute-done.7.refs_1_
  64.4 0.0 copy-done.1
  64.4 3.5 %shard_map.72 = (f32[2,1,8,128,128]{4,3,2,1,0:T(8,128)}, f32[2,2,128,128]{3,2,1,0:T(8,128)S(1)}, f32[2,2,8,128]{3,2,1,0:T(8,128)S(1)}) custom-call(s32[2,1,8]{2,1,0:T(1,128)S(1)} %copy-done.1, f32[2,4,128,128]{3,2,1,0:T(8,128)S(1)} %collective-permute-done.7.refs_1_, f32[2,2,128,128]{3,2,1,0:T(8,128)S(1)} %collective-permute-done.10.refs_2_, ...), custom_call_target="tpu_custom_call" | custom-call | flops 8053063680 | tf_op jit(solution)/shard_map/pallas_call | solution.py:42
  67.8 2.8 %collective-permute-done.12.refs_2_ = f32[2,2,128,128]{3,2,1,0:T(8,128)S(1)} collective-permute-done((f32[2,2,128,128]{3,2,1,0:T(8,128)S(1)}, f32[2,2,128,128]{3,2,1,0:T(8,128)S(1)}, u32[]{:S(2)}, u32[]{:S(2)}) %collective-permute-start.12) | collective-permute-done | bytes 262176 | tf_op jit(solution)/shard_map/ppermute | solution.py:339
  70.6 0.7 %shard_map.73 = f32[2,1,8,128,128]{4,3,2,1,0:T(8,128)} custom-call(f32[2,2,8,128]{3,2,1,0:T(8,128)S(1)} %get-tuple-element.77.refs_0_, f32[2,2,128,128]{3,2,1,0:T(8,128)S(1)} %get-tuple-element.78.refs_1_, f32[2,2,128,128]{3,2,1,0:T(8,128)S(1)} %collective-permute-done.12.refs_2_, ...), custom_call_target="tpu_custom_call", output_to_operand_aliasing={{}: (3, {})} | custom-call | tf_op jit(solution)/shard_map/pallas_call | solution.py:42
  (5 shorter events, 0.1 us)
Async XLA Ops:
  1.3 14.9 %collective-permute-start.2 = (f32[8,128,128]{2,1,0:T(8,128)S(1)}, f32[8,128,128]{2,1,0:T(8,128)S(1)}, u32[]{:S(2)}, u32[]{:S(2)}) collective-permute-start(f32[8,128,128]{2,1,0:T(8,128)S(1)} %get-tuple-element.46), channel_id=1, source_target_pairs={{0,1},{1,0},{2,3},{3,2},{4,5},{5,4},{6,7},{7,6},{8,9},{9,8},{10,11... | collective-permute-start | bytes 1572872 | tf_op jit(solution)/shard_map/ppermute | solution.py:339
  4.3 13.7 %collective-permute-start = (f32[8,128,128]{2,1,0:T(8,128)S(1)}, f32[8,128,128]{2,1,0:T(8,128)S(1)}, u32[]{:S(2)}, u32[]{:S(2)}) collective-permute-start(f32[8,128,128]{2,1,0:T(8,128)S(1)} %get-tuple-element.44), channel_id=1, source_target_pairs={{0,2},{2,0},{4,6},{6,4},{8,10},{10,8},{12,14},{14,12},{16,18},{18,... | collective-permute-start | bytes 1572872 | tf_op jit(solution)/shard_map/ppermute | solution.py:342
  7.6 27.3 %copy-start = (f32[4,4,128,128]{3,2,1,0:T(8,128)}, f32[4,4,128,128]{3,2,1,0:T(8,128)S(1)}, u32[]{:S(2)}) copy-start(f32[4,4,128,128]{3,2,1,0:T(8,128)S(1)} %get-tuple-element.57.refs_0_) | copy-start | bytes 3145732
  16.2 18.7 %copy-start.6 = (f32[8,128,128]{2,1,0:T(8,128)}, f32[8,128,128]{2,1,0:T(8,128)S(1)}, u32[]{:S(2)}) copy-start(f32[8,128,128]{2,1,0:T(8,128)S(1)} %collective-permute-done.2.refs_6_) | copy-start | bytes 1572868
  16.2 14.9 %collective-permute-start.3 = (f32[8,128,128]{2,1,0:T(8,128)S(1)}, f32[8,128,128]{2,1,0:T(8,128)S(1)}, u32[]{:S(2)}, u32[]{:S(2)}) collective-permute-start(f32[8,128,128]{2,1,0:T(8,128)S(1)} %collective-permute-done.2.refs_6_), channel_id=1, source_target_pairs={{0,2},{2,0},{4,6},{6,4},{8,10},{10,8},{12,14},{14,12},{16,18},{18,... | collective-permute-start | bytes 1572872 | tf_op jit(solution)/shard_map/ppermute | solution.py:342
  18.0 16.9 %copy-start.4 = (f32[8,128,128]{2,1,0:T(8,128)}, f32[8,128,128]{2,1,0:T(8,128)S(1)}, u32[]{:S(2)}) copy-start(f32[8,128,128]{2,1,0:T(8,128)S(1)} %collective-permute-done.refs_5_) | copy-start | bytes 1572868
  18.0 16.9 %collective-permute-start.1 = (f32[7,128,128]{2,1,0:T(8,128)S(1)}, f32[7,128,128]{2,1,0:T(8,128)S(1)}, u32[]{:S(2)}, u32[]{:S(2)}) collective-permute-start(f32[7,128,128]{2,1,0:T(8,128)S(1)} %slice.12), channel_id=1, source_target_pairs={{0,4},{4,8},{8,12},{12,16},{16,20},{20,24},{24,28},{6,2},{10,6},{1... | collective-permute-start | bytes 1376264 | tf_op jit(solution)/shard_map/ppermute | solution.py:345
  21.5 23.5 %collective-permute-start.5 = (f32[4,4,128,128]{3,2,1,0:T(8,128)S(1)}, f32[4,4,128,128]{3,2,1,0:T(8,128)S(1)}, u32[]{:S(2)}, u32[]{:S(2)}) collective-permute-start(f32[4,4,128,128]{3,2,1,0:T(8,128)S(1)} %get-tuple-element.57.refs_0_), channel_id=1, source_target_pairs={{0,1},{1,0},{2,3},{3,2},{4,5},{5,4},{6,7},{7,6},{8,9},{9,8},{10,11... | collective-permute-start | bytes 3145736 | tf_op jit(solution)/shard_map/ppermute | solution.py:339
  23.1 17.8 %collective-permute-start.4 = (f32[7,128,128]{2,1,0:T(8,128)S(1)}, f32[7,128,128]{2,1,0:T(8,128)S(1)}, u32[]{:S(2)}, u32[]{:S(2)}) collective-permute-start(f32[7,128,128]{2,1,0:T(8,128)S(1)} %get-tuple-element.50), channel_id=1, source_target_pairs={{0,2},{2,0},{4,6},{6,4},{8,10},{10,8},{12,14},{14,12},{16,18},{18,... | collective-permute-start | bytes 1376264 | tf_op jit(solution)/shard_map/ppermute | solution.py:342
  23.1 28.7 %collective-permute-start.8 = (f32[9,128,128]{2,1,0:T(8,128)S(1)}, f32[9,128,128]{2,1,0:T(8,128)S(1)}, u32[]{:S(2)}, u32[]{:S(2)}) collective-permute-start(f32[9,128,128]{2,1,0:T(8,128)S(1)} %get-tuple-element.60), channel_id=1, source_target_pairs={{0,2},{2,0},{4,6},{6,4},{8,10},{10,8},{12,14},{14,12},{16,18},{18,... | collective-permute-start | bytes 1769480 | tf_op jit(solution)/shard_map/ppermute | solution.py:342
  31.1 3.8 %copy-start.5 = (f32[8,128,128]{2,1,0:T(8,128)}, f32[8,128,128]{2,1,0:T(8,128)S(1)}, u32[]{:S(2)}) copy-start(f32[8,128,128]{2,1,0:T(8,128)S(1)} %collective-permute-done.3.refs_7_) | copy-start | bytes 1572868
  31.1 13.6 %collective-permute-start.6 = (f32[7,128,128]{2,1,0:T(8,128)S(1)}, f32[7,128,128]{2,1,0:T(8,128)S(1)}, u32[]{:S(2)}, u32[]{:S(2)}) collective-permute-start(f32[7,128,128]{2,1,0:T(8,128)S(1)} %slice.13), channel_id=1, source_target_pairs={{0,4},{4,8},{8,12},{12,16},{16,20},{20,24},{24,28},{6,2},{10,6},{1... | collective-permute-start | bytes 1376264 | tf_op jit(solution)/shard_map/ppermute | solution.py:345
  40.9 5.9 %copy-start.3 = (f32[7,128,128]{2,1,0:T(8,128)}, f32[7,128,128]{2,1,0:T(8,128)S(1)}, u32[]{:S(2)}) copy-start(f32[7,128,128]{2,1,0:T(8,128)S(1)} %collective-permute-done.4.refs_0_) | copy-start | bytes 1376260
  40.9 14.4 %collective-permute-start.9 = (f32[7,128,128]{2,1,0:T(8,128)S(1)}, f32[7,128,128]{2,1,0:T(8,128)S(1)}, u32[]{:S(2)}, u32[]{:S(2)}) collective-permute-start(f32[7,128,128]{2,1,0:T(8,128)S(1)} %collective-permute-done.4.refs_0_), channel_id=1, source_target_pairs={{0,4},{4,8},{8,12},{12,16},{16,20},{20,24},{24,28},{6,2},{10,6},{1... | collective-permute-start | bytes 1376264 | tf_op jit(solution)/shard_map/ppermute | solution.py:345
  46.8 17.6 %collective-permute-start.7 = (f32[2,4,128,128]{3,2,1,0:T(8,128)S(1)}, f32[2,4,128,128]{3,2,1,0:T(8,128)S(1)}, u32[]{:S(2)}, u32[]{:S(2)}) collective-permute-start(f32[2,4,128,128]{3,2,1,0:T(8,128)S(1)} %get-tuple-element.58), channel_id=1, source_target_pairs={{0,1},{1,0},{2,3},{3,2},{4,5},{5,4},{6,7},{7,6},{8,9},{9,8},{10,11... | collective-permute-start | bytes 1572872 | tf_op jit(solution)/shard_map/ppermute | solution.py:339
  51.8 3.5 %copy-start.2 = (f32[9,128,128]{2,1,0:T(8,128)}, f32[9,128,128]{2,1,0:T(8,128)S(1)}, u32[]{:S(2)}) copy-start(f32[9,128,128]{2,1,0:T(8,128)S(1)} %collective-permute-done.8.refs_1_) | copy-start | bytes 1769476
  51.8 9.0 %collective-permute-start.11 = (f32[5,128,128]{2,1,0:T(8,128)S(1)}, f32[5,128,128]{2,1,0:T(8,128)S(1)}, u32[]{:S(2)}, u32[]{:S(2)}) collective-permute-start(f32[5,128,128]{2,1,0:T(8,128)S(1)} %slice.14), channel_id=1, source_target_pairs={{0,4},{4,8},{8,12},{12,16},{16,20},{20,24},{24,28},{6,2},{10,6},{1... | collective-permute-start | bytes 983048 | tf_op jit(solution)/shard_map/ppermute | solution.py:345
  57.3 7.1 %collective-permute-start.10 = (f32[2,2,128,128]{3,2,1,0:T(8,128)S(1)}, f32[2,2,128,128]{3,2,1,0:T(8,128)S(1)}, u32[]{:S(2)}, u32[]{:S(2)}) collective-permute-start(f32[2,2,128,128]{3,2,1,0:T(8,128)S(1)} %get-tuple-element.64), channel_id=1, source_target_pairs={{0,1},{1,0},{2,3},{3,2},{4,5},{5,4},{6,7},{7,6},{8,9},{9,8},{10,11... | collective-permute-start | bytes 786440 | tf_op jit(solution)/shard_map/ppermute | solution.py:339
  60.8 3.6 %copy-start.1 = (s32[2,1,8]{2,1,0:T(1,128)S(1)}, s32[2,1,8]{2,1,0:T(1,128)}, u32[]{:S(2)}) copy-start(s32[2,1,8]{2,1,0:T(1,128)} %refs_0_.3) | copy-start | bytes 196
  61.7 8.9 %collective-permute-start.12 = (f32[2,2,128,128]{3,2,1,0:T(8,128)S(1)}, f32[2,2,128,128]{3,2,1,0:T(8,128)S(1)}, u32[]{:S(2)}, u32[]{:S(2)}) collective-permute-start(f32[2,2,128,128]{3,2,1,0:T(8,128)S(1)} %get-tuple-element.79), channel_id=1, source_target_pairs={{0,1},{1,0},{2,3},{3,2},{4,5},{5,4},{6,7},{7,6},{8,9},{9,8},{10,11... | collective-permute-start | bytes 786440 | tf_op jit(solution)/shard_map/ppermute | solution.py:339

commit v8 on v7

--- a/solution.py
+++ b/solution.py
@@ -380,11 +380,10 @@
         [pltpu.SMEM(x.shape, jnp.int32) for x in (p_mask, t_mask)]
         + [vmem(*p_values.shape)]
         + [vmem(2, 24, size, size), vmem(4, 4, size, size), *band, sems(11)],
-        flops=40 * unit,
+        flops=22 * unit,
     )(u_own, p_mask, p_values, t_mask, pe_z, pe_y, pc, pc_y)
     u_y = [over_pair(after(x, pc)) for x in packed]
     u_z = [onto(after(u_y[0], t_own))]
-    keeps = after(keeps, u_y[0])
     rows = [vmem(2, size, 4 * size, dtype=BF16)] * 2
     *t_send, ss, hi, lo = call(
         functools.partial(product_send, size),

time: 72.1 us -> 72.1 us (level)
  transfers between devices with their start and end apart: 13 -> 13, of which waited for: 7 -> 6; matrix products, arithmetic and copies ran while one was open for 0% -> 0% of each run, Pallas kernels for 22% -> 22%
where the time goes in v8:
time: 72.1 us; the launch traced here: 71.4 us
  starting transfers between devices  28.5 us (40%)
  waiting for transfers between devices  25.1 us (35%)
  Pallas kernels  17.4 us (24%)
    pallas_call x10, Pallas kernels, run(): pl.pallas_call(kernel, out_shape=outs, in_specs=[ANY if spec is HBM else...  17.4 us
    ppermute x4, starting transfers between devices, onto(): return lax.ppermute(x, SLABS, onward)  14.4 us
    ppermute x5, waiting for transfers between devices, over_layer(): return lax.ppermute(x, 'layer', swap)  13 us
    ppermute x4, waiting for transfers between devices, over_pair(): return lax.ppermute(x, SLABS, pair)  12.1 us
    ppermute x5, starting transfers between devices, over_layer(): return lax.ppermute(x, 'layer', swap)  8.72 us
    ppermute x4, starting transfers between devices, over_pair(): return lax.ppermute(x, SLABS, pair)  5.37 us
  transfers between devices with their start and end apart: 13, of which 6 were waited for; matrix products, arithmetic and copies ran while one was open for 0% of the time, Pallas kernels for 22%

profile of v8, /device:TPU:0, one launch (start us, length us, event | category | flops | bytes accessed | tf_op | source)
XLA Modules:
  0.0 71.4 jit_solution(6841655885414414498)
XLA Ops:
  0.0 1.3 %shard_map.65 = (f32[8,128,128]{2,1,0:T(8,128)S(1)}, f32[8,128,128]{2,1,0:T(8,128)S(1)}) custom-call(s32[2,1,8]{2,1,0:T(1,128)} %refs_1_.5, f32[2,1,8,128,128]{4,3,2,1,0:T(8,128)} %refs_2_.1), custom_call_target="tpu_custom_call" | custom-call | tf_op jit(solution)/shard_map/pallas_call | solution.py:42
  1.3 3.0 %collective-permute-start.2 = (f32[8,128,128]{2,1,0:T(8,128)S(1)}, f32[8,128,128]{2,1,0:T(8,128)S(1)}, u32[]{:S(2)}, u32[]{:S(2)}) collective-permute-start(f32[8,128,128]{2,1,0:T(8,128)S(1)} %get-tuple-element.45), channel_id=1, source_target_pairs={{0,1},{1,0},{2,3},{3,2},{4,5},{5,4},{6,7},{7,6},{8,9},{9,8},{10,11... | collective-permute-start | bytes 1572872 | tf_op jit(solution)/shard_map/ppermute | solution.py:339
  4.3 1.5 %collective-permute-start = (f32[8,128,128]{2,1,0:T(8,128)S(1)}, f32[8,128,128]{2,1,0:T(8,128)S(1)}, u32[]{:S(2)}, u32[]{:S(2)}) collective-permute-start(f32[8,128,128]{2,1,0:T(8,128)S(1)} %get-tuple-element.43), channel_id=1, source_target_pairs={{0,2},{2,0},{4,6},{6,4},{8,10},{10,8},{12,14},{14,12},{16,18},{18,... | collective-permute-start | bytes 1572872 | tf_op jit(solution)/shard_map/ppermute | solution.py:342
  5.8 1.8 %shard_map.64 = (f32[4,4,128,128]{3,2,1,0:T(8,128)S(1)}, f32[7,128,128]{2,1,0:T(8,128)S(1)}, f32[9,128,128]{2,1,0:T(8,128)S(1)}) custom-call(s32[4,4]{1,0:T(4,128)} %bitcast.2, f32[4,4,1,128,128]{4,3,2,1,0:T(8,128)} %refs_1_.3), custom_call_target="tpu_custom_call" | custom-call | tf_op jit(solution)/shard_map/pallas_call | solution.py:42
  7.6 0.0 copy-start
  7.6 8.6 %collective-permute-done.2.refs_6_ = f32[8,128,128]{2,1,0:T(8,128)S(1)} collective-permute-done((f32[8,128,128]{2,1,0:T(8,128)S(1)}, f32[8,128,128]{2,1,0:T(8,128)S(1)}, u32[]{:S(2)}, u32[]{:S(2)}) %collective-permute-start.2) | collective-permute-done | bytes 524320 | tf_op jit(solution)/shard_map/ppermute | solution.py:339
  16.2 0.0 copy-start.6
  16.2 1.8 %collective-permute-start.3 = (f32[8,128,128]{2,1,0:T(8,128)S(1)}, f32[8,128,128]{2,1,0:T(8,128)S(1)}, u32[]{:S(2)}, u32[]{:S(2)}) collective-permute-start(f32[8,128,128]{2,1,0:T(8,128)S(1)} %collective-permute-done.2.refs_6_), channel_id=1, source_target_pairs={{0,2},{2,0},{4,6},{6,4},{8,10},{10,8},{12,14},{14,12},{16,18},{18,... | collective-permute-start | bytes 1572872 | tf_op jit(solution)/shard_map/ppermute | solution.py:342
  18.0 1.5 %collective-permute-start.4 = (f32[4,4,128,128]{3,2,1,0:T(8,128)S(1)}, f32[4,4,128,128]{3,2,1,0:T(8,128)S(1)}, u32[]{:S(2)}, u32[]{:S(2)}) collective-permute-start(f32[4,4,128,128]{3,2,1,0:T(8,128)S(1)} %get-tuple-element.53.refs_0_), channel_id=1, source_target_pairs={{0,1},{1,0},{2,3},{3,2},{4,5},{5,4},{6,7},{7,6},{8,9},{9,8},{10,11... | collective-permute-start | bytes 3145736 | tf_op jit(solution)/shard_map/ppermute | solution.py:339
  19.5 0.0 collective-permute-done.refs_5_
  19.5 3.5 %collective-permute-start.1 = (f32[7,128,128]{2,1,0:T(8,128)S(1)}, f32[7,128,128]{2,1,0:T(8,128)S(1)}, u32[]{:S(2)}, u32[]{:S(2)}) collective-permute-start(f32[7,128,128]{2,1,0:T(8,128)S(1)} %slice.12), channel_id=1, source_target_pairs={{0,4},{4,8},{8,12},{12,16},{16,20},{20,24},{24,28},{6,2},{10,6},{1... | collective-permute-start | bytes 1376264 | tf_op jit(solution)/shard_map/ppermute | solution.py:345
  23.0 0.1 collective-permute-start.7
  23.1 2.0 %collective-permute-start.8 = (f32[9,128,128]{2,1,0:T(8,128)S(1)}, f32[9,128,128]{2,1,0:T(8,128)S(1)}, u32[]{:S(2)}, u32[]{:S(2)}) collective-permute-start(f32[9,128,128]{2,1,0:T(8,128)S(1)} %get-tuple-element.58), channel_id=1, source_target_pairs={{0,2},{2,0},{4,6},{6,4},{8,10},{10,8},{12,14},{14,12},{16,18},{18,... | collective-permute-start | bytes 1769480 | tf_op jit(solution)/shard_map/ppermute | solution.py:342
  25.1 6.0 %collective-permute-done.3.refs_7_ = f32[8,128,128]{2,1,0:T(8,128)S(1)} collective-permute-done((f32[8,128,128]{2,1,0:T(8,128)S(1)}, f32[8,128,128]{2,1,0:T(8,128)S(1)}, u32[]{:S(2)}, u32[]{:S(2)}) %collective-permute-start.3) | collective-permute-done | bytes 524320 | tf_op jit(solution)/shard_map/ppermute | solution.py:342
  31.1 0.0 copy-start.5
  31.1 3.8 %collective-permute-start.5 = (f32[7,128,128]{2,1,0:T(8,128)S(1)}, f32[7,128,128]{2,1,0:T(8,128)S(1)}, u32[]{:S(2)}, u32[]{:S(2)}) collective-permute-start(f32[7,128,128]{2,1,0:T(8,128)S(1)} %slice.13), channel_id=1, source_target_pairs={{0,4},{4,8},{8,12},{12,16},{16,20},{20,24},{24,28},{6,2},{10,6},{1... | collective-permute-start | bytes 1376264 | tf_op jit(solution)/shard_map/ppermute | solution.py:345
  34.9 0.0 collective-permute-done.1.refs_4_
  34.9 0.0 copy-done
  34.9 0.0 copy-done.6
  34.9 0.0 copy-done.4
  34.9 0.0 copy-done.5
  34.9 3.6 %shard_map.66 = (f32[4,128,512]{2,1,0:T(8,128)S(1)}, bf16[512,768]{1,0:T(8,128)(2,1)S(1)}, bf16[512,768]{1,0:T(8,128)(2,1)S(1)}, bf16[768,768]{1,0:T(8,128)(2,1)...) custom-call(f32[4,4,128,128]{3,2,1,0:T(8,128)} %copy-done, s32[2,1,8]{2,1,0:T(1,128)} %refs_1_.5, ...), custom_call_target="tpu_custom_call" | custom-call | flops 4429185024 | tf_op jit(solution)/shard_map/pallas_call | solution.py:42
  38.5 2.4 %collective-permute-done.7.refs_0_ = f32[7,128,128]{2,1,0:T(8,128)S(1)} collective-permute-done((f32[7,128,128]{2,1,0:T(8,128)S(1)}, f32[7,128,128]{2,1,0:T(8,128)S(1)}, u32[]{:S(2)}, u32[]{:S(2)}) %collective-permute-start.7) | collective-permute-done | bytes 458784 | tf_op jit(solution)/shard_map/ppermute | solution.py:342
  40.9 0.0 copy-start.3
  40.9 3.7 %collective-permute-start.9 = (f32[7,128,128]{2,1,0:T(8,128)S(1)}, f32[7,128,128]{2,1,0:T(8,128)S(1)}, u32[]{:S(2)}, u32[]{:S(2)}) collective-permute-start(f32[7,128,128]{2,1,0:T(8,128)S(1)} %collective-permute-done.7.refs_0_), channel_id=1, source_target_pairs={{0,4},{4,8},{8,12},{12,16},{16,20},{20,24},{24,28},{6,2},{10,6},{1... | collective-permute-start | bytes 1376264 | tf_op jit(solution)/shard_map/ppermute | solution.py:345
  44.6 0.0 collective-permute-done.5.refs_7_
  44.7 0.0 collective-permute-done.4.refs_6_.refs_4_
  44.7 1.7 %shard_map.67 = (bf16[2,128,512]{2,1,0:T(8,128)(2,1)S(1)}, bf16[2,128,512]{2,1,0:T(8,128)(2,1)S(1)}, f32[2,4,128,128]{3,2,1,0:T(8,128)S(1)}, bf16[768,768]{1,0:T(8,128)(2,1)S(1)}, bf16[768,768]{1,0:T(8,128)(2,1)S(1)}) custom-call(f32[4,4,8,128]{3,2,1,0:T(8,128)S(1)} %get-tuple-element.47.refs_0_, ...), custom_call_target="tpu_custom_call", output_to_operand_aliasing={{3}: (4, {}), {4}: (5, {})} | custom-call | flops 805306368 | tf_op jit(solution)/shard_map/pallas_call | solution.py:42
  46.4 0.0 copy-done.3
  46.4 1.6 %collective-permute-start.6 = (f32[2,4,128,128]{3,2,1,0:T(8,128)S(1)}, f32[2,4,128,128]{3,2,1,0:T(8,128)S(1)}, u32[]{:S(2)}, u32[]{:S(2)}) collective-permute-start(f32[2,4,128,128]{3,2,1,0:T(8,128)S(1)} %get-tuple-element.54), channel_id=1, source_target_pairs={{0,1},{1,0},{2,3},{3,2},{4,5},{5,4},{6,7},{7,6},{8,9},{9,8},{10,11... | collective-permute-start | bytes 1572872 | tf_op jit(solution)/shard_map/ppermute | solution.py:339
  48.0 3.8 %collective-permute-done.8.refs_1_ = f32[9,128,128]{2,1,0:T(8,128)S(1)} collective-permute-done((f32[9,128,128]{2,1,0:T(8,128)S(1)}, f32[9,128,128]{2,1,0:T(8,128)S(1)}, u32[]{:S(2)}, u32[]{:S(2)}) %collective-permute-start.8) | collective-permute-done | bytes 589856 | tf_op jit(solution)/shard_map/ppermute | solution.py:342
  51.8 3.4 %collective-permute-start.11 = (f32[5,128,128]{2,1,0:T(8,128)S(1)}, f32[5,128,128]{2,1,0:T(8,128)S(1)}, u32[]{:S(2)}, u32[]{:S(2)}) collective-permute-start(f32[5,128,128]{2,1,0:T(8,128)S(1)} %slice.14), channel_id=1, source_target_pairs={{0,4},{4,8},{8,12},{12,16},{16,20},{20,24},{24,28},{6,2},{10,6},{1... | collective-permute-start | bytes 983048 | tf_op jit(solution)/shard_map/ppermute | solution.py:345
  55.2 0.0 collective-permute-done.9.refs_2_
  55.3 0.0 copy-done.2
  55.3 2.0 %shard_map.68 = (f32[2,2,128,128]{3,2,1,0:T(8,128)S(1)}, bf16[512,1152]{1,0:T(8,128)(2,1)S(1)}, bf16[512,1152]{1,0:T(8,128)(2,1)S(1)}) custom-call(f32[7,128,128]{2,1,0:T(8,128)} %copy-done.3, f32[9,128,128]{2,1,0:T(8,128)} %copy-done.2, f32[7,128,128]{2,1,0:T(8,128)S(1)} %collective-permute-done.9.refs_2_, ...), custom_call_target="tpu_custom_call" | custom-call | flops 201326592 | tf_op jit(solution)/shard_map/pallas_call | solution.py:42
  57.3 1.6 %collective-permute-start.10 = (f32[2,2,128,128]{3,2,1,0:T(8,128)S(1)}, f32[2,2,128,128]{3,2,1,0:T(8,128)S(1)}, u32[]{:S(2)}, u32[]{:S(2)}) collective-permute-start(f32[2,2,128,128]{3,2,1,0:T(8,128)S(1)} %get-tuple-element.62), channel_id=1, source_target_pairs={{0,1},{1,0},{2,3},{3,2},{4,5},{5,4},{6,7},{7,6},{8,9},{9,8},{10,11... | collective-permute-start | bytes 786440 | tf_op jit(solution)/shard_map/ppermute | solution.py:339
  58.9 1.3 %shard_map.70 = (bf16[512,1152]{1,0:T(8,128)(2,1)S(1)}, bf16[512,1152]{1,0:T(8,128)(2,1)S(1)}) custom-call(f32[7,128,128]{2,1,0:T(8,128)} %copy-done.3, f32[9,128,128]{2,1,0:T(8,128)} %copy-done.2, f32[7,128,128]{2,1,0:T(8,128)S(1)} %collective-permute-done.9.refs_2_), custom_call_target="tpu_custom_call" | custom-call | tf_op jit(solution)/shard_map/pallas_call | solution.py:42
  60.2 0.6 shard_map.69
  60.8 0.0 collective-permute-done.11.refs_0_
  60.8 0.0 copy-start.1
  60.8 0.9 %shard_map.71 = (f32[2,2,128,128]{3,2,1,0:T(8,128)S(1)}, bf16[512,1152]{1,0:T(8,128)(2,1)S(1)}, bf16[512,1152]{1,0:T(8,128)(2,1)S(1)}) custom-call(f32[5,128,128]{2,1,0:T(8,128)S(1)} %collective-permute-done.11.refs_0_, bf16[2,128,512]{2,1,0:T(8,128)(2,1)S(1)} %get-tuple-element.60.refs_3_.refs_1_, ...), custom_call_target="tpu_custom_call", output_to_operand_aliasing={{1}: (3, {}), {2}: (4, {})} | custom-call | flops 201326592 | tf_op jit(solution)/shard_map/pallas_call | solution.py:42
  61.7 1.1 %collective-permute-start.12 = (f32[2,2,128,128]{3,2,1,0:T(8,128)S(1)}, f32[2,2,128,128]{3,2,1,0:T(8,128)S(1)}, u32[]{:S(2)}, u32[]{:S(2)}) collective-permute-start(f32[2,2,128,128]{3,2,1,0:T(8,128)S(1)} %get-tuple-element.77), channel_id=1, source_target_pairs={{0,1},{1,0},{2,3},{3,2},{4,5},{5,4},{6,7},{7,6},{8,9},{9,8},{10,11... | collective-permute-start | bytes 786440 | tf_op jit(solution)/shard_map/ppermute | solution.py:339
  62.8 1.6 %collective-permute-done.10.refs_2_ = f32[2,2,128,128]{3,2,1,0:T(8,128)S(1)} collective-permute-done((f32[2,2,128,128]{3,2,1,0:T(8,128)S(1)}, f32[2,2,128,128]{3,2,1,0:T(8,128)S(1)}, u32[]{:S(2)}, u32[]{:S(2)}) %collective-permute-start.10) | collective-permute-done | bytes 262176 | tf_op jit(solution)/shard_map/ppermute | solution.py:339
  64.4 0.0 collective-permute-done.6.refs_1_
  64.4 0.0 copy-done.1
  64.4 3.5 %shard_map.72 = (f32[2,1,8,128,128]{4,3,2,1,0:T(8,128)}, f32[2,2,128,128]{3,2,1,0:T(8,128)S(1)}, f32[2,2,8,128]{3,2,1,0:T(8,128)S(1)}) custom-call(s32[2,1,8]{2,1,0:T(1,128)S(1)} %copy-done.1, f32[2,4,128,128]{3,2,1,0:T(8,128)S(1)} %collective-permute-done.6.refs_1_, f32[2,2,128,128]{3,2,1,0:T(8,128)S(1)} %collective-permute-done.10.refs_2_, ...), custom_call_target="tpu_custom_call" | custom-call | flops 8053063680 | tf_op jit(solution)/shard_map/pallas_call | solution.py:42
  67.8 2.8 %collective-permute-done.12.refs_2_ = f32[2,2,128,128]{3,2,1,0:T(8,128)S(1)} collective-permute-done((f32[2,2,128,128]{3,2,1,0:T(8,128)S(1)}, f32[2,2,128,128]{3,2,1,0:T(8,128)S(1)}, u32[]{:S(2)}, u32[]{:S(2)}) %collective-permute-start.12) | collective-permute-done | bytes 262176 | tf_op jit(solution)/shard_map/ppermute | solution.py:339
  70.6 0.7 %shard_map.73 = f32[2,1,8,128,128]{4,3,2,1,0:T(8,128)} custom-call(f32[2,2,8,128]{3,2,1,0:T(8,128)S(1)} %get-tuple-element.75.refs_0_, f32[2,2,128,128]{3,2,1,0:T(8,128)S(1)} %get-tuple-element.76.refs_1_, f32[2,2,128,128]{3,2,1,0:T(8,128)S(1)} %collective-permute-done.12.refs_2_, ...), custom_call_target="tpu_custom_call", output_to_operand_aliasing={{}: (3, {})} | custom-call | tf_op jit(solution)/shard_map/pallas_call | solution.py:42
  (5 shorter events, 0.1 us)
Async XLA Ops:
  1.3 14.9 %collective-permute-start.2 = (f32[8,128,128]{2,1,0:T(8,128)S(1)}, f32[8,128,128]{2,1,0:T(8,128)S(1)}, u32[]{:S(2)}, u32[]{:S(2)}) collective-permute-start(f32[8,128,128]{2,1,0:T(8,128)S(1)} %get-tuple-element.45), channel_id=1, source_target_pairs={{0,1},{1,0},{2,3},{3,2},{4,5},{5,4},{6,7},{7,6},{8,9},{9,8},{10,11... | collective-permute-start | bytes 1572872 | tf_op jit(solution)/shard_map/ppermute | solution.py:339
  4.3 15.2 %collective-permute-start = (f32[8,128,128]{2,1,0:T(8,128)S(1)}, f32[8,128,128]{2,1,0:T(8,128)S(1)}, u32[]{:S(2)}, u32[]{:S(2)}) collective-permute-start(f32[8,128,128]{2,1,0:T(8,128)S(1)} %get-tuple-element.43), channel_id=1, source_target_pairs={{0,2},{2,0},{4,6},{6,4},{8,10},{10,8},{12,14},{14,12},{16,18},{18,... | collective-permute-start | bytes 1572872 | tf_op jit(solution)/shard_map/ppermute | solution.py:342
  7.6 27.3 %copy-start = (f32[4,4,128,128]{3,2,1,0:T(8,128)}, f32[4,4,128,128]{3,2,1,0:T(8,128)S(1)}, u32[]{:S(2)}) copy-start(f32[4,4,128,128]{3,2,1,0:T(8,128)S(1)} %get-tuple-element.53.refs_0_) | copy-start | bytes 3145732
  16.2 18.7 %copy-start.6 = (f32[8,128,128]{2,1,0:T(8,128)}, f32[8,128,128]{2,1,0:T(8,128)S(1)}, u32[]{:S(2)}) copy-start(f32[8,128,128]{2,1,0:T(8,128)S(1)} %collective-permute-done.2.refs_6_) | copy-start | bytes 1572868
  16.2 14.9 %collective-permute-start.3 = (f32[8,128,128]{2,1,0:T(8,128)S(1)}, f32[8,128,128]{2,1,0:T(8,128)S(1)}, u32[]{:S(2)}, u32[]{:S(2)}) collective-permute-start(f32[8,128,128]{2,1,0:T(8,128)S(1)} %collective-permute-done.2.refs_6_), channel_id=1, source_target_pairs={{0,2},{2,0},{4,6},{6,4},{8,10},{10,8},{12,14},{14,12},{16,18},{18,... | collective-permute-start | bytes 1572872 | tf_op jit(solution)/shard_map/ppermute | solution.py:342
  18.0 26.7 %collective-permute-start.4 = (f32[4,4,128,128]{3,2,1,0:T(8,128)S(1)}, f32[4,4,128,128]{3,2,1,0:T(8,128)S(1)}, u32[]{:S(2)}, u32[]{:S(2)}) collective-permute-start(f32[4,4,128,128]{3,2,1,0:T(8,128)S(1)} %get-tuple-element.53.refs_0_), channel_id=1, source_target_pairs={{0,1},{1,0},{2,3},{3,2},{4,5},{5,4},{6,7},{7,6},{8,9},{9,8},{10,11... | collective-permute-start | bytes 3145736 | tf_op jit(solution)/shard_map/ppermute | solution.py:339
  19.5 15.4 %copy-start.4 = (f32[8,128,128]{2,1,0:T(8,128)}, f32[8,128,128]{2,1,0:T(8,128)S(1)}, u32[]{:S(2)}) copy-start(f32[8,128,128]{2,1,0:T(8,128)S(1)} %collective-permute-done.refs_5_) | copy-start | bytes 1572868
  19.5 15.4 %collective-permute-start.1 = (f32[7,128,128]{2,1,0:T(8,128)S(1)}, f32[7,128,128]{2,1,0:T(8,128)S(1)}, u32[]{:S(2)}, u32[]{:S(2)}) collective-permute-start(f32[7,128,128]{2,1,0:T(8,128)S(1)} %slice.12), channel_id=1, source_target_pairs={{0,4},{4,8},{8,12},{12,16},{16,20},{20,24},{24,28},{6,2},{10,6},{1... | collective-permute-start | bytes 1376264 | tf_op jit(solution)/shard_map/ppermute | solution.py:345
  23.0 17.9 %collective-permute-start.7 = (f32[7,128,128]{2,1,0:T(8,128)S(1)}, f32[7,128,128]{2,1,0:T(8,128)S(1)}, u32[]{:S(2)}, u32[]{:S(2)}) collective-permute-start(f32[7,128,128]{2,1,0:T(8,128)S(1)} %get-tuple-element.56), channel_id=1, source_target_pairs={{0,2},{2,0},{4,6},{6,4},{8,10},{10,8},{12,14},{14,12},{16,18},{18,... | collective-permute-start | bytes 1376264 | tf_op jit(solution)/shard_map/ppermute | solution.py:342
  23.1 28.7 %collective-permute-start.8 = (f32[9,128,128]{2,1,0:T(8,128)S(1)}, f32[9,128,128]{2,1,0:T(8,128)S(1)}, u32[]{:S(2)}, u32[]{:S(2)}) collective-permute-start(f32[9,128,128]{2,1,0:T(8,128)S(1)} %get-tuple-element.58), channel_id=1, source_target_pairs={{0,2},{2,0},{4,6},{6,4},{8,10},{10,8},{12,14},{14,12},{16,18},{18,... | collective-permute-start | bytes 1769480 | tf_op jit(solution)/shard_map/ppermute | solution.py:342
  31.1 3.8 %copy-start.5 = (f32[8,128,128]{2,1,0:T(8,128)}, f32[8,128,128]{2,1,0:T(8,128)S(1)}, u32[]{:S(2)}) copy-start(f32[8,128,128]{2,1,0:T(8,128)S(1)} %collective-permute-done.3.refs_7_) | copy-start | bytes 1572868
  31.1 13.6 %collective-permute-start.5 = (f32[7,128,128]{2,1,0:T(8,128)S(1)}, f32[7,128,128]{2,1,0:T(8,128)S(1)}, u32[]{:S(2)}, u32[]{:S(2)}) collective-permute-start(f32[7,128,128]{2,1,0:T(8,128)S(1)} %slice.13), channel_id=1, source_target_pairs={{0,4},{4,8},{8,12},{12,16},{16,20},{20,24},{24,28},{6,2},{10,6},{1... | collective-permute-start | bytes 1376264 | tf_op jit(solution)/shard_map/ppermute | solution.py:345
  40.9 5.5 %copy-start.3 = (f32[7,128,128]{2,1,0:T(8,128)}, f32[7,128,128]{2,1,0:T(8,128)S(1)}, u32[]{:S(2)}) copy-start(f32[7,128,128]{2,1,0:T(8,128)S(1)} %collective-permute-done.7.refs_0_) | copy-start | bytes 1376260
  40.9 14.4 %collective-permute-start.9 = (f32[7,128,128]{2,1,0:T(8,128)S(1)}, f32[7,128,128]{2,1,0:T(8,128)S(1)}, u32[]{:S(2)}, u32[]{:S(2)}) collective-permute-start(f32[7,128,128]{2,1,0:T(8,128)S(1)} %collective-permute-done.7.refs_0_), channel_id=1, source_target_pairs={{0,4},{4,8},{8,12},{12,16},{16,20},{20,24},{24,28},{6,2},{10,6},{1... | collective-permute-start | bytes 1376264 | tf_op jit(solution)/shard_map/ppermute | solution.py:345
  46.4 18.0 %collective-permute-start.6 = (f32[2,4,128,128]{3,2,1,0:T(8,128)S(1)}, f32[2,4,128,128]{3,2,1,0:T(8,128)S(1)}, u32[]{:S(2)}, u32[]{:S(2)}) collective-permute-start(f32[2,4,128,128]{3,2,1,0:T(8,128)S(1)} %get-tuple-element.54), channel_id=1, source_target_pairs={{0,1},{1,0},{2,3},{3,2},{4,5},{5,4},{6,7},{7,6},{8,9},{9,8},{10,11... | collective-permute-start | bytes 1572872 | tf_op jit(solution)/shard_map/ppermute | solution.py:339
  51.8 3.5 %copy-start.2 = (f32[9,128,128]{2,1,0:T(8,128)}, f32[9,128,128]{2,1,0:T(8,128)S(1)}, u32[]{:S(2)}) copy-start(f32[9,128,128]{2,1,0:T(8,128)S(1)} %collective-permute-done.8.refs_1_) | copy-start | bytes 1769476
  51.8 9.0 %collective-permute-start.11 = (f32[5,128,128]{2,1,0:T(8,128)S(1)}, f32[5,128,128]{2,1,0:T(8,128)S(1)}, u32[]{:S(2)}, u32[]{:S(2)}) collective-permute-start(f32[5,128,128]{2,1,0:T(8,128)S(1)} %slice.14), channel_id=1, source_target_pairs={{0,4},{4,8},{8,12},{12,16},{16,20},{20,24},{24,28},{6,2},{10,6},{1... | collective-permute-start | bytes 983048 | tf_op jit(solution)/shard_map/ppermute | solution.py:345
  57.3 7.1 %collective-permute-start.10 = (f32[2,2,128,128]{3,2,1,0:T(8,128)S(1)}, f32[2,2,128,128]{3,2,1,0:T(8,128)S(1)}, u32[]{:S(2)}, u32[]{:S(2)}) collective-permute-start(f32[2,2,128,128]{3,2,1,0:T(8,128)S(1)} %get-tuple-element.62), channel_id=1, source_target_pairs={{0,1},{1,0},{2,3},{3,2},{4,5},{5,4},{6,7},{7,6},{8,9},{9,8},{10,11... | collective-permute-start | bytes 786440 | tf_op jit(solution)/shard_map/ppermute | solution.py:339
  60.8 3.6 %copy-start.1 = (s32[2,1,8]{2,1,0:T(1,128)S(1)}, s32[2,1,8]{2,1,0:T(1,128)}, u32[]{:S(2)}) copy-start(s32[2,1,8]{2,1,0:T(1,128)} %refs_0_.3) | copy-start | bytes 196
  61.7 8.9 %collective-permute-start.12 = (f32[2,2,128,128]{3,2,1,0:T(8,128)S(1)}, f32[2,2,128,128]{3,2,1,0:T(8,128)S(1)}, u32[]{:S(2)}, u32[]{:S(2)}) collective-permute-start(f32[2,2,128,128]{3,2,1,0:T(8,128)S(1)} %get-tuple-element.77), channel_id=1, source_target_pairs={{0,1},{1,0},{2,3},{3,2},{4,5},{5,4},{6,7},{7,6},{8,9},{9,8},{10,11... | collective-permute-start | bytes 786440 | tf_op jit(solution)/shard_map/ppermute | solution.py:339

commit v9 on v8

--- a/solution.py
+++ b/solution.py
@@ -406,12 +406,12 @@
     halo, *uh_first = call(
         functools.partial(first_halo, size),
         [pair_sums, *uh],
-        [HBM, HBM, ANY, VMEM, VMEM],
+        [HBM, ANY, ANY, VMEM, VMEM],
         [stage, sems(3)],
         flops=unit,
     )(*u_y, u_z[0], *t_send)
     halo_got = over_layer(halo)
-    uh_last = call(functools.partial(halo_matrix, size), uh, [HBM, HBM, ANY], [stage, sems(3)])(
+    uh_last = call(functools.partial(halo_matrix, size), uh, [HBM, ANY, ANY], [stage, sems(3)])(
         after(u_y[0], halo), u_y[1], u_z[0]
     )
     last, *uh_last = call(

time: 72.1 us -> 72.1 us (level)
  the two profiles are of different devices: /device:TPU:0 before, /device:TPU:5 now
where the time goes in v9:
time: 72.1 us; the launch traced here: 71.8 us
  starting transfers between devices  37.8 us (52%)
  Pallas kernels  17.1 us (24%)
  waiting for transfers between devices  16.5 us (23%)
    ppermute x4, starting transfers between devices, onto(): return lax.ppermute(x, SLABS, onward)  30.5 us
    pallas_call x10, Pallas kernels, run(): pl.pallas_call(kernel, out_shape=outs, in_specs=[ANY if spec is HBM else...  17.1 us
    ppermute x5, waiting for transfers between devices, over_layer(): return lax.ppermute(x, 'layer', swap)  14.9 us
    ppermute x5, starting transfers between devices, over_layer(): return lax.ppermute(x, 'layer', swap)  5.3 us
    ppermute x4, starting transfers between devices, over_pair(): return lax.ppermute(x, SLABS, pair)  2.05 us
    ppermute x4, waiting for transfers between devices, over_pair(): return lax.ppermute(x, SLABS, pair)  1.64 us
  transfers between devices with their start and end apart: 13, of which 4 were waited for; matrix products, arithmetic and copies ran while one was open for 0% of the time, Pallas kernels for 21%

profile of v9, /device:TPU:5, one launch (start us, length us, event | category | flops | bytes accessed | tf_op | source)
XLA Modules:
  0.0 71.8 jit_solution(1352882035472941272)
XLA Ops:
  0.0 1.3 %shard_map.65 = (f32[8,128,128]{2,1,0:T(8,128)S(1)}, f32[8,128,128]{2,1,0:T(8,128)S(1)}) custom-call(s32[2,1,8]{2,1,0:T(1,128)} %refs_1_.5, f32[2,1,8,128,128]{4,3,2,1,0:T(8,128)} %refs_2_.1), custom_call_target="tpu_custom_call" | custom-call | tf_op jit(solution)/shard_map/pallas_call | solution.py:42
  1.3 1.3 %collective-permute-start.2 = (f32[8,128,128]{2,1,0:T(8,128)S(1)}, f32[8,128,128]{2,1,0:T(8,128)S(1)}, u32[]{:S(2)}, u32[]{:S(2)}) collective-permute-start(f32[8,128,128]{2,1,0:T(8,128)S(1)} %get-tuple-element.45), channel_id=1, source_target_pairs={{0,1},{1,0},{2,3},{3,2},{4,5},{5,4},{6,7},{7,6},{8,9},{9,8},{10,11... | collective-permute-start | bytes 1572872 | tf_op jit(solution)/shard_map/ppermute | solution.py:339
  2.5 0.2 collective-permute-start
  2.8 1.8 %shard_map.64 = (f32[4,4,128,128]{3,2,1,0:T(8,128)S(1)}, f32[7,128,128]{2,1,0:T(8,128)S(1)}, f32[9,128,128]{2,1,0:T(8,128)S(1)}) custom-call(s32[4,4]{1,0:T(4,128)} %bitcast.2, f32[4,4,1,128,128]{4,3,2,1,0:T(8,128)} %refs_1_.3), custom_call_target="tpu_custom_call" | custom-call | tf_op jit(solution)/shard_map/pallas_call | solution.py:42
  4.6 0.0 copy-start
  4.6 9.5 %collective-permute-done.2.refs_6_ = f32[8,128,128]{2,1,0:T(8,128)S(1)} collective-permute-done((f32[8,128,128]{2,1,0:T(8,128)S(1)}, f32[8,128,128]{2,1,0:T(8,128)S(1)}, u32[]{:S(2)}, u32[]{:S(2)}) %collective-permute-start.2) | collective-permute-done | bytes 524320 | tf_op jit(solution)/shard_map/ppermute | solution.py:339
  14.1 0.0 copy-start.5
  14.1 0.3 collective-permute-start.3
  14.4 1.1 %collective-permute-start.4 = (f32[4,4,128,128]{3,2,1,0:T(8,128)S(1)}, f32[4,4,128,128]{3,2,1,0:T(8,128)S(1)}, u32[]{:S(2)}, u32[]{:S(2)}) collective-permute-start(f32[4,4,128,128]{3,2,1,0:T(8,128)S(1)} %get-tuple-element.53.refs_0_), channel_id=1, source_target_pairs={{0,1},{1,0},{2,3},{3,2},{4,5},{5,4},{6,7},{7,6},{8,9},{9,8},{10,11... | collective-permute-start | bytes 3145736 | tf_op jit(solution)/shard_map/ppermute | solution.py:339
  15.6 0.0 collective-permute-done.refs_5_
  15.6 0.0 copy-start.3
  15.6 7.2 %collective-permute-start.1 = (f32[7,128,128]{2,1,0:T(8,128)S(1)}, f32[7,128,128]{2,1,0:T(8,128)S(1)}, u32[]{:S(2)}, u32[]{:S(2)}) collective-permute-start(f32[7,128,128]{2,1,0:T(8,128)S(1)} %slice.12), channel_id=1, source_target_pairs={{0,4},{4,8},{8,12},{12,16},{16,20},{20,24},{24,28},{6,2},{10,6},{1... | collective-permute-start | bytes 1376264 | tf_op jit(solution)/shard_map/ppermute | solution.py:345
  22.8 0.1 collective-permute-start.7
  22.9 1.5 %collective-permute-start.8 = (f32[9,128,128]{2,1,0:T(8,128)S(1)}, f32[9,128,128]{2,1,0:T(8,128)S(1)}, u32[]{:S(2)}, u32[]{:S(2)}) collective-permute-start(f32[9,128,128]{2,1,0:T(8,128)S(1)} %get-tuple-element.58), channel_id=1, source_target_pairs={{0,2},{2,0},{4,6},{6,4},{8,10},{10,8},{12,14},{14,12},{16,18},{18,... | collective-permute-start | bytes 1769480 | tf_op jit(solution)/shard_map/ppermute | solution.py:342
  24.4 1.6 %collective-permute-done.3.refs_7_ = f32[8,128,128]{2,1,0:T(8,128)S(1)} collective-permute-done((f32[8,128,128]{2,1,0:T(8,128)S(1)}, f32[8,128,128]{2,1,0:T(8,128)S(1)}, u32[]{:S(2)}, u32[]{:S(2)}) %collective-permute-start.3) | collective-permute-done | bytes 524320 | tf_op jit(solution)/shard_map/ppermute | solution.py:342
  26.0 0.0 copy-start.4
  26.0 9.7 %collective-permute-start.5 = (f32[7,128,128]{2,1,0:T(8,128)S(1)}, f32[7,128,128]{2,1,0:T(8,128)S(1)}, u32[]{:S(2)}, u32[]{:S(2)}) collective-permute-start(f32[7,128,128]{2,1,0:T(8,128)S(1)} %slice.13), channel_id=1, source_target_pairs={{0,4},{4,8},{8,12},{12,16},{16,20},{20,24},{24,28},{6,2},{10,6},{1... | collective-permute-start | bytes 1376264 | tf_op jit(solution)/shard_map/ppermute | solution.py:345
  35.7 0.0 collective-permute-done.1.refs_4_
  35.7 0.0 copy-done
  35.7 0.0 copy-done.5
  35.7 0.0 copy-done.3
  35.7 0.0 copy-done.4
  35.7 3.6 %shard_map.66 = (f32[4,128,512]{2,1,0:T(8,128)S(1)}, bf16[512,768]{1,0:T(8,128)(2,1)S(1)}, bf16[512,768]{1,0:T(8,128)(2,1)S(1)}, bf16[768,768]{1,0:T(8,128)(2,1)...) custom-call(f32[4,4,128,128]{3,2,1,0:T(8,128)} %copy-done, s32[2,1,8]{2,1,0:T(1,128)} %refs_1_.5, ...), custom_call_target="tpu_custom_call" | custom-call | flops 4429185024 | tf_op jit(solution)/shard_map/pallas_call | solution.py:42
  39.4 0.0 collective-permute-done.7.refs_0_
  39.4 0.0 copy-start.2
  39.4 6.1 %collective-permute-start.9 = (f32[7,128,128]{2,1,0:T(8,128)S(1)}, f32[7,128,128]{2,1,0:T(8,128)S(1)}, u32[]{:S(2)}, u32[]{:S(2)}) collective-permute-start(f32[7,128,128]{2,1,0:T(8,128)S(1)} %collective-permute-done.7.refs_0_), channel_id=1, source_target_pairs={{0,4},{4,8},{8,12},{12,16},{16,20},{20,24},{24,28},{6,2},{10,6},{1... | collective-permute-start | bytes 1376264 | tf_op jit(solution)/shard_map/ppermute | solution.py:345
  45.5 0.0 collective-permute-done.5.refs_7_
  45.5 0.0 collective-permute-done.4.refs_6_.refs_4_
  45.5 1.7 %shard_map.67 = (bf16[2,128,512]{2,1,0:T(8,128)(2,1)S(1)}, bf16[2,128,512]{2,1,0:T(8,128)(2,1)S(1)}, f32[2,4,128,128]{3,2,1,0:T(8,128)S(1)}, bf16[768,768]{1,0:T(8,128)(2,1)S(1)}, bf16[768,768]{1,0:T(8,128)(2,1)S(1)}) custom-call(f32[4,4,8,128]{3,2,1,0:T(8,128)S(1)} %get-tuple-element.47.refs_0_, ...), custom_call_target="tpu_custom_call", output_to_operand_aliasing={{3}: (4, {}), {4}: (5, {})} | custom-call | flops 805306368 | tf_op jit(solution)/shard_map/pallas_call | solution.py:42
  47.2 0.0 copy-done.2
  47.2 1.3 %collective-permute-start.6 = (f32[2,4,128,128]{3,2,1,0:T(8,128)S(1)}, f32[2,4,128,128]{3,2,1,0:T(8,128)S(1)}, u32[]{:S(2)}, u32[]{:S(2)}) collective-permute-start(f32[2,4,128,128]{3,2,1,0:T(8,128)S(1)} %get-tuple-element.54), channel_id=1, source_target_pairs={{0,1},{1,0},{2,3},{3,2},{4,5},{5,4},{6,7},{7,6},{8,9},{9,8},{10,11... | collective-permute-start | bytes 1572872 | tf_op jit(solution)/shard_map/ppermute | solution.py:339
  48.5 0.0 collective-permute-done.8.refs_1_
  48.6 7.5 %collective-permute-start.11 = (f32[5,128,128]{2,1,0:T(8,128)S(1)}, f32[5,128,128]{2,1,0:T(8,128)S(1)}, u32[]{:S(2)}, u32[]{:S(2)}) collective-permute-start(f32[5,128,128]{2,1,0:T(8,128)S(1)} %slice.14), channel_id=1, source_target_pairs={{0,4},{4,8},{8,12},{12,16},{16,20},{20,24},{24,28},{6,2},{10,6},{1... | collective-permute-start | bytes 983048 | tf_op jit(solution)/shard_map/ppermute | solution.py:345
  56.1 0.0 collective-permute-done.9.refs_2_
  56.1 1.9 %shard_map.68 = (f32[2,2,128,128]{3,2,1,0:T(8,128)S(1)}, bf16[512,1152]{1,0:T(8,128)(2,1)S(1)}, bf16[512,1152]{1,0:T(8,128)(2,1)S(1)}) custom-call(f32[7,128,128]{2,1,0:T(8,128)} %copy-done.2, f32[9,128,128]{2,1,0:T(8,128)S(1)} %collective-permute-done.8.refs_1_, f32[7,128,128]{2,1,0:T(8,128)S(1)} %collective-permute-done.9.refs_2_, ...), custom_call_target="tpu_custom_call" | custom-call | flops 201326592 | tf_op jit(solution)/shard_map/pallas_call | solution.py:42
  58.0 1.3 %collective-permute-start.10 = (f32[2,2,128,128]{3,2,1,0:T(8,128)S(1)}, f32[2,2,128,128]{3,2,1,0:T(8,128)S(1)}, u32[]{:S(2)}, u32[]{:S(2)}) collective-permute-start(f32[2,2,128,128]{3,2,1,0:T(8,128)S(1)} %get-tuple-element.62), channel_id=1, source_target_pairs={{0,1},{1,0},{2,3},{3,2},{4,5},{5,4},{6,7},{7,6},{8,9},{9,8},{10,11... | collective-permute-start | bytes 786440 | tf_op jit(solution)/shard_map/ppermute | solution.py:339
  59.2 1.1 %shard_map.70 = (bf16[512,1152]{1,0:T(8,128)(2,1)S(1)}, bf16[512,1152]{1,0:T(8,128)(2,1)S(1)}) custom-call(f32[7,128,128]{2,1,0:T(8,128)} %copy-done.2, f32[9,128,128]{2,1,0:T(8,128)S(1)} %collective-permute-done.8.refs_1_, f32[7,128,128]{2,1,0:T(8,128)S(1)} %collective-permute-done.9.refs_2_), custom_call_target="tpu_custom_call" | custom-call | tf_op jit(solution)/shard_map/pallas_call | solution.py:42
  60.4 0.6 shard_map.69
  61.0 0.0 collective-permute-done.11.refs_0_
  61.0 0.0 copy-start.1
  61.0 0.8 %shard_map.71 = (f32[2,2,128,128]{3,2,1,0:T(8,128)S(1)}, bf16[512,1152]{1,0:T(8,128)(2,1)S(1)}, bf16[512,1152]{1,0:T(8,128)(2,1)S(1)}) custom-call(f32[5,128,128]{2,1,0:T(8,128)S(1)} %collective-permute-done.11.refs_0_, bf16[2,128,512]{2,1,0:T(8,128)(2,1)S(1)} %get-tuple-element.60.refs_3_.refs_1_, ...), custom_call_target="tpu_custom_call", output_to_operand_aliasing={{1}: (3, {}), {2}: (4, {})} | custom-call | flops 201326592 | tf_op jit(solution)/shard_map/pallas_call | solution.py:42
  61.9 0.3 collective-permute-start.12
  62.2 3.5 %collective-permute-done.10.refs_2_ = f32[2,2,128,128]{3,2,1,0:T(8,128)S(1)} collective-permute-done((f32[2,2,128,128]{3,2,1,0:T(8,128)S(1)}, f32[2,2,128,128]{3,2,1,0:T(8,128)S(1)}, u32[]{:S(2)}, u32[]{:S(2)}) %collective-permute-start.10) | collective-permute-done | bytes 262176 | tf_op jit(solution)/shard_map/ppermute | solution.py:339
  65.7 0.0 collective-permute-done.6.refs_1_
  65.7 0.0 copy-done.1
  65.7 3.5 %shard_map.72 = (f32[2,1,8,128,128]{4,3,2,1,0:T(8,128)}, f32[2,2,128,128]{3,2,1,0:T(8,128)S(1)}, f32[2,2,8,128]{3,2,1,0:T(8,128)S(1)}) custom-call(s32[2,1,8]{2,1,0:T(1,128)S(1)} %copy-done.1, f32[2,4,128,128]{3,2,1,0:T(8,128)S(1)} %collective-permute-done.6.refs_1_, f32[2,2,128,128]{3,2,1,0:T(8,128)S(1)} %collective-permute-done.10.refs_2_, ...), custom_call_target="tpu_custom_call" | custom-call | flops 8053063680 | tf_op jit(solution)/shard_map/pallas_call | solution.py:42
  69.2 1.8 %collective-permute-done.12.refs_2_ = f32[2,2,128,128]{3,2,1,0:T(8,128)S(1)} collective-permute-done((f32[2,2,128,128]{3,2,1,0:T(8,128)S(1)}, f32[2,2,128,128]{3,2,1,0:T(8,128)S(1)}, u32[]{:S(2)}, u32[]{:S(2)}) %collective-permute-start.12) | collective-permute-done | bytes 262176 | tf_op jit(solution)/shard_map/ppermute | solution.py:339
  71.0 0.7 %shard_map.73 = f32[2,1,8,128,128]{4,3,2,1,0:T(8,128)} custom-call(f32[2,2,8,128]{3,2,1,0:T(8,128)S(1)} %get-tuple-element.75.refs_0_, f32[2,2,128,128]{3,2,1,0:T(8,128)S(1)} %get-tuple-element.76.refs_1_, f32[2,2,128,128]{3,2,1,0:T(8,128)S(1)} %collective-permute-done.12.refs_2_, ...), custom_call_target="tpu_custom_call", output_to_operand_aliasing={{}: (3, {})} | custom-call | tf_op jit(solution)/shard_map/pallas_call | solution.py:42
  (3 shorter events, 0.1 us)
Async XLA Ops:
  1.3 12.9 %collective-permute-start.2 = (f32[8,128,128]{2,1,0:T(8,128)S(1)}, f32[8,128,128]{2,1,0:T(8,128)S(1)}, u32[]{:S(2)}, u32[]{:S(2)}) collective-permute-start(f32[8,128,128]{2,1,0:T(8,128)S(1)} %get-tuple-element.45), channel_id=1, source_target_pairs={{0,1},{1,0},{2,3},{3,2},{4,5},{5,4},{6,7},{7,6},{8,9},{9,8},{10,11... | collective-permute-start | bytes 1572872 | tf_op jit(solution)/shard_map/ppermute | solution.py:339
  2.5 13.0 %collective-permute-start = (f32[8,128,128]{2,1,0:T(8,128)S(1)}, f32[8,128,128]{2,1,0:T(8,128)S(1)}, u32[]{:S(2)}, u32[]{:S(2)}) collective-permute-start(f32[8,128,128]{2,1,0:T(8,128)S(1)} %get-tuple-element.43), channel_id=1, source_target_pairs={{0,2},{2,0},{4,6},{6,4},{8,10},{10,8},{12,14},{14,12},{16,18},{18,... | collective-permute-start | bytes 1572872 | tf_op jit(solution)/shard_map/ppermute | solution.py:342
  4.6 31.1 %copy-start = (f32[4,4,128,128]{3,2,1,0:T(8,128)}, f32[4,4,128,128]{3,2,1,0:T(8,128)S(1)}, u32[]{:S(2)}) copy-start(f32[4,4,128,128]{3,2,1,0:T(8,128)S(1)} %get-tuple-element.53.refs_0_) | copy-start | bytes 3145732
  14.1 21.6 %copy-start.5 = (f32[8,128,128]{2,1,0:T(8,128)}, f32[8,128,128]{2,1,0:T(8,128)S(1)}, u32[]{:S(2)}) copy-start(f32[8,128,128]{2,1,0:T(8,128)S(1)} %collective-permute-done.2.refs_6_) | copy-start | bytes 1572868
  14.1 11.9 %collective-permute-start.3 = (f32[8,128,128]{2,1,0:T(8,128)S(1)}, f32[8,128,128]{2,1,0:T(8,128)S(1)}, u32[]{:S(2)}, u32[]{:S(2)}) collective-permute-start(f32[8,128,128]{2,1,0:T(8,128)S(1)} %collective-permute-done.2.refs_6_), channel_id=1, source_target_pairs={{0,2},{2,0},{4,6},{6,4},{8,10},{10,8},{12,14},{14,12},{16,18},{18,... | collective-permute-start | bytes 1572872 | tf_op jit(solution)/shard_map/ppermute | solution.py:342
  14.4 31.1 %collective-permute-start.4 = (f32[4,4,128,128]{3,2,1,0:T(8,128)S(1)}, f32[4,4,128,128]{3,2,1,0:T(8,128)S(1)}, u32[]{:S(2)}, u32[]{:S(2)}) collective-permute-start(f32[4,4,128,128]{3,2,1,0:T(8,128)S(1)} %get-tuple-element.53.refs_0_), channel_id=1, source_target_pairs={{0,1},{1,0},{2,3},{3,2},{4,5},{5,4},{6,7},{7,6},{8,9},{9,8},{10,11... | collective-permute-start | bytes 3145736 | tf_op jit(solution)/shard_map/ppermute | solution.py:339
  15.6 20.2 %copy-start.3 = (f32[8,128,128]{2,1,0:T(8,128)}, f32[8,128,128]{2,1,0:T(8,128)S(1)}, u32[]{:S(2)}) copy-start(f32[8,128,128]{2,1,0:T(8,128)S(1)} %collective-permute-done.refs_5_) | copy-start | bytes 1572868
  15.6 20.1 %collective-permute-start.1 = (f32[7,128,128]{2,1,0:T(8,128)S(1)}, f32[7,128,128]{2,1,0:T(8,128)S(1)}, u32[]{:S(2)}, u32[]{:S(2)}) collective-permute-start(f32[7,128,128]{2,1,0:T(8,128)S(1)} %slice.12), channel_id=1, source_target_pairs={{0,4},{4,8},{8,12},{12,16},{16,20},{20,24},{24,28},{6,2},{10,6},{1... | collective-permute-start | bytes 1376264 | tf_op jit(solution)/shard_map/ppermute | solution.py:345
  22.8 16.5 %collective-permute-start.7 = (f32[7,128,128]{2,1,0:T(8,128)S(1)}, f32[7,128,128]{2,1,0:T(8,128)S(1)}, u32[]{:S(2)}, u32[]{:S(2)}) collective-permute-start(f32[7,128,128]{2,1,0:T(8,128)S(1)} %get-tuple-element.56), channel_id=1, source_target_pairs={{0,2},{2,0},{4,6},{6,4},{8,10},{10,8},{12,14},{14,12},{16,18},{18,... | collective-permute-start | bytes 1376264 | tf_op jit(solution)/shard_map/ppermute | solution.py:342
  22.9 25.6 %collective-permute-start.8 = (f32[9,128,128]{2,1,0:T(8,128)S(1)}, f32[9,128,128]{2,1,0:T(8,128)S(1)}, u32[]{:S(2)}, u32[]{:S(2)}) collective-permute-start(f32[9,128,128]{2,1,0:T(8,128)S(1)} %get-tuple-element.58), channel_id=1, source_target_pairs={{0,2},{2,0},{4,6},{6,4},{8,10},{10,8},{12,14},{14,12},{16,18},{18,... | collective-permute-start | bytes 1769480 | tf_op jit(solution)/shard_map/ppermute | solution.py:342
  26.0 9.7 %copy-start.4 = (f32[8,128,128]{2,1,0:T(8,128)}, f32[8,128,128]{2,1,0:T(8,128)S(1)}, u32[]{:S(2)}) copy-start(f32[8,128,128]{2,1,0:T(8,128)S(1)} %collective-permute-done.3.refs_7_) | copy-start | bytes 1572868
  26.0 19.4 %collective-permute-start.5 = (f32[7,128,128]{2,1,0:T(8,128)S(1)}, f32[7,128,128]{2,1,0:T(8,128)S(1)}, u32[]{:S(2)}, u32[]{:S(2)}) collective-permute-start(f32[7,128,128]{2,1,0:T(8,128)S(1)} %slice.13), channel_id=1, source_target_pairs={{0,4},{4,8},{8,12},{12,16},{16,20},{20,24},{24,28},{6,2},{10,6},{1... | collective-permute-start | bytes 1376264 | tf_op jit(solution)/shard_map/ppermute | solution.py:345
  39.4 7.8 %copy-start.2 = (f32[7,128,128]{2,1,0:T(8,128)}, f32[7,128,128]{2,1,0:T(8,128)S(1)}, u32[]{:S(2)}) copy-start(f32[7,128,128]{2,1,0:T(8,128)S(1)} %collective-permute-done.7.refs_0_) | copy-start | bytes 1376260
  39.4 16.7 %collective-permute-start.9 = (f32[7,128,128]{2,1,0:T(8,128)S(1)}, f32[7,128,128]{2,1,0:T(8,128)S(1)}, u32[]{:S(2)}, u32[]{:S(2)}) collective-permute-start(f32[7,128,128]{2,1,0:T(8,128)S(1)} %collective-permute-done.7.refs_0_), channel_id=1, source_target_pairs={{0,4},{4,8},{8,12},{12,16},{16,20},{20,24},{24,28},{6,2},{10,6},{1... | collective-permute-start | bytes 1376264 | tf_op jit(solution)/shard_map/ppermute | solution.py:345
  47.2 18.5 %collective-permute-start.6 = (f32[2,4,128,128]{3,2,1,0:T(8,128)S(1)}, f32[2,4,128,128]{3,2,1,0:T(8,128)S(1)}, u32[]{:S(2)}, u32[]{:S(2)}) collective-permute-start(f32[2,4,128,128]{3,2,1,0:T(8,128)S(1)} %get-tuple-element.54), channel_id=1, source_target_pairs={{0,1},{1,0},{2,3},{3,2},{4,5},{5,4},{6,7},{7,6},{8,9},{9,8},{10,11... | collective-permute-start | bytes 1572872 | tf_op jit(solution)/shard_map/ppermute | solution.py:339
  48.6 12.5 %collective-permute-start.11 = (f32[5,128,128]{2,1,0:T(8,128)S(1)}, f32[5,128,128]{2,1,0:T(8,128)S(1)}, u32[]{:S(2)}, u32[]{:S(2)}) collective-permute-start(f32[5,128,128]{2,1,0:T(8,128)S(1)} %slice.14), channel_id=1, source_target_pairs={{0,4},{4,8},{8,12},{12,16},{16,20},{20,24},{24,28},{6,2},{10,6},{1... | collective-permute-start | bytes 983048 | tf_op jit(solution)/shard_map/ppermute | solution.py:345
  58.0 7.8 %collective-permute-start.10 = (f32[2,2,128,128]{3,2,1,0:T(8,128)S(1)}, f32[2,2,128,128]{3,2,1,0:T(8,128)S(1)}, u32[]{:S(2)}, u32[]{:S(2)}) collective-permute-start(f32[2,2,128,128]{3,2,1,0:T(8,128)S(1)} %get-tuple-element.62), channel_id=1, source_target_pairs={{0,1},{1,0},{2,3},{3,2},{4,5},{5,4},{6,7},{7,6},{8,9},{9,8},{10,11... | collective-permute-start | bytes 786440 | tf_op jit(solution)/shard_map/ppermute | solution.py:339
  61.0 4.7 %copy-start.1 = (s32[2,1,8]{2,1,0:T(1,128)S(1)}, s32[2,1,8]{2,1,0:T(1,128)}, u32[]{:S(2)}) copy-start(s32[2,1,8]{2,1,0:T(1,128)} %refs_0_.3) | copy-start | bytes 196
  61.9 9.1 %collective-permute-start.12 = (f32[2,2,128,128]{3,2,1,0:T(8,128)S(1)}, f32[2,2,128,128]{3,2,1,0:T(8,128)S(1)}, u32[]{:S(2)}, u32[]{:S(2)}) collective-permute-start(f32[2,2,128,128]{3,2,1,0:T(8,128)S(1)} %get-tuple-element.77), channel_id=1, source_target_pairs={{0,1},{1,0},{2,3},{3,2},{4,5},{5,4},{6,7},{7,6},{8,9},{9,8},{10,11... | collective-permute-start | bytes 786440 | tf_op jit(solution)/shard_map/ppermute | solution.py:339
